TPU v7x, 128 devices: a whole 4x4x4 slice. The times are simulated.
128 devices in a mesh: pa: 32 (over y, x, core), mu: 4 (over z).
Axes of the slice: x: 4, y: 4, z: 4, core: 2. Of those that a mesh axis runs over, the one named last changes fastest.
Arguments:
- three_center: bfloat16 [4096, 256, 512], P('pa', 'mu'), may hold values from -6 to 6
- center_mask: int32 [64, 4, 8], P('pa', 'mu'), may hold values 0 or 1
- density: bfloat16 [512, 512], P('mu'), may hold values from -0.25 to 0.25
- density_mask: int32 [8, 8], P('mu'), may hold values 0 or 1
- metric_band: bfloat16 [4096, 384], P('pa'), may hold values from -0.3125 to 0.3125
Outputs:
- fitted: bfloat16 [4096, 256, 512], P('pa', 'mu')
- exchange_blocks: float32 [256, 64], P('mu')
All inputs are finite; a program needn't handle non-finite values. No bound on the sum of `center_mask` or of `density_mask` on one device may be relied on, other than what follows from the above.
Results may differ from a plain program's by a relative error of at most 0.0051.
Values may be sent and summed in bfloat16 or wider, within the bound.
No kernel may reach another device: no remote copies, remote signals or barrier semaphores. Data moves between devices by JAX's collectives and lax.ppermute only.
A program may use at most 192 MiB of HBM per device.

v0:
```python
import math

import jax
import jax.numpy as jnp
from jax import lax
from jax.sharding import PartitionSpec as P

BS = 64


def with_halo(block, sides, width):
    for axis, dim in sides:
        count = lax.axis_size(axis)
        forward = [(i, i + 1) for i in range(count - 1)]
        backward = [(target, source) for source, target in forward]
        low = lax.ppermute(
            lax.slice_in_dim(block, block.shape[dim] - width, None, axis=dim), axis, forward
        )
        high = lax.ppermute(lax.slice_in_dim(block, 0, width, axis=dim), axis, backward)
        block = jnp.concatenate([low, block, high], axis=dim)
    return block


def on_device(three_center, center_mask, density, density_mask, metric_band):
    rows, cols, width = three_center.shape
    blocks = three_center.reshape(rows // BS, BS, cols // BS, BS, width // BS, BS)
    masked = (blocks * center_mask.astype(jnp.bfloat16)[:, None, :, None, :, None]).reshape(
        rows, cols, width
    )
    drows = density.shape[0]
    local_dens = (
        density.reshape(drows // BS, BS, width // BS, BS)
        * density_mask.astype(jnp.bfloat16)[:, None, :, None]
    ).reshape(drows, width)
    dens = lax.all_gather(local_dens, "mu", axis=0, tiled=True)
    count = masked.shape[0]
    flat = jnp.dot(masked.reshape(count * cols, width), dens, preferred_element_type=jnp.float32)
    half = flat.astype(jnp.bfloat16).reshape(count, cols, width)
    wide_half = with_halo(half, (("pa", 0),), rows)
    fitted = jnp.dot(
        metric_band, wide_half.reshape(3 * rows, cols * width), preferred_element_type=jnp.float32
    )
    fitted = fitted.astype(jnp.bfloat16).reshape(rows, cols, width)
    partial_block = lax.dot_general(
        fitted, masked, (((0, 2), (0, 2)), ((), ())), preferred_element_type=jnp.float32
    )
    total = lax.psum(partial_block, "pa")
    scale = 1.0 / math.sqrt(rows * lax.axis_size("pa") * width)
    return (fitted, total * scale)


def solution(mesh):
    placed = (P("pa", "mu", None), P("pa", "mu", None), P("mu", None), P("mu", None), P("pa", None))
    return jax.shard_map(
        on_device,
        mesh=mesh,
        in_specs=placed,
        out_specs=(P("pa", "mu", None), P("mu", None)),
        check_vma=False,
    )
```

profile of v0, /device:TPU:0, one launch (start us, length us, event | category | flops | bytes accessed | tf_op | source)
XLA Modules:
  0.0 338.7 jit_solution(10048462136055628702)
XLA Ops:
  0.6 0.0 copy-start
  0.6 0.7 convert_element_type.15
  1.4 6.2 %mul.42 = bf16[2,64,1,64,8,64]{5,4,3,1,0,2:T(8,128)(2,1)} broadcast(bf16[2,8]{1,0:T(2,128)(2,1)S(1)} %bitcast.30), dimensions={0,4} | broadcast | bytes 8388640 | tf_op jit(solution)/shard_map/mul | solution.py:27
  7.6 0.0 copy-start.2
  7.6 0.0 copy-start.1
  7.6 22.5 %mul.43 = bf16[8192,512]{1,0:T(8,128)(2,1)} reshape(bf16[2,64,1,64,8,64]{5,4,3,1,0,2:T(8,128)(2,1)} %mul.42) | data formatting | bytes 16777216 | tf_op jit(solution)/shard_map/mul | solution.py:27
  30.1 0.0 copy-done.2
  30.1 0.1 mul.45
  30.2 0.2 mul.46
  30.4 0.0 copy-done.1
  30.5 14.1 %all_gather.3 = bf16[512,512]{1,0:T(8,128)(2,1)S(1)} all-gather(bf16[128,512]{1,0:T(8,128)(2,1)S(1)} %mul.47), channel_id=1, replica_groups=mesh['pa'=32,'mu'=4] {'mu'}, dimensions={0}, use_global_device_ids=true | all-gather | bytes 655360 | tf_op jit(solution)/shard_map/all_gather | solution.py:35
  44.6 6.4 %bitcast_multiply_fusion = bf16[8192,512]{1,0:T(8,128)(2,1)S(1)} fusion(bf16[8192,512]{1,0:T(8,128)(2,1)} %mul.43, bf16[128,64,512]{2,1,0:T(8,128)(2,1)} %param.5), kind=kLoop, calls=%fused_computation.7 | loop fusion | flops 4194304 | bytes 25165824 | tf_op jit(solution)/shard_map/mul | solution.py:27
  50.9 6.7 %convolution_convert_fusion.1 = bf16[8192,512]{1,0:T(8,128)(2,1)} fusion(bf16[8192,512]{1,0:T(8,128)(2,1)S(1)} %bitcast_multiply_fusion, bf16[512,512]{1,0:T(8,128)(2,1)S(1)} %all_gather.3), kind=kOutput, calls=%fused_computation.6 | convolution fusion | flops 4299161600 | bytes 17301504 | tf_op jit(solution)/shard_map/dot_general | solution.py:37
  57.6 4.5 %collective-permute-start = (bf16[128,64,512]{2,1,0:T(8,128)(2,1)}, bf16[128,64,512]{2,1,0:T(8,128)(2,1)}, u32[]{:S(2)}, u32[]{:S(2)}) collective-permute-start(bf16[128,64,512]{2,1,0:T(8,128)(2,1)} %bitcast.1), channel_id=1, source_target_pairs={{0,4},{4,8},{8,12},{12,16},{16,20},{20,24},{24,28},{28,32},{32,36}... | collective-permute-start | bytes 25165832 | tf_op jit(solution)/shard_map/ppermute | solution.py:16
  62.1 1.3 collective-permute-start.1
  63.4 13.5 %concatenate.11 = bf16[128,32768]{1,0:T(8,128)(2,1)} reshape(bf16[8192,512]{1,0:T(8,128)(2,1)} %convolution_convert_fusion.1) | data formatting | bytes 16777216 | tf_op jit(solution)/shard_map/concatenate | solution.py:20
  76.9 0.1 mul.48
  77.0 0.2 mul.49
  77.2 0.0 collective-permute-done
  77.2 12.5 %copy.10 = bf16[16,8,64,512]{3,1,2,0:T(8,128)(2,1)} copy(bf16[16,8,64,512]{3,2,1,0:T(8,128)(2,1)} %bitcast.10) | data formatting | bytes 16777216
  89.7 0.0 collective-permute-done.1
  89.7 12.8 %copy.11 = bf16[16,8,64,512]{3,1,2,0:T(8,128)(2,1)} copy(bf16[16,8,64,512]{3,2,1,0:T(8,128)(2,1)} %bitcast.12) | data formatting | bytes 16777216
  102.5 0.0 copy-done
  102.5 15.4 %convolution_convert_fusion = bf16[32768,128]{1,0:T(8,128)(2,1)} fusion(bf16[128,384]{1,0:T(8,128)(2,1)S(1)} %copy-done, bf16[128,32768]{1,0:T(8,128)(2,1)} %bitcast.28, bf16[128,32768]{1,0:T(8,128)(2,1)} %concatenate.11, bf16[128,32768]{1,0:T(8,128)(2,1)} %bitcast.27), kind=kOutput, calls=%fused_computation | convolution fusion | flops 3300917248 | bytes 33652736 | tf_op jit(solution)/shard_map/dot_general | solution.py:40
  117.9 12.6 %copy.8 = bf16[128,64,512]{2,1,0:T(8,128)(2,1)} copy(bf16[128,64,512]{0,2,1:T(8,128)(2,1)} %bitcast.29) | data formatting | bytes 16777216
  130.5 8.1 %fusion.8 = f32[64,64]{1,0:T(8,128)S(1)} fusion(bf16[128,64,512]{2,1,0:T(8,128)(2,1)} %copy.8, bf16[128,64,512]{2,1,0:T(8,128)(2,1)} %param.5, bf16[128,512]{1,0:T(8,128)(2,1)S(1)} %mul.49), kind=kOutput, calls=%fused_computation.11 | convolution fusion | flops 541065216 | bytes 16924672 | tf_op jit(solution)/shard_map/dot_general | solution.py:44
  138.6 199.5 %psum.7 = f32[64,64]{1,0:T(8,128)S(1)} all-reduce(f32[64,64]{1,0:T(8,128)S(1)} %fusion.8), channel_id=1, replica_groups=mesh['pa'=32,'mu'=4] {'pa'}, use_global_device_ids=true, to_apply=%region_0.0 | all-reduce | flops 4096 | bytes 32768 | tf_op jit(solution)/shard_map/psum | solution.py:47
  338.1 0.6 broadcast_multiply_fusion
  (3 shorter events, 0.0 us)
Async XLA Ops:
  0.6 101.9 %copy-start = (bf16[128,384]{1,0:T(8,128)(2,1)S(1)}, bf16[128,384]{1,0:T(8,128)(2,1)}, u32[]{:S(2)}) copy-start(bf16[128,384]{1,0:T(8,128)(2,1)} %param.9) | copy-start | bytes 294916
  7.6 22.5 %copy-start.2 = (s32[2,8]{1,0:T(2,128)S(1)}, s32[2,8]{1,0:T(2,128)}, u32[]{:S(2)}) copy-start(s32[2,8]{1,0:T(2,128)} %param.8) | copy-start | bytes 196
  7.6 22.8 %copy-start.1 = (bf16[128,512]{1,0:T(8,128)(2,1)S(1)}, bf16[128,512]{1,0:T(8,128)(2,1)}, u32[]{:S(2)}) copy-start(bf16[128,512]{1,0:T(8,128)(2,1)} %param.7) | copy-start | bytes 393220
  57.6 19.6 %collective-permute-start = (bf16[128,64,512]{2,1,0:T(8,128)(2,1)}, bf16[128,64,512]{2,1,0:T(8,128)(2,1)}, u32[]{:S(2)}, u32[]{:S(2)}) collective-permute-start(bf16[128,64,512]{2,1,0:T(8,128)(2,1)} %bitcast.1), channel_id=1, source_target_pairs={{0,4},{4,8},{8,12},{12,16},{16,20},{20,24},{24,28},{28,32},{32,36}... | collective-permute-start | bytes 25165832 | tf_op jit(solution)/shard_map/ppermute | solution.py:16
  62.1 27.6 %collective-permute-start.1 = (bf16[128,64,512]{2,1,0:T(8,128)(2,1)}, bf16[128,64,512]{2,1,0:T(8,128)(2,1)}, u32[]{:S(2)}, u32[]{:S(2)}) collective-permute-start(bf16[128,64,512]{2,1,0:T(8,128)(2,1)} %bitcast.1), channel_id=1, source_target_pairs={{4,0},{8,4},{12,8},{16,12},{20,16},{24,20},{28,24},{32,28},{36,32}... | collective-permute-start | bytes 25165832 | tf_op jit(solution)/shard_map/ppermute | solution.py:19
where the time goes:
time: 340 us; the launch traced here: 339 us
  blocking collectives  214 us (63%)
  local copies, waits for them, and re-layouts  80.8 us (24%)
  matrix products  30.2 us (9%)
  other arithmetic  7.73 us (2%)
  starting transfers between devices  5.78 us (2%)
    psum x1, blocking collectives, on_device(): total = lax.psum(partial_block, 'pa')  199 us
    unnamed x10, local copies, waits for them, and re-layouts  37.9 us
    mul x4, local copies, waits for them, and re-layouts, on_device(): blocks * center_mask.astype(jnp.bfloat16)[:, None, :, None, :, None]  29.1 us
    dot_general x1, matrix products, on_device(): jnp.dot(metric_band, wide_half.reshape(3 * rows, cols * width), preferred...  15.4 us
    all_gather x1, blocking collectives, on_device(): dens = lax.all_gather(local_dens, 'mu', axis=0, tiled=True)  14.1 us
    concatenate x1, local copies, waits for them, and re-layouts, with_halo(): block = jnp.concatenate([low, block, high], axis=dim)  13.5 us
    dot_general x1, matrix products, on_device(): lax.dot_general(fitted, masked, (((0, 2), (0, 2)), ((), ())), preferred_e...  8.07 us
  transfers between devices with their start and end apart: 2, of which 0 were waited for; matrix products, arithmetic and copies ran while one was open for 8% of the time, Pallas kernels for 0%

commit v1 on v0

v1 whole, which is shorter than its diff:
```python
import math

import jax
import jax.numpy as jnp
from jax import lax
from jax.experimental import pallas as pl
from jax.experimental.pallas import tpu as pltpu
from jax.sharding import PartitionSpec as P

BS = 64
SIG = 128
PB = 16
QB = 8

CHUNKS = ((0, 0, 64), (128, 0, 64), (256, 0, 64), (384, 0, 32), (384, 32, 16), (384, 48, 16))
HALF_CALLS = ((0,), (1, 2, 3, 4, 5))


def half_kernel(chunks, s0, mask_ref, tc_ref, dens_ref, *refs):
    outs, scratch = refs[:-1], refs[-1]
    step = pl.program_id(0)
    cols = tc_ref.shape[1]
    mask = mask_ref[pl.ds((step * PB) // BS, 1), :]
    x = tc_ref[...].reshape(PB * cols, tc_ref.shape[2]) * mask.astype(jnp.bfloat16)
    flat = jnp.dot(x, dens_ref[...], preferred_element_type=jnp.float32)
    for t in range(scratch.shape[0]):
        scratch[t] = flat[:, t * SIG:(t + 1) * SIG]
    for out, (s, mu0, count) in zip(outs, chunks):
        for m in range(count):
            out[m] = scratch[(s - s0) // SIG, pl.ds(mu0 + m, PB, stride=cols), :].astype(jnp.bfloat16)


def half_call(tc, mask, dens, chunks):
    rows, cols, width = tc.shape
    s0 = min(s for s, _, _ in chunks)
    s1 = max(s for s, _, _ in chunks) + SIG
    return pl.pallas_call(
        lambda *refs: half_kernel(chunks, s0, *refs),
        grid=(rows // PB,),
        in_specs=[
            pl.BlockSpec(mask.shape, lambda i: (0, 0)),
            pl.BlockSpec((PB, cols, width), lambda i: (i, 0, 0)),
            pl.BlockSpec((width, s1 - s0), lambda i: (0, s0 // (s1 - s0))),
        ] if s0 % (s1 - s0) == 0 else [
            pl.BlockSpec(mask.shape, lambda i: (0, 0)),
            pl.BlockSpec((PB, cols, width), lambda i: (i, 0, 0)),
            pl.BlockSpec((width, s1 - s0), lambda i: (0, 0)),
        ],
        out_specs=[pl.BlockSpec((n, PB, SIG), lambda i: (0, i, 0)) for _, _, n in chunks],
        out_shape=[jax.ShapeDtypeStruct((n, rows, SIG), jnp.bfloat16) for _, _, n in chunks],
        scratch_shapes=[pltpu.VMEM(((s1 - s0) // SIG, PB * cols, SIG), jnp.float32)],
        compiler_params=pltpu.CompilerParams(vmem_limit_bytes=32 * 2**20),
        cost_estimate=pl.CostEstimate(
            flops=2 * rows * cols * width * (s1 - s0),
            bytes_accessed=2 * rows * cols * (width + s1 - s0),
            transcendentals=0,
        ),
    )(mask, tc, dens if s0 % (s1 - s0) == 0 else dens[:, s0:s1])


def fit_kernel(mu0, low_ref, own_ref, high_ref, metric_ref, tc_ref, mask_ref, acc_ref, *refs):
    fitted_ref, exch_ref, scratch = refs[-3:]
    count, rows, _ = own_ref.shape
    metric = metric_ref[...]

    def fit(pair, carry):
        columns = []
        for m in (2 * pair, 2 * pair + 1):
            columns.append(jnp.concatenate([low_ref[m], own_ref[m], high_ref[m]], axis=0))
        y = jnp.dot(metric, jnp.concatenate(columns, axis=1), preferred_element_type=jnp.float32)
        scratch[pl.ds(2 * pair, rows, stride=count), :] = y[:, :SIG]
        scratch[pl.ds(2 * pair + 1, rows, stride=count), :] = y[:, SIG:]
        return carry

    lax.fori_loop(0, count // 2, fit, 0, unroll=4)

    def contract(step, total):
        f = scratch[pl.ds(pl.multiple_of(step * QB * count, QB * count), QB * count), :]
        f = f.astype(jnp.bfloat16)
        first = pl.multiple_of(step * QB, QB)
        fitted_ref[pl.ds(first, QB)] = f.reshape(QB, count, SIG)
        g = f * mask_ref[pl.ds((step * QB) // BS, 1), :].astype(jnp.bfloat16)
        left = jnp.concatenate([g[q * count:(q + 1) * count] for q in range(QB)], axis=1)
        right = jnp.concatenate([tc_ref[first + q] for q in range(QB)], axis=1)
        return total + lax.dot_general(
            left, right, (((1,), (1,)), ((), ())), preferred_element_type=jnp.float32
        )

    total = lax.fori_loop(
        0, rows // QB, contract, jnp.zeros((count, tc_ref.shape[1]), jnp.float32), unroll=2
    )
    exch_ref[...] = acc_ref[...]
    exch_ref[mu0:mu0 + count, :] = acc_ref[mu0:mu0 + count, :] + total


def fit_call(chunk, low, own, high, metric, tc, mask, acc, fitted):
    s, mu0, count = chunk
    rows, cols, width = tc.shape
    block = pl.BlockSpec((count, rows, SIG), lambda i: (0, 0, 0))
    args = [low, own, high, metric, tc, mask, acc]
    in_specs = [
        block,
        block,
        block,
        pl.BlockSpec(metric.shape, lambda i: (0, 0)),
        pl.BlockSpec((rows, cols, SIG), lambda i: (0, 0, s // SIG)),
        pl.BlockSpec((mask.shape[0], SIG), lambda i: (0, s // SIG)),
        pl.BlockSpec(acc.shape, lambda i: (0, 0)),
    ]
    aliases = {}
    if fitted is not None:
        aliases = {len(args): 0}
        args.append(fitted)
        in_specs.append(pl.BlockSpec(memory_space=pl.ANY))
    return pl.pallas_call(
        lambda *refs: fit_kernel(mu0, *refs),
        grid=(1,),
        in_specs=in_specs,
        out_specs=[
            pl.BlockSpec((rows, count, SIG), lambda i: (0, mu0 // count, s // SIG)),
            pl.BlockSpec(acc.shape, lambda i: (0, 0)),
        ],
        out_shape=[
            jax.ShapeDtypeStruct(tc.shape, jnp.bfloat16),
            jax.ShapeDtypeStruct(acc.shape, jnp.float32),
        ],
        scratch_shapes=[pltpu.VMEM((rows * count, SIG), jnp.float32)],
        input_output_aliases=aliases,
        compiler_params=pltpu.CompilerParams(vmem_limit_bytes=40 * 2**20),
        cost_estimate=pl.CostEstimate(
            flops=2 * rows * count * SIG * (3 * rows + cols),
            bytes_accessed=2 * rows * SIG * (4 * count + cols),
            transcendentals=0,
        ),
    )(*args)


def gather_mu(local):
    count = lax.axis_size("mu")
    me = lax.axis_index("mu")
    parts = [local]
    for k in range(1, count):
        parts.append(lax.ppermute(local, "mu", [((i + k) % count, i) for i in range(count)]))
    twice = jnp.concatenate(parts + parts, axis=0)
    rows = local.shape[0]
    return lax.dynamic_slice_in_dim(twice, ((count - me) % count) * rows, count * rows, 0)


def rotate(value, stride, count, k):
    size = lax.axis_size("pa")
    span = stride * count
    pairs = [
        (i, (i // span) * span + ((i // stride + k) % count) * stride + i % stride)
        for i in range(size)
    ]
    return lax.ppermute(value, "pa", pairs)


def sum_pa(value):
    value = value + rotate(value, 1, 2, 1)
    for stride in (2, 8):
        parts = [rotate(value, stride, 4, k) for k in (1, 2, 3)]
        value = (value + parts[1]) + (parts[0] + parts[2])
    return value


def on_device(three_center, center_mask, density, density_mask, metric_band):
    rows, cols, width = three_center.shape
    drows = density.shape[0]
    block_mask = jnp.repeat(jnp.repeat(density_mask, BS, axis=0), BS, axis=1)
    dens = gather_mu(density * block_mask.astype(jnp.bfloat16))
    mask = jnp.repeat(center_mask[:, 0, :], BS, axis=1).astype(jnp.float32)

    count = lax.axis_size("pa")
    forward = [(i, i + 1) for i in range(count - 1)]
    backward = [(b, a) for a, b in forward]
    own = {}
    for call in HALF_CALLS:
        chunks = [CHUNKS[c] for c in call]
        for c, piece in zip(call, half_call(three_center, mask, dens, chunks)):
            own[c] = piece
    low = {c: lax.ppermute(own[c], "pa", forward) for c in own}
    high = {c: lax.ppermute(own[c], "pa", backward) for c in own}

    acc = jnp.zeros((cols, cols), jnp.float32)
    fitted = None
    for c, chunk in enumerate(CHUNKS):
        fitted, acc = fit_call(
            chunk, low[c], own[c], high[c], metric_band, three_center, mask, acc, fitted
        )
    scale = 1.0 / math.sqrt(rows * count * width)
    return (fitted, sum_pa(acc) * scale)


def solution(mesh):
    placed = (P("pa", "mu", None), P("pa", "mu", None), P("mu", None), P("mu", None), P("pa", None))
    return jax.shard_map(
        on_device,
        mesh=mesh,
        in_specs=placed,
        out_specs=(P("pa", "mu", None), P("mu", None)),
        check_vma=False,
    )
```

time: 340 us -> 194 us (0.57)
  blocking collectives: 214 us -> 0 us
  starting transfers between devices: 5.78 us -> 99.3 us
  local copies, waits for them, and re-layouts: 80.8 us -> 11.2 us
  Pallas kernels: 0 us -> 65.5 us
  matrix products: 30.2 us -> 0 us
  waiting for transfers between devices: 0.01 us -> 13 us
  other arithmetic: 7.73 us -> 2.95 us
    psum x1 -> x0, blocking collectives: 199 us -> none  [on_device(): total = lax.psum(partial_block, 'pa')]
    ppermute x2 -> x22, starting transfers between devices: 5.78 us -> 99.3 us  [the longest x6 72.9 us: on_device(): low = {c: lax.ppermute(own[c], 'pa', forward) for c in own}]
    pallas_call x0 -> x8, Pallas kernels: none -> 65.5 us  [the longest x6 41.6 us: fit_call(): pl.pallas_call(lambda *refs: fit_kernel(mu0, *refs), grid=(1,), in_specs=...]
    dot_general x3 -> x0, matrix products: 30.2 us -> none  [the longest x1 15.4 us: on_device(): jnp.dot(metric_band, wide_half.reshape(3 * rows, cols * width), preferred...]
    mul x6 -> x0, local copies, waits for them, and re-layouts: 29.4 us -> none  [the longest x4 29.1 us: on_device(): blocks * center_mask.astype(jnp.bfloat16)[:, None, :, None, :, None]]
    unnamed x10 -> x28, local copies, waits for them, and re-layouts: 37.9 us -> 10.5 us
    all_gather x1 -> x0, blocking collectives: 14.1 us -> none  [on_device(): dens = lax.all_gather(local_dens, 'mu', axis=0, tiled=True)]
    concatenate x1, local copies, waits for them, and re-layouts: 13.5 us -> 0.01 us  [gather_mu(): twice = jnp.concatenate(parts + parts, axis=0)]
  transfers between devices with their start and end apart: 2 -> 22, of which waited for: 0 -> 7; matrix products, arithmetic and copies ran while one was open for 8% -> 0% of each run, Pallas kernels for 0% -> 28%
where the time goes in v1:
time: 194 us; the launch traced here: 193 us
  starting transfers between devices  99.3 us (51%)
  Pallas kernels  65.5 us (34%)
  waiting for transfers between devices  13 us (7%)
  local copies, waits for them, and re-layouts  11.2 us (6%)
  other arithmetic  2.95 us (2%)
    ppermute x6, starting transfers between devices, on_device(): low = {c: lax.ppermute(own[c], 'pa', forward) for c in own}  72.9 us
    pallas_call x6, Pallas kernels, fit_call(): pl.pallas_call(lambda *refs: fit_kernel(mu0, *refs), grid=(1,), in_specs=...  41.6 us
    pallas_call x2, Pallas kernels, half_call(): pl.pallas_call(lambda *refs: half_kernel(chunks, s0, *refs), grid=(rows /...  23.8 us
    ppermute x7, starting transfers between devices, rotate(): return lax.ppermute(value, 'pa', pairs)  13.2 us
    unnamed x28, local copies, waits for them, and re-layouts  10.5 us
    ppermute x6, starting transfers between devices, on_device(): high = {c: lax.ppermute(own[c], 'pa', backward) for c in own}  7.72 us
    ppermute x3, waiting for transfers between devices, gather_mu(): lax.ppermute(local, 'mu', [((i + k) % count, i) for i in range(count)])  6.86 us
    ppermute x7, waiting for transfers between devices, rotate(): return lax.ppermute(value, 'pa', pairs)  6.12 us
  transfers between devices with their start and end apart: 22, of which 7 were waited for; matrix products, arithmetic and copies ran while one was open for 0% of the time, Pallas kernels for 28%

profile of v1, /device:TPU:0, one launch (start us, length us, event | category | flops | bytes accessed | tf_op | source)
XLA Modules:
  0.0 192.8 jit_solution(15489875248109868501)
XLA Ops:
  0.6 0.7 convert_element_type.21
  1.3 0.1 copy.12
  1.5 0.1 convert_element_type.22
  1.6 0.1 copy.13
  1.7 0.9 constant_dynamic-update-slice_fusion.7
  2.7 4.2 %collective-permute-start = (bf16[128,512]{1,0:T(8,128)(2,1)S(1)}, bf16[128,512]{1,0:T(8,128)(2,1)S(1)}, u32[]{:S(2)}, u32[]{:S(2)}) collective-permute-start(bf16[128,512]{1,0:T(8,128)(2,1)S(1)} %get-tuple-element.37), channel_id=1, source_target_pairs={{1,0},{2,1},{3,2},{0,3},{5,4},{6,5},{7,6},{4,7},{9,8},{10,9},{11,1... | collective-permute-start | bytes 393224 | tf_op jit(solution)/shard_map/ppermute | solution.py:143
  6.9 1.3 collective-permute-start.2
  8.1 0.7 convert_element_type.18
  9.0 3.5 %collective-permute-done = bf16[128,512]{1,0:T(8,128)(2,1)S(1)} collective-permute-done((bf16[128,512]{1,0:T(8,128)(2,1)S(1)}, bf16[128,512]{1,0:T(8,128)(2,1)S(1)}, u32[]{:S(2)}, u32[]{:S(2)}) %collective-permute-start) | collective-permute-done | bytes 131104 | tf_op jit(solution)/shard_map/ppermute | solution.py:143
  12.4 2.3 %collective-permute-done.1 = bf16[128,512]{1,0:T(8,128)(2,1)S(1)} collective-permute-done((bf16[128,512]{1,0:T(8,128)(2,1)S(1)}, bf16[128,512]{1,0:T(8,128)(2,1)S(1)}, u32[]{:S(2)}, u32[]{:S(2)}) %collective-permute-start.1) | collective-permute-done | bytes 131104 | tf_op jit(solution)/shard_map/ppermute | solution.py:143
  14.8 1.1 collective-permute-done.2
  16.0 3.4 %copy-done = bf16[128,64,512]{2,1,0:T(8,128)(2,1)S(1)} copy-done((bf16[128,64,512]{2,1,0:T(8,128)(2,1)S(1)}, bf16[128,64,512]{2,1,0:T(8,128)(2,1)}, u32[]{:S(2)}) %copy-start) | copy-done | bytes 8388632
  19.4 6.6 %shard_map.69.refs_1_ = bf16[64,128,128]{2,1,0:T(8,128)(2,1)S(1)} custom-call(f32[2,512]{1,0:T(2,128)S(1)} %convert_element_type.20.refs_0_.refs_5_, bf16[128,64,512]{2,1,0:T(8,128)(2,1)S(1)} %copy-done, bf16[512,512]{1,0:T(8,128)(2,1)S(1)} %constant_dynamic-slice_fusion.refs_2_), custom_call_target="tpu_custom_call" | custom-call | flops 1073741824 | bytes 10485760 | tf_op jit(solution)/shard_map/pallas_call | solution.py:37
  25.9 2.9 %collective-permute-start.13 = (bf16[64,128,128]{2,1,0:T(8,128)(2,1)S(1)}, bf16[64,128,128]{2,1,0:T(8,128)(2,1)}, u32[]{:S(2)}, u32[]{:S(2)}) collective-permute-start(bf16[64,128,128]{2,1,0:T(8,128)(2,1)S(1)} %shard_map.69.refs_1_), channel_id=1, source_target_pairs={{0,4},{4,8},{8,12},{12,16},{16,20},{20,24},{24,28},{28,32},{32,36}... | collective-permute-start | bytes 6291464 | tf_op jit(solution)/shard_map/ppermute | solution.py:182
  28.9 3.4 %copy-done.1 = bf16[128,64,512]{2,1,0:T(8,128)(2,1)S(1)} copy-done((bf16[128,64,512]{2,1,0:T(8,128)(2,1)S(1)}, bf16[128,64,512]{2,1,0:T(8,128)(2,1)}, u32[]{:S(2)}) %copy-start.1) | copy-done | bytes 8388632
  32.3 17.3 %shard_map.68 = (bf16[64,128,128]{2,1,0:T(8,128)(2,1)S(1)}, bf16[64,128,128]{2,1,0:T(8,128)(2,1)S(1)}, bf16[32,128,128]{2,1,0:T(8,128)(2,1)S(1)}, bf16[16,128,128]{2,1,0:T(8,128)(2,1)}, bf16[16,128,128]{2,1,0:T(8,128)(2,1)}) custom-call(f32[2,512]{1,0:T(2,128)S(1)} %convert_element_type.20.refs_0_.refs_5_, bf16[128,64,512]{2,1,0:T(8,128)(2,1)S(1)} %copy-done.1, ...), custom_call_target="tpu_custom_call" | custom-call | flops 3221225472 | bytes 14680064 | tf_op jit(solution)/shard_map/pallas_call | solution.py:37
  49.6 2.6 %collective-permute-start.7 = (bf16[32,128,128]{2,1,0:T(8,128)(2,1)S(1)}, bf16[32,128,128]{2,1,0:T(8,128)(2,1)S(1)}, u32[]{:S(2)}, u32[]{:S(2)}) collective-permute-start(bf16[32,128,128]{2,1,0:T(8,128)(2,1)S(1)} %get-tuple-element.21.refs_1_), channel_id=1, source_target_pairs={{0,4},{4,8},{8,12},{12,16},{16,20},{20,24},{24,28},{28,32},{32,36}... | collective-permute-start | bytes 3145736 | tf_op jit(solution)/shard_map/ppermute | solution.py:182
  52.1 1.3 collective-permute-start.14
  53.4 3.2 %collective-permute-start.11 = (bf16[64,128,128]{2,1,0:T(8,128)(2,1)S(1)}, bf16[64,128,128]{2,1,0:T(8,128)(2,1)S(1)}, u32[]{:S(2)}, u32[]{:S(2)}) collective-permute-start(bf16[64,128,128]{2,1,0:T(8,128)(2,1)S(1)} %get-tuple-element.23.refs_1_), channel_id=1, source_target_pairs={{0,4},{4,8},{8,12},{12,16},{16,20},{20,24},{24,28},{28,32},{32,36}... | collective-permute-start | bytes 6291464 | tf_op jit(solution)/shard_map/ppermute | solution.py:182
  56.6 1.3 collective-permute-start.12
  57.9 1.0 copy-done.7
  58.9 1.3 collective-permute-start.10
  60.2 8.6 %collective-permute-start.9 = (bf16[64,128,128]{2,1,0:T(8,128)(2,1)S(1)}, bf16[64,128,128]{2,1,0:T(8,128)(2,1)S(1)}, u32[]{:S(2)}, u32[]{:S(2)}) collective-permute-start(bf16[64,128,128]{2,1,0:T(8,128)(2,1)S(1)} %get-tuple-element.22.refs_1_), channel_id=1, source_target_pairs={{0,4},{4,8},{8,12},{12,16},{16,20},{20,24},{24,28},{28,32},{32,36}... | collective-permute-start | bytes 6291464 | tf_op jit(solution)/shard_map/ppermute | solution.py:182
  68.8 1.3 collective-permute-start.8
  70.1 18.9 %collective-permute-start.5 = (bf16[16,128,128]{2,1,0:T(8,128)(2,1)}, bf16[16,128,128]{2,1,0:T(8,128)(2,1)}, u32[]{:S(2)}, u32[]{:S(2)}) collective-permute-start(bf16[16,128,128]{2,1,0:T(8,128)(2,1)} %get-tuple-element.20.refs_1_), channel_id=1, source_target_pairs={{0,4},{4,8},{8,12},{12,16},{16,20},{20,24},{24,28},{28,32},{32,36}... | collective-permute-start | bytes 1572872 | tf_op jit(solution)/shard_map/ppermute | solution.py:182
  89.0 1.3 collective-permute-start.6
  90.3 1.3 copy-done.3
  91.6 36.8 %collective-permute-start.3 = (bf16[16,128,128]{2,1,0:T(8,128)(2,1)}, bf16[16,128,128]{2,1,0:T(8,128)(2,1)}, u32[]{:S(2)}, u32[]{:S(2)}) collective-permute-start(bf16[16,128,128]{2,1,0:T(8,128)(2,1)} %get-tuple-element.19.refs_1_), channel_id=1, source_target_pairs={{0,4},{4,8},{8,12},{12,16},{16,20},{20,24},{24,28},{28,32},{32,36}... | collective-permute-start | bytes 1572872 | tf_op jit(solution)/shard_map/ppermute | solution.py:182
  128.4 1.4 copy-done.5
  129.8 1.3 collective-permute-start.4
  131.1 9.4 %shard_map.70 = (bf16[128,64,512]{2,1,0:T(8,128)(2,1)}, f32[64,64]{1,0:T(8,128)S(1)}) custom-call(bf16[64,128,128]{2,1,0:T(8,128)(2,1)} %collective-permute-done.13.refs_0_, bf16[64,128,128]{2,1,0:T(8,128)(2,1)S(1)} %shard_map.69.refs_1_, bf16[64,128,128]{2,1,0:T(8,128)(2,1)S(1)} %collective-permute-done.14.refs_2_, bf16[128,384]{1,0:T(8,128)(2,1)S(1)} %copy-done.2, ...), custom_call_target="tpu_custom_call" | custom-call | flops 939524096 | bytes 10485760 | tf_op jit(solution)/shard_map/pallas_call | solution.py:115
  140.5 8.9 %shard_map.71 = (bf16[128,64,512]{2,1,0:T(8,128)(2,1)}, f32[64,64]{1,0:T(8,128)S(1)}) custom-call(bf16[64,128,128]{2,1,0:T(8,128)(2,1)S(1)} %collective-permute-done.11.refs_0_, bf16[64,128,128]{2,1,0:T(8,128)(2,1)S(1)} %get-tuple-element.23.refs_1_, bf16[64,128,128]{2,1,0:T(8,128)(2,1)S(1)} %collective-permute-done.12.refs_2_, ...), custom_call_target="tpu_custom_call", output_to_operand_aliasing={{0}: (7, {})} | custom-call | flops 939524096 | bytes 10485760 | tf_op jit(solution)/shard_map/pallas_call | solution.py:115
  149.4 8.9 %shard_map.72 = (bf16[128,64,512]{2,1,0:T(8,128)(2,1)}, f32[64,64]{1,0:T(8,128)S(1)}) custom-call(bf16[64,128,128]{2,1,0:T(8,128)(2,1)S(1)} %copy-done.6, bf16[64,128,128]{2,1,0:T(8,128)(2,1)S(1)} %get-tuple-element.22.refs_1_, bf16[64,128,128]{2,1,0:T(8,128)(2,1)S(1)} %copy-done.4, bf16[128,384]{1,0:T(8,128)(2,1)S(1)} %copy-done.2, ...), custom_call_target="tpu_custom_call", output_to_operand_aliasing={{0}: (7, {})} | custom-call | flops 939524096 | bytes 10485760 | tf_op jit(solution)/shard_map/pallas_call | solution.py:115
  158.3 5.9 %shard_map.73 = (bf16[128,64,512]{2,1,0:T(8,128)(2,1)}, f32[64,64]{1,0:T(8,128)S(1)}) custom-call(bf16[32,128,128]{2,1,0:T(8,128)(2,1)S(1)} %copy-done.8, bf16[32,128,128]{2,1,0:T(8,128)(2,1)S(1)} %get-tuple-element.21.refs_1_, bf16[32,128,128]{2,1,0:T(8,128)(2,1)} %collective-permute-done.8.refs_2_, ...), custom_call_target="tpu_custom_call", output_to_operand_aliasing={{0}: (7, {})} | custom-call | flops 469762048 | bytes 6291456 | tf_op jit(solution)/shard_map/pallas_call | solution.py:115
  164.2 4.4 %shard_map.74 = (bf16[128,64,512]{2,1,0:T(8,128)(2,1)}, f32[64,64]{1,0:T(8,128)S(1)}) custom-call(bf16[16,128,128]{2,1,0:T(8,128)(2,1)} %collective-permute-done.5.refs_0_, bf16[16,128,128]{2,1,0:T(8,128)(2,1)} %get-tuple-element.20.refs_1_, bf16[16,128,128]{2,1,0:T(8,128)(2,1)} %collective-permute-done.6.refs_2_, ...), custom_call_target="tpu_custom_call", output_to_operand_aliasing={{0}: (7, {})} | custom-call | flops 234881024 | bytes 4194304 | tf_op jit(solution)/shard_map/pallas_call | solution.py:115
  168.6 4.2 %shard_map.75 = (bf16[128,64,512]{2,1,0:T(8,128)(2,1)}, f32[64,64]{1,0:T(8,128)S(1)}) custom-call(bf16[16,128,128]{2,1,0:T(8,128)(2,1)} %collective-permute-done.3.refs_0_, bf16[16,128,128]{2,1,0:T(8,128)(2,1)} %get-tuple-element.19.refs_1_, bf16[16,128,128]{2,1,0:T(8,128)(2,1)S(1)} %collective-permute-done.4.refs_2_, ...), custom_call_target="tpu_custom_call", output_to_operand_aliasing={{0}: (7, {})} | custom-call | flops 234881024 | bytes 4194304 | tf_op jit(solution)/shard_map/pallas_call | solution.py:115
  172.8 1.1 collective-permute-start.15
  173.9 0.9 collective-permute-done.15
  174.8 2.2 %collective-permute-start.16 = (f32[64,64]{1,0:T(8,128)S(1)}, f32[64,64]{1,0:T(8,128)S(1)}, u32[]{:S(2)}, u32[]{:S(2)}) collective-permute-start(f32[64,64]{1,0:T(8,128)S(1)} %add.30), channel_id=1, source_target_pairs={{0,16},{4,20},{8,24},{12,28},{16,0},{20,4},{24,8},{28,12},{32,48},... | collective-permute-start | bytes 49160 | tf_op jit(solution)/shard_map/ppermute | solution.py:156
  177.0 2.7 %collective-permute-start.17 = (f32[64,64]{1,0:T(8,128)S(1)}, f32[64,64]{1,0:T(8,128)S(1)}, u32[]{:S(2)}, u32[]{:S(2)}) collective-permute-start(f32[64,64]{1,0:T(8,128)S(1)} %add.30), channel_id=1, source_target_pairs={{0,8},{4,12},{8,16},{12,20},{16,24},{20,28},{24,0},{28,4},{32,40},... | collective-permute-start | bytes 49160 | tf_op jit(solution)/shard_map/ppermute | solution.py:156
  179.7 0.5 collective-permute-start.18
  180.3 1.9 collective-permute-done.17
  182.2 1.5 collective-permute-done.18
  183.6 3.4 %collective-permute-start.19 = (f32[64,64]{1,0:T(8,128)S(1)}, f32[64,64]{1,0:T(8,128)S(1)}, u32[]{:S(2)}, u32[]{:S(2)}) collective-permute-start(f32[64,64]{1,0:T(8,128)S(1)} %add_add_fusion), channel_id=1, source_target_pairs={{0,64},{4,68},{8,72},{12,76},{16,80},{20,84},{24,88},{28,92},{32,9... | collective-permute-start | bytes 49160 | tf_op jit(solution)/shard_map/ppermute | solution.py:156
  187.0 0.7 collective-permute-start.20
  187.7 2.6 %collective-permute-start.21 = (f32[64,64]{1,0:T(8,128)S(1)}, f32[64,64]{1,0:T(8,128)S(1)}, u32[]{:S(2)}, u32[]{:S(2)}) collective-permute-start(f32[64,64]{1,0:T(8,128)S(1)} %add_add_fusion), channel_id=1, source_target_pairs={{0,96},{4,100},{8,104},{12,108},{16,112},{20,116},{24,120},{28,124... | collective-permute-start | bytes 49160 | tf_op jit(solution)/shard_map/ppermute | solution.py:156
  190.3 1.9 collective-permute-done.20
  192.2 0.6 add_multiply_fusion
  (50 shorter events, 0.5 us)
Async XLA Ops:
  2.7 9.8 %collective-permute-start = (bf16[128,512]{1,0:T(8,128)(2,1)S(1)}, bf16[128,512]{1,0:T(8,128)(2,1)S(1)}, u32[]{:S(2)}, u32[]{:S(2)}) collective-permute-start(bf16[128,512]{1,0:T(8,128)(2,1)S(1)} %get-tuple-element.37), channel_id=1, source_target_pairs={{1,0},{2,1},{3,2},{0,3},{5,4},{6,5},{7,6},{4,7},{9,8},{10,9},{11,1... | collective-permute-start | bytes 393224 | tf_op jit(solution)/shard_map/ppermute | solution.py:143
  6.9 7.9 %collective-permute-start.1 = (bf16[128,512]{1,0:T(8,128)(2,1)S(1)}, bf16[128,512]{1,0:T(8,128)(2,1)S(1)}, u32[]{:S(2)}, u32[]{:S(2)}) collective-permute-start(bf16[128,512]{1,0:T(8,128)(2,1)S(1)} %get-tuple-element.37), channel_id=1, source_target_pairs={{2,0},{3,1},{0,2},{1,3},{6,4},{7,5},{4,6},{5,7},{10,8},{11,9},{8,1... | collective-permute-start | bytes 393224 | tf_op jit(solution)/shard_map/ppermute | solution.py:143
  6.9 9.0 %collective-permute-start.2 = (bf16[128,512]{1,0:T(8,128)(2,1)S(1)}, bf16[128,512]{1,0:T(8,128)(2,1)S(1)}, u32[]{:S(2)}, u32[]{:S(2)}) collective-permute-start(bf16[128,512]{1,0:T(8,128)(2,1)S(1)} %get-tuple-element.37), channel_id=1, source_target_pairs={{3,0},{0,1},{1,2},{2,3},{7,4},{4,5},{5,6},{6,7},{11,8},{8,9},{9,10... | collective-permute-start | bytes 393224 | tf_op jit(solution)/shard_map/ppermute | solution.py:143
  16.0 3.4 %copy-start = (bf16[128,64,512]{2,1,0:T(8,128)(2,1)S(1)}, bf16[128,64,512]{2,1,0:T(8,128)(2,1)}, u32[]{:S(2)}) copy-start(bf16[128,64,512]{2,1,0:T(8,128)(2,1)} %refs_4_.11) | copy-start | bytes 25165828
  25.9 34.3 %collective-permute-start.13 = (bf16[64,128,128]{2,1,0:T(8,128)(2,1)S(1)}, bf16[64,128,128]{2,1,0:T(8,128)(2,1)}, u32[]{:S(2)}, u32[]{:S(2)}) collective-permute-start(bf16[64,128,128]{2,1,0:T(8,128)(2,1)S(1)} %shard_map.69.refs_1_), channel_id=1, source_target_pairs={{0,4},{4,8},{8,12},{12,16},{16,20},{20,24},{24,28},{28,32},{32,36}... | collective-permute-start | bytes 6291464 | tf_op jit(solution)/shard_map/ppermute | solution.py:182
  28.9 3.4 %copy-start.1 = (bf16[128,64,512]{2,1,0:T(8,128)(2,1)S(1)}, bf16[128,64,512]{2,1,0:T(8,128)(2,1)}, u32[]{:S(2)}) copy-start(bf16[128,64,512]{2,1,0:T(8,128)(2,1)} %refs_4_.11) | copy-start | bytes 25165828
  32.3 98.8 %copy-start.2 = (bf16[128,384]{1,0:T(8,128)(2,1)S(1)}, bf16[128,384]{1,0:T(8,128)(2,1)}, u32[]{:S(2)}) copy-start(bf16[128,384]{1,0:T(8,128)(2,1)} %refs_3_.11) | copy-start | bytes 294916
  49.6 8.3 %collective-permute-start.7 = (bf16[32,128,128]{2,1,0:T(8,128)(2,1)S(1)}, bf16[32,128,128]{2,1,0:T(8,128)(2,1)S(1)}, u32[]{:S(2)}, u32[]{:S(2)}) collective-permute-start(bf16[32,128,128]{2,1,0:T(8,128)(2,1)S(1)} %get-tuple-element.21.refs_1_), channel_id=1, source_target_pairs={{0,4},{4,8},{8,12},{12,16},{16,20},{20,24},{24,28},{28,32},{32,36}... | collective-permute-start | bytes 3145736 | tf_op jit(solution)/shard_map/ppermute | solution.py:182
  52.1 16.6 %collective-permute-start.14 = (bf16[64,128,128]{2,1,0:T(8,128)(2,1)S(1)}, bf16[64,128,128]{2,1,0:T(8,128)(2,1)S(1)}, u32[]{:S(2)}, u32[]{:S(2)}) collective-permute-start(bf16[64,128,128]{2,1,0:T(8,128)(2,1)S(1)} %shard_map.69.refs_1_), channel_id=1, source_target_pairs={{4,0},{8,4},{12,8},{16,12},{20,16},{24,20},{28,24},{32,28},{36,32}... | collective-permute-start | bytes 6291464 | tf_op jit(solution)/shard_map/ppermute | solution.py:183
  53.4 16.6 %collective-permute-start.11 = (bf16[64,128,128]{2,1,0:T(8,128)(2,1)S(1)}, bf16[64,128,128]{2,1,0:T(8,128)(2,1)S(1)}, u32[]{:S(2)}, u32[]{:S(2)}) collective-permute-start(bf16[64,128,128]{2,1,0:T(8,128)(2,1)S(1)} %get-tuple-element.23.refs_1_), channel_id=1, source_target_pairs={{0,4},{4,8},{8,12},{12,16},{16,20},{20,24},{24,28},{28,32},{32,36}... | collective-permute-start | bytes 6291464 | tf_op jit(solution)/shard_map/ppermute | solution.py:182
  56.6 32.4 %collective-permute-start.12 = (bf16[64,128,128]{2,1,0:T(8,128)(2,1)S(1)}, bf16[64,128,128]{2,1,0:T(8,128)(2,1)S(1)}, u32[]{:S(2)}, u32[]{:S(2)}) collective-permute-start(bf16[64,128,128]{2,1,0:T(8,128)(2,1)S(1)} %get-tuple-element.23.refs_1_), channel_id=1, source_target_pairs={{4,0},{8,4},{12,8},{16,12},{20,16},{24,20},{28,24},{32,28},{36,32}... | collective-permute-start | bytes 6291464 | tf_op jit(solution)/shard_map/ppermute | solution.py:183
  57.9 1.0 copy-start.7
  58.9 31.4 %collective-permute-start.10 = (bf16[64,128,128]{2,1,0:T(8,128)(2,1)S(1)}, bf16[64,128,128]{2,1,0:T(8,128)(2,1)S(1)}, u32[]{:S(2)}, u32[]{:S(2)}) collective-permute-start(bf16[64,128,128]{2,1,0:T(8,128)(2,1)S(1)} %get-tuple-element.22.refs_1_), channel_id=1, source_target_pairs={{4,0},{8,4},{12,8},{16,12},{20,16},{24,20},{28,24},{32,28},{36,32}... | collective-permute-start | bytes 6291464 | tf_op jit(solution)/shard_map/ppermute | solution.py:183
  60.2 68.2 %collective-permute-start.9 = (bf16[64,128,128]{2,1,0:T(8,128)(2,1)S(1)}, bf16[64,128,128]{2,1,0:T(8,128)(2,1)S(1)}, u32[]{:S(2)}, u32[]{:S(2)}) collective-permute-start(bf16[64,128,128]{2,1,0:T(8,128)(2,1)S(1)} %get-tuple-element.22.refs_1_), channel_id=1, source_target_pairs={{0,4},{4,8},{8,12},{12,16},{16,20},{20,24},{24,28},{28,32},{32,36}... | collective-permute-start | bytes 6291464 | tf_op jit(solution)/shard_map/ppermute | solution.py:182
  68.8 89.5 %collective-permute-start.8 = (bf16[32,128,128]{2,1,0:T(8,128)(2,1)S(1)}, bf16[32,128,128]{2,1,0:T(8,128)(2,1)}, u32[]{:S(2)}, u32[]{:S(2)}) collective-permute-start(bf16[32,128,128]{2,1,0:T(8,128)(2,1)S(1)} %get-tuple-element.21.refs_1_), channel_id=1, source_target_pairs={{4,0},{8,4},{12,8},{16,12},{20,16},{24,20},{28,24},{32,28},{36,32}... | collective-permute-start | bytes 3145736 | tf_op jit(solution)/shard_map/ppermute | solution.py:183
  70.1 94.1 %collective-permute-start.5 = (bf16[16,128,128]{2,1,0:T(8,128)(2,1)}, bf16[16,128,128]{2,1,0:T(8,128)(2,1)}, u32[]{:S(2)}, u32[]{:S(2)}) collective-permute-start(bf16[16,128,128]{2,1,0:T(8,128)(2,1)} %get-tuple-element.20.refs_1_), channel_id=1, source_target_pairs={{0,4},{4,8},{8,12},{12,16},{16,20},{20,24},{24,28},{28,32},{32,36}... | collective-permute-start | bytes 1572872 | tf_op jit(solution)/shard_map/ppermute | solution.py:182
  89.0 75.2 %collective-permute-start.6 = (bf16[16,128,128]{2,1,0:T(8,128)(2,1)}, bf16[16,128,128]{2,1,0:T(8,128)(2,1)}, u32[]{:S(2)}, u32[]{:S(2)}) collective-permute-start(bf16[16,128,128]{2,1,0:T(8,128)(2,1)} %get-tuple-element.20.refs_1_), channel_id=1, source_target_pairs={{4,0},{8,4},{12,8},{16,12},{20,16},{24,20},{28,24},{32,28},{36,32}... | collective-permute-start | bytes 1572872 | tf_op jit(solution)/shard_map/ppermute | solution.py:183
  90.3 1.3 copy-start.3
  91.6 77.0 %collective-permute-start.3 = (bf16[16,128,128]{2,1,0:T(8,128)(2,1)}, bf16[16,128,128]{2,1,0:T(8,128)(2,1)}, u32[]{:S(2)}, u32[]{:S(2)}) collective-permute-start(bf16[16,128,128]{2,1,0:T(8,128)(2,1)} %get-tuple-element.19.refs_1_), channel_id=1, source_target_pairs={{0,4},{4,8},{8,12},{12,16},{16,20},{20,24},{24,28},{28,32},{32,36}... | collective-permute-start | bytes 1572872 | tf_op jit(solution)/shard_map/ppermute | solution.py:182
  128.4 1.4 copy-start.5
  129.8 38.8 %collective-permute-start.4 = (bf16[16,128,128]{2,1,0:T(8,128)(2,1)}, bf16[16,128,128]{2,1,0:T(8,128)(2,1)S(1)}, u32[]{:S(2)}, u32[]{:S(2)}) collective-permute-start(bf16[16,128,128]{2,1,0:T(8,128)(2,1)} %get-tuple-element.19.refs_1_), channel_id=1, source_target_pairs={{4,0},{8,4},{12,8},{16,12},{20,16},{24,20},{28,24},{32,28},{36,32}... | collective-permute-start | bytes 1572872 | tf_op jit(solution)/shard_map/ppermute | solution.py:183
  140.5 8.9 %copy-start.4 = (bf16[64,128,128]{2,1,0:T(8,128)(2,1)S(1)}, bf16[64,128,128]{2,1,0:T(8,128)(2,1)}, u32[]{:S(2)}) copy-start(bf16[64,128,128]{2,1,0:T(8,128)(2,1)} %copy-done.3) | copy-start | bytes 6291460
  140.5 8.9 %copy-start.6 = (bf16[64,128,128]{2,1,0:T(8,128)(2,1)S(1)}, bf16[64,128,128]{2,1,0:T(8,128)(2,1)}, u32[]{:S(2)}) copy-start(bf16[64,128,128]{2,1,0:T(8,128)(2,1)} %copy-done.5) | copy-start | bytes 6291460
  149.3 8.9 %slice-start = ((s8[8388608]{0:T(1024)(128)(4,1)}), s8[4194304]{0:T(1024)(128)(4,1)S(1)}, s32[]{:S(2)}) async-start(s8[8388608]{0:T(1024)(128)(4,1)} %bitcast.4), calls=%async_computation | async-start | bytes 8388608
  149.3 8.9 %slice-start.1 = ((s8[8388608]{0:T(1024)(128)(4,1)}), s8[4194304]{0:T(1024)(128)(4,1)S(1)}, s32[]{:S(2)}) async-start(s8[8388608]{0:T(1024)(128)(4,1)} %bitcast.4), calls=%async_computation.1 | async-start | bytes 8388608
  149.3 8.9 %copy-start.8 = (bf16[32,128,128]{2,1,0:T(8,128)(2,1)S(1)}, bf16[32,128,128]{2,1,0:T(8,128)(2,1)}, u32[]{:S(2)}) copy-start(bf16[32,128,128]{2,1,0:T(8,128)(2,1)} %copy-done.7) | copy-start | bytes 3145732
  172.8 2.0 %collective-permute-start.15 = (f32[64,64]{1,0:T(8,128)S(1)}, f32[64,64]{1,0:T(8,128)S(1)}, u32[]{:S(2)}, u32[]{:S(2)}) collective-permute-start(f32[64,64]{1,0:T(8,128)S(1)} %get-tuple-element.35), channel_id=1, source_target_pairs={{0,4},{4,0},{8,12},{12,8},{16,20},{20,16},{24,28},{28,24},{32,36},... | collective-permute-start | bytes 49160 | tf_op jit(solution)/shard_map/ppermute | solution.py:156
  174.8 5.5 %collective-permute-start.16 = (f32[64,64]{1,0:T(8,128)S(1)}, f32[64,64]{1,0:T(8,128)S(1)}, u32[]{:S(2)}, u32[]{:S(2)}) collective-permute-start(f32[64,64]{1,0:T(8,128)S(1)} %add.30), channel_id=1, source_target_pairs={{0,16},{4,20},{8,24},{12,28},{16,0},{20,4},{24,8},{28,12},{32,48},... | collective-permute-start | bytes 49160 | tf_op jit(solution)/shard_map/ppermute | solution.py:156
  177.0 5.1 %collective-permute-start.17 = (f32[64,64]{1,0:T(8,128)S(1)}, f32[64,64]{1,0:T(8,128)S(1)}, u32[]{:S(2)}, u32[]{:S(2)}) collective-permute-start(f32[64,64]{1,0:T(8,128)S(1)} %add.30), channel_id=1, source_target_pairs={{0,8},{4,12},{8,16},{12,20},{16,24},{20,28},{24,0},{28,4},{32,40},... | collective-permute-start | bytes 49160 | tf_op jit(solution)/shard_map/ppermute | solution.py:156
  179.7 3.9 %collective-permute-start.18 = (f32[64,64]{1,0:T(8,128)S(1)}, f32[64,64]{1,0:T(8,128)S(1)}, u32[]{:S(2)}, u32[]{:S(2)}) collective-permute-start(f32[64,64]{1,0:T(8,128)S(1)} %add.30), channel_id=1, source_target_pairs={{0,24},{4,28},{8,0},{12,4},{16,8},{20,12},{24,16},{28,20},{32,56},... | collective-permute-start | bytes 49160 | tf_op jit(solution)/shard_map/ppermute | solution.py:156
  183.6 6.6 %collective-permute-start.19 = (f32[64,64]{1,0:T(8,128)S(1)}, f32[64,64]{1,0:T(8,128)S(1)}, u32[]{:S(2)}, u32[]{:S(2)}) collective-permute-start(f32[64,64]{1,0:T(8,128)S(1)} %add_add_fusion), channel_id=1, source_target_pairs={{0,64},{4,68},{8,72},{12,76},{16,80},{20,84},{24,88},{28,92},{32,9... | collective-permute-start | bytes 49160 | tf_op jit(solution)/shard_map/ppermute | solution.py:156
  187.0 5.1 %collective-permute-start.20 = (f32[64,64]{1,0:T(8,128)S(1)}, f32[64,64]{1,0:T(8,128)S(1)}, u32[]{:S(2)}, u32[]{:S(2)}) collective-permute-start(f32[64,64]{1,0:T(8,128)S(1)} %add_add_fusion), channel_id=1, source_target_pairs={{0,32},{4,36},{8,40},{12,44},{16,48},{20,52},{24,56},{28,60},{32,6... | collective-permute-start | bytes 49160 | tf_op jit(solution)/shard_map/ppermute | solution.py:156
  187.7 4.5 %collective-permute-start.21 = (f32[64,64]{1,0:T(8,128)S(1)}, f32[64,64]{1,0:T(8,128)S(1)}, u32[]{:S(2)}, u32[]{:S(2)}) collective-permute-start(f32[64,64]{1,0:T(8,128)S(1)} %add_add_fusion), channel_id=1, source_target_pairs={{0,96},{4,100},{8,104},{12,108},{16,112},{20,116},{24,120},{28,124... | collective-permute-start | bytes 49160 | tf_op jit(solution)/shard_map/ppermute | solution.py:156

commit v2 on v1

v2 whole, which is shorter than its diff:
```python
import math

import jax
import jax.numpy as jnp
from jax import lax
from jax.experimental import pallas as pl
from jax.experimental.pallas import tpu as pltpu
from jax.sharding import PartitionSpec as P

BS = 64
SIG = 128
PB = 16
QB = 16
VMEM_BYTES = 56 * 2**20

RAW = (0, 4, 48, 16)
CHUNKS = ((0, 1, 0, 48), (128, 1, 0, 48), (256, 1, 0, 48), (384, 1, 0, 32), (384, 1, 32, 16))


def half_kernel(chunks, mu0, cols, mask_ref, tc_ref, dens_ref, *refs):
    outs, scratch = refs[:-1], refs[-1]
    x = tc_ref[...].reshape(PB * cols, tc_ref.shape[2])
    if mask_ref is not None:
        mask = mask_ref[pl.ds((pl.program_id(0) * PB) // BS, 1), :]
        x = x * mask.astype(jnp.bfloat16)
    flat = jnp.dot(x, dens_ref[...], preferred_element_type=jnp.float32)
    s0 = min(s for s, _, _, _ in chunks)
    pitch = cols + 1
    for t in range(scratch.shape[0]):
        for p in range(PB):
            scratch[t, p * pitch:p * pitch + cols] = flat[
                p * cols:(p + 1) * cols, t * SIG:(t + 1) * SIG
            ]
    for out, (s, tiles, first, count) in zip(outs, chunks):
        for t in range(tiles):
            for m in range(count):
                out[m, :, t * SIG:(t + 1) * SIG] = scratch[
                    (s - s0) // SIG + t, pl.ds(first - mu0 + m, PB, stride=pitch), :
                ].astype(jnp.bfloat16)


def half_call(tc, mask, dens, chunks, mu0, cols):
    rows, _, width = tc.shape
    s0 = min(s for s, _, _, _ in chunks)
    s1 = max(s + t * SIG for s, t, _, _ in chunks)
    args = [tc, dens[:, s0:s1]]
    in_specs = [
        pl.BlockSpec((PB, cols, width), lambda i: (i, 0, 0)),
        pl.BlockSpec((width, s1 - s0), lambda i: (0, 0)),
    ]
    if mask is not None:
        args.insert(0, mask)
        in_specs.insert(0, pl.BlockSpec(mask.shape, lambda i: (0, 0)))

    def kernel(*refs):
        half_kernel(chunks, mu0, cols, *(refs if mask is not None else (None,) + refs))

    return pl.pallas_call(
        kernel,
        grid=(rows // PB,),
        in_specs=in_specs,
        out_specs=[pl.BlockSpec((n, PB, t * SIG), lambda i: (0, i, 0)) for _, t, _, n in chunks],
        out_shape=[
            jax.ShapeDtypeStruct((n, rows, t * SIG), jnp.bfloat16) for _, t, _, n in chunks
        ],
        scratch_shapes=[
            pltpu.VMEM(((s1 - s0) // SIG, PB * (cols + 1) + 8, SIG), jnp.float32)
        ],
        compiler_params=pltpu.CompilerParams(vmem_limit_bytes=VMEM_BYTES),
        cost_estimate=pl.CostEstimate(
            flops=2 * rows * cols * width * (s1 - s0),
            bytes_accessed=2 * rows * cols * (width + s1 - s0),
            transcendentals=0,
        ),
    )(*args)


def fit_kernel(mu0, low_ref, own_ref, high_ref, metric_ref, tc_ref, mask_ref, acc_ref, *refs):
    fitted_ref, exch_ref, scratch = refs[-3:]
    count, rows, _ = own_ref.shape
    pitch = count + 1
    metric = metric_ref[...]

    def fit(pair, carry):
        columns = []
        for m in (2 * pair, 2 * pair + 1):
            columns.append(jnp.concatenate([low_ref[m], own_ref[m], high_ref[m]], axis=0))
        y = jnp.dot(metric, jnp.concatenate(columns, axis=1), preferred_element_type=jnp.float32)
        scratch[pl.ds(2 * pair, rows, stride=pitch), :] = y[:, :SIG]
        scratch[pl.ds(2 * pair + 1, rows, stride=pitch), :] = y[:, SIG:]
        return carry

    lax.fori_loop(0, count // 2, fit, 0, unroll=4)

    def contract(step, total):
        first = pl.multiple_of(step * QB, QB)
        fs = []
        for q in range(QB):
            fs.append(scratch[pl.ds((first + q) * pitch, count), :].astype(jnp.bfloat16))
            fitted_ref[first + q] = fs[-1]
        mask = mask_ref[pl.ds((step * QB) // BS, 1), :].astype(jnp.bfloat16)
        left = jnp.concatenate([f * mask for f in fs], axis=1)
        right = jnp.concatenate([tc_ref[first + q] for q in range(QB)], axis=1)
        return total + lax.dot_general(
            left, right, (((1,), (1,)), ((), ())), preferred_element_type=jnp.float32
        )

    total = lax.fori_loop(
        0, rows // QB, contract, jnp.zeros((count, tc_ref.shape[1]), jnp.float32), unroll=2
    )

    @pl.when(pl.program_id(0) == 0)
    def _():
        exch_ref[...] = acc_ref[...]

    exch_ref[mu0:mu0 + count, :] += total


def fit_call(chunk, low, own, high, metric, tc, mask, acc, fitted):
    s, tiles, mu0, count = chunk
    rows, cols, width = tc.shape
    block = pl.BlockSpec((count, rows, SIG), lambda i: (0, 0, i))
    args = [low, own, high, metric, tc, mask, acc]
    in_specs = [
        block,
        block,
        block,
        pl.BlockSpec(metric.shape, lambda i: (0, 0)),
        pl.BlockSpec((rows, cols, SIG), lambda i: (0, 0, s // SIG + i)),
        pl.BlockSpec((mask.shape[0], SIG), lambda i: (0, s // SIG + i)),
        pl.BlockSpec(acc.shape, lambda i: (0, 0)),
    ]
    aliases = {}
    if fitted is not None:
        aliases = {len(args): 0}
        args.append(fitted)
        in_specs.append(pl.BlockSpec(memory_space=pl.ANY))
    return pl.pallas_call(
        lambda *refs: fit_kernel(mu0, *refs),
        grid=(tiles,),
        in_specs=in_specs,
        out_specs=[
            pl.BlockSpec((rows, count, SIG), lambda i: (0, mu0 // count, s // SIG + i)),
            pl.BlockSpec(acc.shape, lambda i: (0, 0)),
        ],
        out_shape=[
            jax.ShapeDtypeStruct(tc.shape, jnp.bfloat16),
            jax.ShapeDtypeStruct(acc.shape, jnp.float32),
        ],
        scratch_shapes=[pltpu.VMEM((rows * (count + 1), SIG), jnp.float32)],
        input_output_aliases=aliases,
        compiler_params=pltpu.CompilerParams(vmem_limit_bytes=VMEM_BYTES),
        cost_estimate=pl.CostEstimate(
            flops=2 * rows * count * tiles * SIG * (3 * rows + cols),
            bytes_accessed=2 * rows * tiles * SIG * (4 * count + cols),
            transcendentals=0,
        ),
    )(*args)


def gather_mu(local):
    count = lax.axis_size("mu")
    me = lax.axis_index("mu")
    parts = [local]
    for k in range(1, count):
        parts.append(lax.ppermute(local, "mu", [((i + k) % count, i) for i in range(count)]))
    twice = jnp.concatenate(parts + parts, axis=0)
    rows = local.shape[0]
    return lax.dynamic_slice_in_dim(twice, ((count - me) % count) * rows, count * rows, 0)


def rotate(value, stride, count, k):
    size = lax.axis_size("pa")
    span = stride * count
    pairs = [
        (i, (i // span) * span + ((i // stride + k) % count) * stride + i % stride)
        for i in range(size)
    ]
    return lax.ppermute(value, "pa", pairs)


def sum_pa(value):
    value = value + rotate(value, 1, 2, 1)
    for stride in (2, 8):
        parts = [rotate(value, stride, 4, k) for k in (1, 2, 3)]
        value = (value + parts[1]) + (parts[0] + parts[2])
    return value


def on_device(three_center, center_mask, density, density_mask, metric_band):
    rows, cols, width = three_center.shape
    size = lax.axis_size("pa")
    forward = [(i, i + 1) for i in range(size - 1)]
    backward = [(b, a) for a, b in forward]

    mask = jnp.repeat(center_mask[:, 0, :], BS, axis=1).astype(jnp.float32)
    s, tiles, mu0, count = RAW
    raw = three_center[:, mu0:mu0 + count, :].reshape(rows // BS, BS, count, width)
    raw = (raw * mask.astype(jnp.bfloat16)[:, None, None, :]).reshape(rows, count, width)
    raw_low = lax.ppermute(raw, "pa", forward)
    raw_high = lax.ppermute(raw, "pa", backward)

    block_mask = jnp.repeat(jnp.repeat(density_mask, BS, axis=0), BS, axis=1)
    dens_local = density * block_mask.astype(jnp.bfloat16)
    dens = gather_mu(dens_local)

    own = list(half_call(three_center, mask, dens, CHUNKS[:1], 0, 48))
    *rest, own_raw = half_call(three_center, mask, dens, CHUNKS[1:] + (RAW,), 0, cols)
    own += rest

    def send(c, *after):
        piece, *_ = lax.optimization_barrier((own[c],) + after)
        return lax.ppermute(piece, "pa", forward), lax.ppermute(piece, "pa", backward)

    arrived = {0: send(0), 1: send(1)}
    (low,) = half_call(raw_low, None, dens, (RAW,), mu0, count)
    (high,) = half_call(raw_high, None, dens, (RAW,), mu0, count)
    acc = jnp.zeros((cols, cols), jnp.float32)
    fitted, acc = fit_call(RAW, low, own_raw, high, metric_band, three_center, mask, acc, None)
    arrived[2] = send(2, acc)
    for c, chunk in enumerate(CHUNKS):
        low, high = arrived[c]
        fitted, acc = fit_call(
            chunk, low, own[c], high, metric_band, three_center, mask, acc, fitted
        )
        if c + 3 < len(CHUNKS):
            arrived[c + 3] = send(c + 3, acc)
    scale = 1.0 / math.sqrt(rows * size * width)
    return (fitted, sum_pa(acc) * scale)


def solution(mesh):
    placed = (P("pa", "mu", None), P("pa", "mu", None), P("mu", None), P("mu", None), P("pa", None))
    return jax.shard_map(
        on_device,
        mesh=mesh,
        in_specs=placed,
        out_specs=(P("pa", "mu", None), P("mu", None)),
        check_vma=False,
    )
```

time: 194 us -> 163 us (0.84)
  starting transfers between devices: 99.3 us -> 58.2 us
  Pallas kernels: 65.5 us -> 76.5 us
  local copies, waits for them, and re-layouts: 11.2 us -> 5.82 us
  waiting for transfers between devices: 13 us -> 15.8 us
    ppermute x12, starting transfers between devices: 80.6 us -> 31.3 us  [the longest x5 19.5 us: send(): lax.ppermute(piece, 'pa', forward)]
    pallas_call x8 -> x10, Pallas kernels: 65.5 us -> 76.5 us  [the longest x6 43.1 us: fit_call(): pl.pallas_call(lambda *refs: fit_kernel(mu0, *refs), grid=(tiles,), in_sp...]
    ppermute x7, starting transfers between devices: 13.2 us -> 21.5 us  [rotate(): return lax.ppermute(value, 'pa', pairs)]
    unnamed x28, local copies, waits for them, and re-layouts: 10.5 us -> 3.12 us
  transfers between devices with their start and end apart: 22 -> 22, of which waited for: 7 -> 7; matrix products, arithmetic and copies ran while one was open for 0% -> 3% of each run, Pallas kernels for 28% -> 44%
where the time goes in v2:
time: 163 us; the launch traced here: 162 us
  Pallas kernels  76.5 us (47%)
  starting transfers between devices  58.2 us (36%)
  waiting for transfers between devices  15.8 us (10%)
  local copies, waits for them, and re-layouts  5.82 us (4%)
  other arithmetic  4.64 us (3%)
    pallas_call x6, Pallas kernels, fit_call(): pl.pallas_call(lambda *refs: fit_kernel(mu0, *refs), grid=(tiles,), in_sp...  43.1 us
    pallas_call x4, Pallas kernels, half_call(): pl.pallas_call(kernel, grid=(rows // PB,), in_specs=in_specs, out_specs=[...  33.4 us
    ppermute x7, starting transfers between devices, rotate(): return lax.ppermute(value, 'pa', pairs)  21.5 us
    ppermute x5, starting transfers between devices, send(): lax.ppermute(piece, 'pa', forward)  19.5 us
    ppermute x3, waiting for transfers between devices, gather_mu(): lax.ppermute(local, 'mu', [((i + k) % count, i) for i in range(count)])  8.54 us
    ppermute x7, waiting for transfers between devices, rotate(): return lax.ppermute(value, 'pa', pairs)  7.26 us
    ppermute x5, starting transfers between devices, send(): lax.ppermute(piece, 'pa', backward)  6.41 us
    ppermute x3, starting transfers between devices, gather_mu(): lax.ppermute(local, 'mu', [((i + k) % count, i) for i in range(count)])  5.38 us
  transfers between devices with their start and end apart: 22, of which 7 were waited for; matrix products, arithmetic and copies ran while one was open for 3% of the time, Pallas kernels for 44%

profile of v2, /device:TPU:0, one launch (start us, length us, event | category | flops | bytes accessed | tf_op | source)
XLA Modules:
  0.0 161.9 jit_solution(11236564832166774741)
XLA Ops:
  0.6 0.7 convert_element_type.25
  1.5 1.9 %slice_multiply_fusion = bf16[128,16,512]{2,1,0:T(8,128)(2,1)S(1)} fusion(bf16[128,64,512]{2,1,0:T(8,128)(2,1)} %refs_4_.11, bf16[128,512]{1,0:T(8,128)(2,1)S(1)} %bitcast.5), kind=kLoop, calls=%fused_computation | loop fusion | flops 1048576 | bytes 4325376 | tf_op jit(solution)/shard_map/mul | solution.py:199
  3.4 1.3 collective-permute-start.8
  5.1 0.7 constant_dynamic-update-slice_fusion.7
  5.8 4.1 %collective-permute-start = (bf16[128,512]{1,0:T(8,128)(2,1)}, bf16[128,512]{1,0:T(8,128)(2,1)S(1)}, u32[]{:S(2)}, u32[]{:S(2)}) collective-permute-start(bf16[128,512]{1,0:T(8,128)(2,1)} %get-tuple-element.43), channel_id=1, source_target_pairs={{1,0},{2,1},{3,2},{0,3},{5,4},{6,5},{7,6},{4,7},{9,8},{10,9},{11,1... | collective-permute-start | bytes 393224 | tf_op jit(solution)/shard_map/ppermute | solution.py:166
  9.9 4.1 %collective-permute-start.7 = (bf16[128,16,512]{2,1,0:T(8,128)(2,1)S(1)}, bf16[128,16,512]{2,1,0:T(8,128)(2,1)}, u32[]{:S(2)}, u32[]{:S(2)}) collective-permute-start(bf16[128,16,512]{2,1,0:T(8,128)(2,1)S(1)} %slice_multiply_fusion), channel_id=1, source_target_pairs={{0,4},{4,8},{8,12},{12,16},{16,20},{20,24},{24,28},{28,32},{32,36}... | collective-permute-start | bytes 6291464 | tf_op jit(solution)/shard_map/ppermute | solution.py:200
  14.2 1.1 collective-permute-start.2
  15.3 6.8 %collective-permute-done.1 = bf16[128,512]{1,0:T(8,128)(2,1)S(1)} collective-permute-done((bf16[128,512]{1,0:T(8,128)(2,1)}, bf16[128,512]{1,0:T(8,128)(2,1)S(1)}, u32[]{:S(2)}, u32[]{:S(2)}) %collective-permute-start.1) | collective-permute-done | bytes 131104 | tf_op jit(solution)/shard_map/ppermute | solution.py:166
  22.2 1.7 %collective-permute-done.2 = bf16[128,512]{1,0:T(8,128)(2,1)S(1)} collective-permute-done((bf16[128,512]{1,0:T(8,128)(2,1)}, bf16[128,512]{1,0:T(8,128)(2,1)S(1)}, u32[]{:S(2)}, u32[]{:S(2)}) %collective-permute-start.2) | collective-permute-done | bytes 131104 | tf_op jit(solution)/shard_map/ppermute | solution.py:166
  23.9 0.9 constant_dynamic-update-slice_fusion.3
  24.9 0.7 constant_dynamic-slice_fusion.refs_2_
  25.5 7.9 %shard_map.69.refs_1_ = bf16[48,128,128]{2,1,0:T(8,128)(2,1)} custom-call(f32[2,512]{1,0:T(2,128)} %copy-done.8, bf16[128,64,512]{2,1,0:T(8,128)(2,1)} %refs_4_.11, bf16[512,128]{1,0:T(8,128)(2,1)} %constant_dynamic-slice_fusion.refs_2_), custom_call_target="tpu_custom_call" | custom-call | flops 805306368 | bytes 7864320 | tf_op jit(solution)/shard_map/pallas_call | solution.py:58
  33.4 1.3 collective-permute-start.6
  34.7 4.2 %collective-permute-start.5 = (bf16[48,128,128]{2,1,0:T(8,128)(2,1)}, bf16[48,128,128]{2,1,0:T(8,128)(2,1)}, u32[]{:S(2)}, u32[]{:S(2)}) collective-permute-start(bf16[48,128,128]{2,1,0:T(8,128)(2,1)} %shard_map.69.refs_1_), channel_id=1, source_target_pairs={{0,4},{4,8},{8,12},{12,16},{16,20},{20,24},{24,28},{28,32},{32,36}... | collective-permute-start | bytes 4718600 | tf_op jit(solution)/shard_map/ppermute | solution.py:213
  38.9 0.8 constant_dynamic-slice_fusion.1.refs_2_.refs_1_
  39.7 11.3 %shard_map.68 = (bf16[48,128,128]{2,1,0:T(8,128)(2,1)}, bf16[48,128,128]{2,1,0:T(8,128)(2,1)}, bf16[32,128,128]{2,1,0:T(8,128)(2,1)}, bf16[16,128,128]{2,1,0:T(8,128)(2,1)}, bf16[16,128,512]{2,1,0:T(8,128)(2,1)}) custom-call(f32[2,512]{1,0:T(2,128)} %copy-done.8, bf16[128,64,512]{2,1,0:T(8,128)(2,1)} %refs_4_.11, ...), custom_call_target="tpu_custom_call" | custom-call | flops 4294967296 | bytes 16777216 | tf_op jit(solution)/shard_map/pallas_call | solution.py:58
  51.0 1.3 collective-permute-start.4
  52.3 4.2 %collective-permute-start.3 = (bf16[48,128,128]{2,1,0:T(8,128)(2,1)}, bf16[48,128,128]{2,1,0:T(8,128)(2,1)}, u32[]{:S(2)}, u32[]{:S(2)}) collective-permute-start(bf16[48,128,128]{2,1,0:T(8,128)(2,1)} %get-tuple-element.23.refs_1_), channel_id=1, source_target_pairs={{0,4},{4,8},{8,12},{12,16},{16,20},{20,24},{24,28},{28,32},{32,36}... | collective-permute-start | bytes 4718600 | tf_op jit(solution)/shard_map/ppermute | solution.py:213
  56.5 7.1 %shard_map.71.refs_2_ = bf16[16,128,512]{2,1,0:T(8,128)(2,1)} custom-call(bf16[128,16,512]{2,1,0:T(8,128)(2,1)} %collective-permute-done.8.refs_0_, bf16[512,512]{1,0:T(8,128)(2,1)} %constant_dynamic-slice_fusion.1.refs_2_.refs_1_), custom_call_target="tpu_custom_call" | custom-call | flops 1073741824 | bytes 4194304 | tf_op jit(solution)/shard_map/pallas_call | solution.py:58
  63.7 7.1 %shard_map.70.refs_0_ = bf16[16,128,512]{2,1,0:T(8,128)(2,1)} custom-call(bf16[128,16,512]{2,1,0:T(8,128)(2,1)} %collective-permute-done.7.refs_0_, bf16[512,512]{1,0:T(8,128)(2,1)} %constant_dynamic-slice_fusion.1.refs_2_.refs_1_), custom_call_target="tpu_custom_call" | custom-call | flops 1073741824 | bytes 4194304 | tf_op jit(solution)/shard_map/pallas_call | solution.py:58
  70.8 0.6 broadcast_in_dim.16.refs_6_
  71.4 11.1 %shard_map.72 = (bf16[128,64,512]{2,1,0:T(8,128)(2,1)}, f32[64,64]{1,0:T(8,128)}) custom-call(bf16[16,128,512]{2,1,0:T(8,128)(2,1)} %shard_map.70.refs_0_, bf16[16,128,512]{2,1,0:T(8,128)(2,1)} %get-tuple-element.24.refs_1_, bf16[16,128,512]{2,1,0:T(8,128)(2,1)} %shard_map.71.refs_2_, bf16[128,384]{1,0:T(8,128)(2,1)} %refs_3_.11, ...), custom_call_target="tpu_custom_call" | custom-call | flops 939524096 | bytes 16777216 | tf_op jit(solution)/shard_map/pallas_call | solution.py:138
  82.5 1.3 collective-permute-start.14
  83.8 3.1 %collective-permute-start.13 = (bf16[48,128,128]{2,1,0:T(8,128)(2,1)S(1)}, bf16[48,128,128]{2,1,0:T(8,128)(2,1)S(1)}, u32[]{:S(2)}, u32[]{:S(2)}) collective-permute-start(bf16[48,128,128]{2,1,0:T(8,128)(2,1)S(1)} %copy-done), channel_id=1, source_target_pairs={{0,4},{4,8},{8,12},{12,16},{16,20},{20,24},{24,28},{28,32},{32,36}... | collective-permute-start | bytes 4718600 | tf_op jit(solution)/shard_map/ppermute | solution.py:213
  86.9 7.2 %shard_map.73 = (bf16[128,64,512]{2,1,0:T(8,128)(2,1)}, f32[64,64]{1,0:T(8,128)}) custom-call(bf16[48,128,128]{2,1,0:T(8,128)(2,1)} %collective-permute-done.5.refs_0_, bf16[48,128,128]{2,1,0:T(8,128)(2,1)} %shard_map.69.refs_1_, bf16[48,128,128]{2,1,0:T(8,128)(2,1)} %collective-permute-done.6.refs_2_, ...), custom_call_target="tpu_custom_call", output_to_operand_aliasing={{0}: (7, {})} | custom-call | flops 704643072 | bytes 8388608 | tf_op jit(solution)/shard_map/pallas_call | solution.py:138
  94.2 1.3 collective-permute-start.12
  95.5 4.6 %collective-permute-start.11 = (bf16[32,128,128]{2,1,0:T(8,128)(2,1)S(1)}, bf16[32,128,128]{2,1,0:T(8,128)(2,1)}, u32[]{:S(2)}, u32[]{:S(2)}) collective-permute-start(bf16[32,128,128]{2,1,0:T(8,128)(2,1)S(1)} %copy-done.4), channel_id=1, source_target_pairs={{0,4},{4,8},{8,12},{12,16},{16,20},{20,24},{24,28},{28,32},{32,36}... | collective-permute-start | bytes 3145736 | tf_op jit(solution)/shard_map/ppermute | solution.py:213
  100.1 7.2 %shard_map.74 = (bf16[128,64,512]{2,1,0:T(8,128)(2,1)}, f32[64,64]{1,0:T(8,128)}) custom-call(bf16[48,128,128]{2,1,0:T(8,128)(2,1)} %collective-permute-done.3.refs_0_, bf16[48,128,128]{2,1,0:T(8,128)(2,1)} %get-tuple-element.23.refs_1_, bf16[48,128,128]{2,1,0:T(8,128)(2,1)} %copy-done.1, ...), custom_call_target="tpu_custom_call", output_to_operand_aliasing={{0}: (7, {})} | custom-call | flops 704643072 | bytes 8388608 | tf_op jit(solution)/shard_map/pallas_call | solution.py:138
  107.3 1.3 collective-permute-start.10
  108.6 3.3 %collective-permute-start.9 = (bf16[16,128,128]{2,1,0:T(8,128)(2,1)S(1)}, bf16[16,128,128]{2,1,0:T(8,128)(2,1)S(1)}, u32[]{:S(2)}, u32[]{:S(2)}) collective-permute-start(bf16[16,128,128]{2,1,0:T(8,128)(2,1)S(1)} %copy-done.5), channel_id=1, source_target_pairs={{0,4},{4,8},{8,12},{12,16},{16,20},{20,24},{24,28},{28,32},{32,36}... | collective-permute-start | bytes 1572872 | tf_op jit(solution)/shard_map/ppermute | solution.py:213
  112.0 1.2 copy-done.3
  113.2 7.2 %shard_map.75 = (bf16[128,64,512]{2,1,0:T(8,128)(2,1)}, f32[64,64]{1,0:T(8,128)}) custom-call(bf16[48,128,128]{2,1,0:T(8,128)(2,1)} %copy-done.3, bf16[48,128,128]{2,1,0:T(8,128)(2,1)} %get-tuple-element.34.refs_1_, bf16[48,128,128]{2,1,0:T(8,128)(2,1)} %copy-done.2, bf16[128,384]{1,0:T(8,128)(2,1)} %refs_3_.11, ...), custom_call_target="tpu_custom_call", output_to_operand_aliasing={{0}: (7, {})} | custom-call | flops 704643072 | bytes 8388608 | tf_op jit(solution)/shard_map/pallas_call | solution.py:138
  120.4 5.9 %shard_map.76 = (bf16[128,64,512]{2,1,0:T(8,128)(2,1)}, f32[64,64]{1,0:T(8,128)}) custom-call(bf16[32,128,128]{2,1,0:T(8,128)(2,1)} %collective-permute-done.11.refs_0_, bf16[32,128,128]{2,1,0:T(8,128)(2,1)} %get-tuple-element.32.refs_1_, bf16[32,128,128]{2,1,0:T(8,128)(2,1)} %collective-permute-done.12.refs_2_, ...), custom_call_target="tpu_custom_call", output_to_operand_aliasing={{0}: (7, {})} | custom-call | flops 469762048 | bytes 6291456 | tf_op jit(solution)/shard_map/pallas_call | solution.py:138
  126.3 0.8 copy-done.6
  127.0 0.2 copy-done.7
  127.2 4.5 %shard_map.77 = (bf16[128,64,512]{2,1,0:T(8,128)(2,1)}, f32[64,64]{1,0:T(8,128)}) custom-call(bf16[16,128,128]{2,1,0:T(8,128)(2,1)} %copy-done.7, bf16[16,128,128]{2,1,0:T(8,128)(2,1)} %get-tuple-element.30.refs_1_, bf16[16,128,128]{2,1,0:T(8,128)(2,1)} %copy-done.6, bf16[128,384]{1,0:T(8,128)(2,1)} %refs_3_.11, ...), custom_call_target="tpu_custom_call", output_to_operand_aliasing={{0}: (7, {})} | custom-call | flops 234881024 | bytes 4194304 | tf_op jit(solution)/shard_map/pallas_call | solution.py:138
  131.8 1.7 %collective-permute-start.15 = (f32[64,64]{1,0:T(8,128)}, f32[64,64]{1,0:T(8,128)S(1)}, u32[]{:S(2)}, u32[]{:S(2)}) collective-permute-start(f32[64,64]{1,0:T(8,128)} %get-tuple-element.41), channel_id=1, source_target_pairs={{0,4},{4,0},{8,12},{12,8},{16,20},{20,16},{24,28},{28,24},{32,36},... | collective-permute-start | bytes 49160 | tf_op jit(solution)/shard_map/ppermute | solution.py:179
  133.5 1.1 collective-permute-done.15
  134.5 0.8 add.30
  135.3 13.0 %collective-permute-start.18 = (f32[64,64]{1,0:T(8,128)S(1)}, f32[64,64]{1,0:T(8,128)S(1)}, u32[]{:S(2)}, u32[]{:S(2)}) collective-permute-start(f32[64,64]{1,0:T(8,128)S(1)} %add.30), channel_id=1, source_target_pairs={{0,24},{4,28},{8,0},{12,4},{16,8},{20,12},{24,16},{28,20},{32,56},... | collective-permute-start | bytes 49160 | tf_op jit(solution)/shard_map/ppermute | solution.py:179
  148.3 1.5 collective-permute-start.16
  149.9 3.9 %collective-permute-done.17 = f32[64,64]{1,0:T(8,128)S(1)} collective-permute-done((f32[64,64]{1,0:T(8,128)S(1)}, f32[64,64]{1,0:T(8,128)S(1)}, u32[]{:S(2)}, u32[]{:S(2)}) %collective-permute-start.17) | collective-permute-done | bytes 16416 | tf_op jit(solution)/shard_map/ppermute | solution.py:179
  153.7 1.3 collective-permute-start.21
  155.1 0.8 collective-permute-start.20
  155.8 3.2 %collective-permute-start.19 = (f32[64,64]{1,0:T(8,128)S(1)}, f32[64,64]{1,0:T(8,128)S(1)}, u32[]{:S(2)}, u32[]{:S(2)}) collective-permute-start(f32[64,64]{1,0:T(8,128)S(1)} %add_add_fusion), channel_id=1, source_target_pairs={{0,64},{4,68},{8,72},{12,76},{16,80},{20,84},{24,88},{28,92},{32,9... | collective-permute-start | bytes 49160 | tf_op jit(solution)/shard_map/ppermute | solution.py:179
  159.0 1.2 collective-permute-done.20
  160.2 1.1 collective-permute-done.19
  161.3 0.6 add_multiply_fusion
  (54 shorter events, 0.9 us)
Async XLA Ops:
  1.5 1.9 %copy-start.8 = (f32[2,512]{1,0:T(2,128)}, f32[2,512]{1,0:T(2,128)S(1)}, u32[]{:S(2)}) copy-start(f32[2,512]{1,0:T(2,128)S(1)} %convert_element_type.27.refs_0_.refs_5_) | copy-start | bytes 12292
  1.5 3.2 %copy-start.10 = (s32[2,8]{1,0:T(2,128)S(1)}, s32[2,8]{1,0:T(2,128)}, u32[]{:S(2)}) copy-start(s32[2,8]{1,0:T(2,128)} %param.8) | copy-start | bytes 196
  1.5 3.6 %copy-start.9 = (bf16[128,512]{1,0:T(8,128)(2,1)S(1)}, bf16[128,512]{1,0:T(8,128)(2,1)}, u32[]{:S(2)}) copy-start(bf16[128,512]{1,0:T(8,128)(2,1)} %param.7) | copy-start | bytes 393220
  3.4 48.9 %collective-permute-start.8 = (bf16[128,16,512]{2,1,0:T(8,128)(2,1)S(1)}, bf16[128,16,512]{2,1,0:T(8,128)(2,1)}, u32[]{:S(2)}, u32[]{:S(2)}) collective-permute-start(bf16[128,16,512]{2,1,0:T(8,128)(2,1)S(1)} %slice_multiply_fusion), channel_id=1, source_target_pairs={{4,0},{8,4},{12,8},{16,12},{20,16},{24,20},{28,24},{32,28},{36,32}... | collective-permute-start | bytes 6291464 | tf_op jit(solution)/shard_map/ppermute | solution.py:201
  5.8 9.5 %collective-permute-start = (bf16[128,512]{1,0:T(8,128)(2,1)}, bf16[128,512]{1,0:T(8,128)(2,1)S(1)}, u32[]{:S(2)}, u32[]{:S(2)}) collective-permute-start(bf16[128,512]{1,0:T(8,128)(2,1)} %get-tuple-element.43), channel_id=1, source_target_pairs={{1,0},{2,1},{3,2},{0,3},{5,4},{6,5},{7,6},{4,7},{9,8},{10,9},{11,1... | collective-permute-start | bytes 393224 | tf_op jit(solution)/shard_map/ppermute | solution.py:166
  9.9 53.7 %collective-permute-start.7 = (bf16[128,16,512]{2,1,0:T(8,128)(2,1)S(1)}, bf16[128,16,512]{2,1,0:T(8,128)(2,1)}, u32[]{:S(2)}, u32[]{:S(2)}) collective-permute-start(bf16[128,16,512]{2,1,0:T(8,128)(2,1)S(1)} %slice_multiply_fusion), channel_id=1, source_target_pairs={{0,4},{4,8},{8,12},{12,16},{16,20},{20,24},{24,28},{28,32},{32,36}... | collective-permute-start | bytes 6291464 | tf_op jit(solution)/shard_map/ppermute | solution.py:200
  14.0 8.1 %collective-permute-start.1 = (bf16[128,512]{1,0:T(8,128)(2,1)}, bf16[128,512]{1,0:T(8,128)(2,1)S(1)}, u32[]{:S(2)}, u32[]{:S(2)}) collective-permute-start(bf16[128,512]{1,0:T(8,128)(2,1)} %get-tuple-element.43), channel_id=1, source_target_pairs={{2,0},{3,1},{0,2},{1,3},{6,4},{7,5},{4,6},{5,7},{10,8},{11,9},{8,1... | collective-permute-start | bytes 393224 | tf_op jit(solution)/shard_map/ppermute | solution.py:166
  14.2 9.7 %collective-permute-start.2 = (bf16[128,512]{1,0:T(8,128)(2,1)}, bf16[128,512]{1,0:T(8,128)(2,1)S(1)}, u32[]{:S(2)}, u32[]{:S(2)}) collective-permute-start(bf16[128,512]{1,0:T(8,128)(2,1)} %get-tuple-element.43), channel_id=1, source_target_pairs={{3,0},{0,1},{1,2},{2,3},{7,4},{4,5},{5,6},{6,7},{11,8},{8,9},{9,10... | collective-permute-start | bytes 393224 | tf_op jit(solution)/shard_map/ppermute | solution.py:166
  33.4 50.3 %collective-permute-start.6 = (bf16[48,128,128]{2,1,0:T(8,128)(2,1)}, bf16[48,128,128]{2,1,0:T(8,128)(2,1)}, u32[]{:S(2)}, u32[]{:S(2)}) collective-permute-start(bf16[48,128,128]{2,1,0:T(8,128)(2,1)} %shard_map.69.refs_1_), channel_id=1, source_target_pairs={{4,0},{8,4},{12,8},{16,12},{20,16},{24,20},{28,24},{32,28},{36,32}... | collective-permute-start | bytes 4718600 | tf_op jit(solution)/shard_map/ppermute | solution.py:213
  34.7 52.2 %collective-permute-start.5 = (bf16[48,128,128]{2,1,0:T(8,128)(2,1)}, bf16[48,128,128]{2,1,0:T(8,128)(2,1)}, u32[]{:S(2)}, u32[]{:S(2)}) collective-permute-start(bf16[48,128,128]{2,1,0:T(8,128)(2,1)} %shard_map.69.refs_1_), channel_id=1, source_target_pairs={{0,4},{4,8},{8,12},{12,16},{16,20},{20,24},{24,28},{28,32},{32,36}... | collective-permute-start | bytes 4718600 | tf_op jit(solution)/shard_map/ppermute | solution.py:213
  51.0 44.5 %collective-permute-start.4 = (bf16[48,128,128]{2,1,0:T(8,128)(2,1)}, bf16[48,128,128]{2,1,0:T(8,128)(2,1)S(1)}, u32[]{:S(2)}, u32[]{:S(2)}) collective-permute-start(bf16[48,128,128]{2,1,0:T(8,128)(2,1)} %get-tuple-element.23.refs_1_), channel_id=1, source_target_pairs={{4,0},{8,4},{12,8},{16,12},{20,16},{24,20},{28,24},{32,28},{36,32}... | collective-permute-start | bytes 4718600 | tf_op jit(solution)/shard_map/ppermute | solution.py:213
  52.3 47.8 %collective-permute-start.3 = (bf16[48,128,128]{2,1,0:T(8,128)(2,1)}, bf16[48,128,128]{2,1,0:T(8,128)(2,1)}, u32[]{:S(2)}, u32[]{:S(2)}) collective-permute-start(bf16[48,128,128]{2,1,0:T(8,128)(2,1)} %get-tuple-element.23.refs_1_), channel_id=1, source_target_pairs={{0,4},{4,8},{8,12},{12,16},{16,20},{20,24},{24,28},{28,32},{32,36}... | collective-permute-start | bytes 4718600 | tf_op jit(solution)/shard_map/ppermute | solution.py:213
  71.4 11.1 %copy-start = (bf16[48,128,128]{2,1,0:T(8,128)(2,1)S(1)}, bf16[48,128,128]{2,1,0:T(8,128)(2,1)}, u32[]{:S(2)}) copy-start(bf16[48,128,128]{2,1,0:T(8,128)(2,1)} %get-tuple-element.34.refs_1_) | copy-start | bytes 4718596
  82.5 26.2 %collective-permute-start.14 = (bf16[48,128,128]{2,1,0:T(8,128)(2,1)S(1)}, bf16[48,128,128]{2,1,0:T(8,128)(2,1)S(1)}, u32[]{:S(2)}, u32[]{:S(2)}) collective-permute-start(bf16[48,128,128]{2,1,0:T(8,128)(2,1)S(1)} %copy-done), channel_id=1, source_target_pairs={{4,0},{8,4},{12,8},{16,12},{20,16},{24,20},{28,24},{32,28},{36,32}... | collective-permute-start | bytes 4718600 | tf_op jit(solution)/shard_map/ppermute | solution.py:213
  83.8 28.2 %collective-permute-start.13 = (bf16[48,128,128]{2,1,0:T(8,128)(2,1)S(1)}, bf16[48,128,128]{2,1,0:T(8,128)(2,1)S(1)}, u32[]{:S(2)}, u32[]{:S(2)}) collective-permute-start(bf16[48,128,128]{2,1,0:T(8,128)(2,1)S(1)} %copy-done), channel_id=1, source_target_pairs={{0,4},{4,8},{8,12},{12,16},{16,20},{20,24},{24,28},{28,32},{32,36}... | collective-permute-start | bytes 4718600 | tf_op jit(solution)/shard_map/ppermute | solution.py:213
  86.9 7.3 %copy-start.4 = (bf16[32,128,128]{2,1,0:T(8,128)(2,1)S(1)}, bf16[32,128,128]{2,1,0:T(8,128)(2,1)}, u32[]{:S(2)}) copy-start(bf16[32,128,128]{2,1,0:T(8,128)(2,1)} %get-tuple-element.32.refs_1_) | copy-start | bytes 3145732
  94.2 26.2 %collective-permute-start.12 = (bf16[32,128,128]{2,1,0:T(8,128)(2,1)S(1)}, bf16[32,128,128]{2,1,0:T(8,128)(2,1)}, u32[]{:S(2)}, u32[]{:S(2)}) collective-permute-start(bf16[32,128,128]{2,1,0:T(8,128)(2,1)S(1)} %copy-done.4), channel_id=1, source_target_pairs={{4,0},{8,4},{12,8},{16,12},{20,16},{24,20},{28,24},{32,28},{36,32}... | collective-permute-start | bytes 3145736 | tf_op jit(solution)/shard_map/ppermute | solution.py:213
  95.5 4.6 %copy-start.1 = (bf16[48,128,128]{2,1,0:T(8,128)(2,1)}, bf16[48,128,128]{2,1,0:T(8,128)(2,1)S(1)}, u32[]{:S(2)}) copy-start(bf16[48,128,128]{2,1,0:T(8,128)(2,1)S(1)} %collective-permute-done.4.refs_2_) | copy-start | bytes 4718596
  95.5 24.9 %collective-permute-start.11 = (bf16[32,128,128]{2,1,0:T(8,128)(2,1)S(1)}, bf16[32,128,128]{2,1,0:T(8,128)(2,1)}, u32[]{:S(2)}, u32[]{:S(2)}) collective-permute-start(bf16[32,128,128]{2,1,0:T(8,128)(2,1)S(1)} %copy-done.4), channel_id=1, source_target_pairs={{0,4},{4,8},{8,12},{12,16},{16,20},{20,24},{24,28},{28,32},{32,36}... | collective-permute-start | bytes 3145736 | tf_op jit(solution)/shard_map/ppermute | solution.py:213
  100.1 7.2 %copy-start.5 = (bf16[16,128,128]{2,1,0:T(8,128)(2,1)S(1)}, bf16[16,128,128]{2,1,0:T(8,128)(2,1)}, u32[]{:S(2)}) copy-start(bf16[16,128,128]{2,1,0:T(8,128)(2,1)} %get-tuple-element.30.refs_1_) | copy-start | bytes 1572868
  107.3 18.9 %collective-permute-start.10 = (bf16[16,128,128]{2,1,0:T(8,128)(2,1)S(1)}, bf16[16,128,128]{2,1,0:T(8,128)(2,1)S(1)}, u32[]{:S(2)}, u32[]{:S(2)}) collective-permute-start(bf16[16,128,128]{2,1,0:T(8,128)(2,1)S(1)} %copy-done.5), channel_id=1, source_target_pairs={{4,0},{8,4},{12,8},{16,12},{20,16},{24,20},{28,24},{32,28},{36,32}... | collective-permute-start | bytes 1572872 | tf_op jit(solution)/shard_map/ppermute | solution.py:213
  108.6 3.4 %copy-start.2 = (bf16[48,128,128]{2,1,0:T(8,128)(2,1)}, bf16[48,128,128]{2,1,0:T(8,128)(2,1)S(1)}, u32[]{:S(2)}) copy-start(bf16[48,128,128]{2,1,0:T(8,128)(2,1)S(1)} %collective-permute-done.14.refs_2_) | copy-start | bytes 4718596
  108.6 17.6 %collective-permute-start.9 = (bf16[16,128,128]{2,1,0:T(8,128)(2,1)S(1)}, bf16[16,128,128]{2,1,0:T(8,128)(2,1)S(1)}, u32[]{:S(2)}, u32[]{:S(2)}) collective-permute-start(bf16[16,128,128]{2,1,0:T(8,128)(2,1)S(1)} %copy-done.5), channel_id=1, source_target_pairs={{0,4},{4,8},{8,12},{12,16},{16,20},{20,24},{24,28},{28,32},{32,36}... | collective-permute-start | bytes 1572872 | tf_op jit(solution)/shard_map/ppermute | solution.py:213
  112.0 1.2 copy-start.3
  126.2 0.8 copy-start.6
  126.3 1.0 copy-start.7
  131.8 2.8 %collective-permute-start.15 = (f32[64,64]{1,0:T(8,128)}, f32[64,64]{1,0:T(8,128)S(1)}, u32[]{:S(2)}, u32[]{:S(2)}) collective-permute-start(f32[64,64]{1,0:T(8,128)} %get-tuple-element.41), channel_id=1, source_target_pairs={{0,4},{4,0},{8,12},{12,8},{16,20},{20,16},{24,28},{28,24},{32,36},... | collective-permute-start | bytes 49160 | tf_op jit(solution)/shard_map/ppermute | solution.py:179
  135.3 14.6 %collective-permute-start.18 = (f32[64,64]{1,0:T(8,128)S(1)}, f32[64,64]{1,0:T(8,128)S(1)}, u32[]{:S(2)}, u32[]{:S(2)}) collective-permute-start(f32[64,64]{1,0:T(8,128)S(1)} %add.30), channel_id=1, source_target_pairs={{0,24},{4,28},{8,0},{12,4},{16,8},{20,12},{24,16},{28,20},{32,56},... | collective-permute-start | bytes 49160 | tf_op jit(solution)/shard_map/ppermute | solution.py:179
  148.3 5.5 %collective-permute-start.17 = (f32[64,64]{1,0:T(8,128)S(1)}, f32[64,64]{1,0:T(8,128)S(1)}, u32[]{:S(2)}, u32[]{:S(2)}) collective-permute-start(f32[64,64]{1,0:T(8,128)S(1)} %add.30), channel_id=1, source_target_pairs={{0,8},{4,12},{8,16},{12,20},{16,24},{20,28},{24,0},{28,4},{32,40},... | collective-permute-start | bytes 49160 | tf_op jit(solution)/shard_map/ppermute | solution.py:179
  148.3 5.5 %collective-permute-start.16 = (f32[64,64]{1,0:T(8,128)S(1)}, f32[64,64]{1,0:T(8,128)S(1)}, u32[]{:S(2)}, u32[]{:S(2)}) collective-permute-start(f32[64,64]{1,0:T(8,128)S(1)} %add.30), channel_id=1, source_target_pairs={{0,16},{4,20},{8,24},{12,28},{16,0},{20,4},{24,8},{28,12},{32,48},... | collective-permute-start | bytes 49160 | tf_op jit(solution)/shard_map/ppermute | solution.py:179
  153.7 5.3 %collective-permute-start.21 = (f32[64,64]{1,0:T(8,128)S(1)}, f32[64,64]{1,0:T(8,128)S(1)}, u32[]{:S(2)}, u32[]{:S(2)}) collective-permute-start(f32[64,64]{1,0:T(8,128)S(1)} %add_add_fusion), channel_id=1, source_target_pairs={{0,96},{4,100},{8,104},{12,108},{16,112},{20,116},{24,120},{28,124... | collective-permute-start | bytes 49160 | tf_op jit(solution)/shard_map/ppermute | solution.py:179
  155.1 5.1 %collective-permute-start.20 = (f32[64,64]{1,0:T(8,128)S(1)}, f32[64,64]{1,0:T(8,128)S(1)}, u32[]{:S(2)}, u32[]{:S(2)}) collective-permute-start(f32[64,64]{1,0:T(8,128)S(1)} %add_add_fusion), channel_id=1, source_target_pairs={{0,32},{4,36},{8,40},{12,44},{16,48},{20,52},{24,56},{28,60},{32,6... | collective-permute-start | bytes 49160 | tf_op jit(solution)/shard_map/ppermute | solution.py:179
  155.8 5.4 %collective-permute-start.19 = (f32[64,64]{1,0:T(8,128)S(1)}, f32[64,64]{1,0:T(8,128)S(1)}, u32[]{:S(2)}, u32[]{:S(2)}) collective-permute-start(f32[64,64]{1,0:T(8,128)S(1)} %add_add_fusion), channel_id=1, source_target_pairs={{0,64},{4,68},{8,72},{12,76},{16,80},{20,84},{24,88},{28,92},{32,9... | collective-permute-start | bytes 49160 | tf_op jit(solution)/shard_map/ppermute | solution.py:179

commit v3 on v0

v3 whole, which is shorter than its diff:
```python
import math

import jax
import jax.numpy as jnp
from jax import lax
from jax.experimental import pallas as pl
from jax.experimental.pallas import tpu as pltpu
from jax.sharding import PartitionSpec as P

BS = 64
SIG = 128
PB = 16
QB = 16
VMEM_BYTES = 56 * 2**20

RAW = (0, 4, 32, 32)
CHUNKS = ((0, 1, 0, 32), (128, 2, 0, 32), (384, 1, 0, 16), (384, 1, 16, 16))
WITH_RAW = (True, True, True, False)
ANY = pl.BlockSpec(memory_space=pl.ANY)
WHOLE = pl.BlockSpec(memory_space=pltpu.VMEM)
SCALE = 4.0
PARAMS = pltpu.CompilerParams(vmem_limit_bytes=VMEM_BYTES)


def cost(us):
    return pl.CostEstimate(
        flops=int(us * SCALE * 1e9), bytes_accessed=int(us * SCALE * 3.0e6), transcendentals=0
    )


def half_kernel(chunks, mu0, cols, mask_ref, dens_ref, tc_hbm, *refs):
    n = len(chunks)
    outs, staged = refs[:n], refs[n:2 * n]
    tc_buf, scratch, in_sem, out_sem = refs[2 * n:]
    blocks = tc_buf.shape[0] // PB
    s0 = min(s for s, _, _, _ in chunks)
    tiles_all = scratch.shape[0]
    pitch = cols + 1

    def fetch(b):
        rows = pl.ds(b * PB, PB)
        return pltpu.make_async_copy(
            tc_hbm.at[rows, pl.ds(0, cols)], tc_buf.at[rows], in_sem.at[b]
        )

    def put(k, b):
        return pltpu.make_async_copy(staged[k].at[:, b], outs[k].at[:, b], out_sem.at[k])

    for b in range(blocks):
        fetch(b).start()

    def step(b, carry):
        fetch(b).wait()
        x = tc_buf[pl.ds(b * PB, PB)].reshape(PB * cols, tc_buf.shape[2])
        if mask_ref is not None:
            x = x * mask_ref[(b * PB) // BS].astype(jnp.bfloat16)
        flat = jnp.dot(
            x, dens_ref[:, s0:s0 + tiles_all * SIG], preferred_element_type=jnp.float32
        )
        for t in range(tiles_all):
            for p in range(PB):
                scratch[t, p * pitch:p * pitch + cols] = flat[
                    p * cols:(p + 1) * cols, t * SIG:(t + 1) * SIG
                ]
        for k, (s, tiles, first, count) in enumerate(chunks):
            for t in range(tiles):
                for m in range(count):
                    staged[k][t, b, m] = scratch[
                        (s - s0) // SIG + t, pl.ds(first - mu0 + m, PB, stride=pitch), :
                    ].astype(jnp.bfloat16)
            put(k, b).start()
        return carry

    lax.fori_loop(0, blocks, step, 0)
    for k in range(n):
        pltpu.make_async_copy(staged[k], outs[k], out_sem.at[k]).wait()


def half_call(tc, mask, dens, chunks, mu0, cols):
    rows, _, width = tc.shape
    s0 = min(s for s, _, _, _ in chunks)
    s1 = max(s + t * SIG for s, t, _, _ in chunks)
    shapes = [(t, rows // PB, n, PB, SIG) for _, t, _, n in chunks]

    def kernel(*refs):
        half_kernel(chunks, mu0, cols, *(refs if mask is not None else (None,) + refs))

    return pl.pallas_call(
        kernel,
        in_specs=([WHOLE] if mask is not None else []) + [WHOLE, ANY],
        out_specs=[ANY] * len(chunks),
        out_shape=[jax.ShapeDtypeStruct(shape, jnp.bfloat16) for shape in shapes],
        scratch_shapes=[pltpu.VMEM(shape, jnp.bfloat16) for shape in shapes] + [
            pltpu.VMEM((rows, cols, width), jnp.bfloat16),
            pltpu.VMEM(((s1 - s0) // SIG, PB * (cols + 1) + 8, SIG), jnp.float32),
            pltpu.SemaphoreType.DMA((rows // PB,)),
            pltpu.SemaphoreType.DMA((len(chunks),)),
        ],
        compiler_params=PARAMS,
        cost_estimate=cost(6 if len(chunks) < 2 else 10),
    )(*([mask] if mask is not None else []), dens, tc)


def fit_tile(bufs, metric_ref, scratch, pitch):
    metric = metric_ref[...]
    rows = metric.shape[0]
    count = bufs[0].shape[1]

    def fit(pair, carry):
        columns = []
        for m in (2 * pair, 2 * pair + 1):
            columns.append(jnp.concatenate([r[:, m].reshape(rows, SIG) for r in bufs], axis=0))
        y = jnp.dot(metric, jnp.concatenate(columns, axis=1), preferred_element_type=jnp.float32)
        scratch[pl.ds(2 * pair, rows, stride=pitch), :] = y[:, :SIG]
        scratch[pl.ds(2 * pair + 1, rows, stride=pitch), :] = y[:, SIG:]
        return carry

    lax.fori_loop(0, count // 2, fit, 0, unroll=8)


def fit_raw_kernel(metric_ref, far, own, near, fitted, raw_rows, *refs):
    bufs, (staged, scratch, in_sem, out_sem) = refs[:3], refs[3:]
    s, tiles, mu0, count = RAW
    rows = metric_ref.shape[0]
    pitch = count + 1

    def fetch(t):
        return [
            pltpu.make_async_copy(src.at[t], buf.at[t], in_sem.at[k, t])
            for k, (src, buf) in enumerate(zip((far, own, near), bufs))
        ]

    def put(t):
        lanes = pl.ds(pl.multiple_of(s + t * SIG, SIG), SIG)
        return [
            pltpu.make_async_copy(
                staged.at[t], fitted.at[:, pl.ds(mu0, count), lanes], out_sem.at[0, t]
            ),
            pltpu.make_async_copy(staged.at[t], raw_rows.at[t], out_sem.at[1, t]),
        ]

    for t in range(tiles):
        for copy in fetch(t):
            copy.start()

    def tile(t, carry):
        for copy in fetch(t):
            copy.wait()
        fit_tile([buf.at[t] for buf in bufs], metric_ref, scratch, pitch)

        def store(step, inner):
            for q in range(QB):
                row = step * QB + q
                staged[t, row] = scratch[pl.ds(row * pitch, count), :].astype(jnp.bfloat16)
            return inner

        lax.fori_loop(0, rows // QB, store, 0)
        for copy in put(t):
            copy.start()
        return carry

    lax.fori_loop(0, tiles, tile, 0)
    for t in range(tiles):
        for copy in put(t):
            copy.wait()


def fit_raw_call(far, own, near, metric, shape):
    _, tiles, _, count = RAW
    rows = shape[0]
    buf = pltpu.VMEM((tiles, rows // PB, count, PB, SIG), jnp.bfloat16)
    return pl.pallas_call(
        fit_raw_kernel,
        in_specs=[WHOLE, ANY, ANY, ANY],
        out_specs=[ANY, ANY],
        out_shape=[
            jax.ShapeDtypeStruct(shape, jnp.bfloat16),
            jax.ShapeDtypeStruct((tiles, rows, count, SIG), jnp.bfloat16),
        ],
        scratch_shapes=[
            buf,
            buf,
            buf,
            pltpu.VMEM((tiles, rows, count, SIG), jnp.bfloat16),
            pltpu.VMEM((rows * (count + 1), SIG), jnp.float32),
            pltpu.SemaphoreType.DMA((3, tiles)),
            pltpu.SemaphoreType.DMA((2, tiles)),
        ],
        compiler_params=PARAMS,
        cost_estimate=cost(6),
    )(metric, far, own, near)


def fit_kernel(chunk, with_raw, metric_ref, mask_ref, acc_ref, far, own, near, tc, *refs):
    s, tiles, mu0, count = chunk
    raw, refs = (refs[0], refs[1:]) if with_raw else (None, refs)
    _, fitted, exch_ref, far_buf, own_buf, near_buf, tc_buf = refs[:7]
    raw_buf, refs = (refs[7], refs[8:]) if with_raw else (None, refs[7:])
    staged, scratch, in_sem, out_sem = refs
    rows = metric_ref.shape[0]
    pitch = count + 1
    lines = count + (RAW[3] if with_raw else 0)
    fit_bufs = (far_buf, own_buf, near_buf)

    def fetch(t):
        lanes = pl.ds(s + t * SIG, SIG)
        copies = [
            pltpu.make_async_copy(src.at[t], buf.at[t], in_sem.at[k, t])
            for k, (src, buf) in enumerate(zip((far, own, near), fit_bufs))
        ]
        copies.append(pltpu.make_async_copy(tc.at[:, :, lanes], tc_buf.at[t], in_sem.at[3, t]))
        if with_raw:
            copies.append(
                pltpu.make_async_copy(raw.at[s // SIG + t], raw_buf.at[t], in_sem.at[4, t])
            )
        return copies

    def put(t):
        lanes = pl.ds(s + t * SIG, SIG)
        return pltpu.make_async_copy(
            staged.at[t], fitted.at[:, pl.ds(mu0, count), lanes], out_sem.at[t]
        )

    for t in range(tiles):
        for copy in fetch(t):
            copy.start()
    exch_ref[...] = acc_ref[...]
    for t in range(tiles):
        copies = fetch(t)
        for copy in copies[:3]:
            copy.wait()
        fit_tile([buf.at[t] for buf in fit_bufs], metric_ref, scratch, pitch)
        for copy in copies[3:]:
            copy.wait()

        def contract(block, total, t=t):
            first = pl.multiple_of(block * QB, QB)
            mask = mask_ref[(block * QB) // BS, :, s + t * SIG:s + (t + 1) * SIG]
            mask = mask.astype(jnp.bfloat16)
            left = []
            for q in range(QB):
                f = scratch[pl.ds((first + q) * pitch, count), :].astype(jnp.bfloat16)
                staged[t, first + q] = f
                if with_raw:
                    f = jnp.concatenate([f, raw_buf[t, first + q]], axis=0)
                left.append(f * mask)
            right = [tc_buf[t, first + q] for q in range(QB)]
            return total + lax.dot_general(
                jnp.concatenate(left, axis=1),
                jnp.concatenate(right, axis=1),
                (((1,), (1,)), ((), ())),
                preferred_element_type=jnp.float32,
            )

        total = lax.fori_loop(
            0, rows // QB, contract, jnp.zeros((lines, acc_ref.shape[1]), jnp.float32), unroll=2
        )
        put(t).start()
        exch_ref[mu0:mu0 + count, :] += total[:count]
        if with_raw:
            exch_ref[RAW[2]:RAW[2] + RAW[3], :] += total[count:]
    for t in range(tiles):
        put(t).wait()


def fit_call(chunk, far, own, near, metric, tc, mask, acc, raw_rows, fitted):
    s, tiles, mu0, count = chunk
    rows, cols, width = tc.shape
    with_raw = raw_rows is not None
    args = [metric, mask, acc, far, own, near, tc] + ([raw_rows] if with_raw else []) + [fitted]
    buf = pltpu.VMEM((tiles, rows // PB, count, PB, SIG), jnp.bfloat16)
    return pl.pallas_call(
        lambda *refs: fit_kernel(chunk, with_raw, *refs),
        in_specs=[WHOLE] * 3 + [ANY] * (len(args) - 3),
        out_specs=[ANY, WHOLE],
        out_shape=[
            jax.ShapeDtypeStruct(tc.shape, jnp.bfloat16),
            jax.ShapeDtypeStruct(acc.shape, jnp.float32),
        ],
        scratch_shapes=[buf, buf, buf, pltpu.VMEM((tiles, rows, cols, SIG), jnp.bfloat16)]
        + ([pltpu.VMEM((tiles, rows, RAW[3], SIG), jnp.bfloat16)] if with_raw else [])
        + [
            pltpu.VMEM((tiles, rows, count, SIG), jnp.bfloat16),
            pltpu.VMEM((rows * (count + 1), SIG), jnp.float32),
            pltpu.SemaphoreType.DMA((5, tiles)),
            pltpu.SemaphoreType.DMA((tiles,)),
        ],
        input_output_aliases={len(args) - 1: 0},
        compiler_params=PARAMS,
        cost_estimate=cost(3 + tiles * count / 16),
    )(*args)


def gather_mu(local):
    count = lax.axis_size("mu")
    me = lax.axis_index("mu")
    parts = [local]
    for k in range(1, count):
        parts.append(lax.ppermute(local, "mu", [((i + k) % count, i) for i in range(count)]))
    twice = jnp.concatenate(parts + parts, axis=0)
    rows = local.shape[0]
    return lax.dynamic_slice_in_dim(twice, ((count - me) % count) * rows, count * rows, 0)


def rotate(value, stride, count, k):
    size = lax.axis_size("pa")
    span = stride * count
    pairs = [
        (i, (i // span) * span + ((i // stride + k) % count) * stride + i % stride)
        for i in range(size)
    ]
    return lax.ppermute(value, "pa", pairs)


def sum_pa(value):
    value = value + rotate(value, 1, 2, 1)
    for stride in (2, 8):
        parts = [rotate(value, stride, 4, k) for k in (1, 2, 3)]
        value = (value + parts[1]) + (parts[0] + parts[2])
    return value


def after(value, *earlier):
    return lax.optimization_barrier((value,) + earlier)[0]


def on_device(three_center, center_mask, density, density_mask, metric_band):
    rows, cols, width = three_center.shape
    size = lax.axis_size("pa")
    near_pairs = [(i, i ^ 1) for i in range(size)]
    far_pairs = [(i, i + 1 if i % 2 else i - 1) for i in range(1, size - 1)]

    def to_near(value, *earlier):
        return lax.ppermute(after(value, *earlier), "pa", near_pairs)

    def to_far(value, *earlier):
        return lax.ppermute(after(value, *earlier), "pa", far_pairs)

    mask = jnp.repeat(center_mask, BS, axis=2).astype(jnp.float32)
    _, _, mu0, count = RAW
    raw = three_center[:, mu0:mu0 + count, :].reshape(rows // BS, BS, count, width)
    raw = (raw * mask.astype(jnp.bfloat16)[:, None]).reshape(rows, count, width)
    raw_far = to_far(raw)

    block_mask = jnp.repeat(jnp.repeat(density_mask, BS, axis=0), BS, axis=1)
    dens = gather_mu(after(density * block_mask.astype(jnp.bfloat16), raw))
    low, middle, high = jnp.split(metric_band, 3, axis=1)
    metric = jnp.where(
        lax.axis_index("pa") % 2 == 0,
        metric_band,
        jnp.concatenate([high, middle, low], axis=1),
    )

    *own, own_raw = half_call(three_center, mask, dens, CHUNKS + (RAW,), 0, cols)
    far = [to_far(own[0]), to_far(own[1])]
    near_raw = to_near(own_raw)
    (half_far,) = half_call(raw_far, None, after(dens, own_raw), (RAW,), mu0, count)
    near = [to_near(own[0], half_far)]
    fitted, raw_rows = fit_raw_call(half_far, own_raw, near_raw, metric, three_center.shape)
    far.append(to_far(own[2], raw_rows))
    near.append(to_near(own[1], raw_rows))
    acc = jnp.zeros((cols, cols), jnp.float32)
    for c, chunk in enumerate(CHUNKS):
        fitted, acc = fit_call(
            chunk, far[c], own[c], near[c], metric, three_center, mask, acc,
            raw_rows if WITH_RAW[c] else None, fitted,
        )
        if c + 3 < len(CHUNKS):
            far.append(to_far(own[c + 3], acc))
        if c + 2 < len(CHUNKS):
            near.append(to_near(own[c + 2], acc))
    scale = 1.0 / math.sqrt(rows * size * width)
    return (fitted, sum_pa(acc) * scale)


def solution(mesh):
    placed = (P("pa", "mu", None), P("pa", "mu", None), P("mu", None), P("mu", None), P("pa", None))
    return jax.shard_map(
        on_device,
        mesh=mesh,
        in_specs=placed,
        out_specs=(P("pa", "mu", None), P("mu", None)),
        check_vma=False,
    )
```

time: 340 us -> 140 us (0.41)
  blocking collectives: 214 us -> 0 us
  local copies, waits for them, and re-layouts: 80.8 us -> 5.87 us
  starting transfers between devices: 5.78 us -> 61.7 us
  Pallas kernels: 0 us -> 52.5 us
  matrix products: 30.2 us -> 0 us
  waiting for transfers between devices: 0.01 us -> 9.79 us
    psum x1 -> x0, blocking collectives: 199 us -> none  [on_device(): total = lax.psum(partial_block, 'pa')]
    ppermute x2 -> x20, starting transfers between devices: 5.78 us -> 61.7 us  [the longest x5 35.7 us: to_near(): return lax.ppermute(after(value, *earlier), 'pa', near_pairs)]
    pallas_call x0 -> x7, Pallas kernels: none -> 52.5 us  [the longest x4 25.7 us: fit_call(): pl.pallas_call(lambda *refs: fit_kernel(chunk, with_raw, *refs), in_specs...]
    unnamed x10 -> x28, local copies, waits for them, and re-layouts: 37.9 us -> 3.06 us
    dot_general x3 -> x0, matrix products: 30.2 us -> none  [the longest x1 15.4 us: on_device(): jnp.dot(metric_band, wide_half.reshape(3 * rows, cols * width), preferred...]
    mul x6 -> x1, local copies, waits for them, and re-layouts: 29.4 us -> 0.01 us  [on_device(): raw = (raw * mask.astype(jnp.bfloat16)[:, None]).reshape(rows, count, width)]
    all_gather x1 -> x0, blocking collectives: 14.1 us -> none  [on_device(): dens = lax.all_gather(local_dens, 'mu', axis=0, tiled=True)]
    concatenate x1, local copies, waits for them, and re-layouts: 13.5 us -> 0.01 us  [gather_mu(): twice = jnp.concatenate(parts + parts, axis=0)]
  transfers between devices with their start and end apart: 2 -> 20, of which waited for: 0 -> 7; matrix products, arithmetic and copies ran while one was open for 8% -> 2% of each run, Pallas kernels for 0% -> 34%
where the time goes in v3:
time: 140 us; the launch traced here: 139 us
  starting transfers between devices  61.7 us (44%)
  Pallas kernels  52.5 us (38%)
  waiting for transfers between devices  9.79 us (7%)
  other arithmetic  8.08 us (6%)
  local copies, waits for them, and re-layouts  5.87 us (4%)
    ppermute x5, starting transfers between devices, to_near(): return lax.ppermute(after(value, *earlier), 'pa', near_pairs)  35.7 us
    pallas_call x4, Pallas kernels, fit_call(): pl.pallas_call(lambda *refs: fit_kernel(chunk, with_raw, *refs), in_specs...  25.7 us
    pallas_call x2, Pallas kernels, half_call(): pl.pallas_call(kernel, in_specs=([WHOLE] if mask is not None else []) + [...  16.8 us
    ppermute x7, starting transfers between devices, rotate(): return lax.ppermute(value, 'pa', pairs)  13.2 us
    pallas_call x1, Pallas kernels, fit_raw_call(): pl.pallas_call(fit_raw_kernel, in_specs=[WHOLE, ANY, ANY, ANY], out_specs...  9.93 us
    ppermute x5, starting transfers between devices, to_far(): return lax.ppermute(after(value, *earlier), 'pa', far_pairs)  7.37 us
    ppermute x7, waiting for transfers between devices, rotate(): return lax.ppermute(value, 'pa', pairs)  5.48 us
    ppermute x3, starting transfers between devices, gather_mu(): lax.ppermute(local, 'mu', [((i + k) % count, i) for i in range(count)])  5.45 us
  transfers between devices with their start and end apart: 20, of which 7 were waited for; matrix products, arithmetic and copies ran while one was open for 2% of the time, Pallas kernels for 34%

profile of v3, /device:TPU:0, one launch (start us, length us, event | category | flops | bytes accessed | tf_op | source)
XLA Modules:
  0.0 138.9 jit_solution(6838308956710584380)
XLA Ops:
  0.6 0.7 convert_convert_fusion
  1.4 0.1 convert_element_type.42
  1.5 0.7 convert_element_type.37
  2.2 0.1 copy.11
  2.5 0.1 copy.12
  2.6 4.6 %slice_multiply_fusion = bf16[128,32,512]{2,1,0:T(8,128)(2,1)} fusion(bf16[128,64,512]{2,1,0:T(8,128)(2,1)} %refs_6_.7, bf16[128,512]{1,0:T(8,128)(2,1)S(1)} %bitcast.8), kind=kLoop, calls=%fused_computation | loop fusion | flops 2097152 | bytes 8519680 | tf_op jit(solution)/shard_map/mul | solution.py:342
  7.3 4.2 %collective-permute-start = (bf16[128,512]{1,0:T(8,128)(2,1)S(1)}, bf16[128,512]{1,0:T(8,128)(2,1)S(1)}, u32[]{:S(2)}, u32[]{:S(2)}) collective-permute-start(bf16[128,512]{1,0:T(8,128)(2,1)S(1)} %mul.25), channel_id=1, source_target_pairs={{1,0},{2,1},{3,2},{0,3},{5,4},{6,5},{7,6},{4,7},{9,8},{10,9},{11,1... | collective-permute-start | bytes 393224 | tf_op jit(solution)/shard_map/ppermute | solution.py:299
  11.4 1.3 collective-permute-start.2
  12.7 2.6 %collective-permute-start.4 = (bf16[128,32,512]{2,1,0:T(8,128)(2,1)}, bf16[128,32,512]{2,1,0:T(8,128)(2,1)}, u32[]{:S(2)}, u32[]{:S(2)}) collective-permute-start(bf16[128,32,512]{2,1,0:T(8,128)(2,1)} %slice_multiply_fusion), channel_id=1, source_target_pairs={{4,8},{8,4},{12,16},{16,12},{20,24},{24,20},{28,32},{32,28},{36,40... | collective-permute-start | bytes 12582920 | tf_op jit(solution)/shard_map/ppermute | solution.py:337
  15.4 0.7 convert_element_type.36.refs_0_.refs_1_
  16.1 0.9 collective-permute-done
  17.0 2.3 %collective-permute-done.1 = bf16[128,512]{1,0:T(8,128)(2,1)S(1)} collective-permute-done((bf16[128,512]{1,0:T(8,128)(2,1)S(1)}, bf16[128,512]{1,0:T(8,128)(2,1)S(1)}, u32[]{:S(2)}, u32[]{:S(2)}) %collective-permute-start.1) | collective-permute-done | bytes 131104 | tf_op jit(solution)/shard_map/ppermute | solution.py:299
  19.4 1.1 collective-permute-done.2
  20.5 0.9 constant_dynamic-slice_fusion.refs_1_.refs_0_
  21.4 9.9 %shard_map.68 = (bf16[1,8,32,16,128]{4,3,2,1,0:T(8,128)(2,1)}, bf16[2,8,32,16,128]{4,3,2,1,0:T(8,128)(2,1)}, bf16[1,8,16,16,128]{4,3,2,1,0:T(8,128)(2,1)}, bf16[...) custom-call(f32[2,1,512]{2,1,0:T(1,128)} %convert_element_type.36.refs_0_.refs_1_, ...), custom_call_target="tpu_custom_call" | custom-call | flops 40000000000 | bytes 120000000 | tf_op jit(solution)/shard_map/pallas_call | solution.py:88
  31.4 0.7 maximum_select_fusion.metric_ref.refs_0_
  32.1 1.6 %collective-permute-start.3 = (bf16[1,8,32,16,128]{4,3,2,1,0:T(8,128)(2,1)}, bf16[1,8,32,16,128]{4,3,2,1,0:T(8,128)(2,1)}, u32[]{:S(2)}, u32[]{:S(2)}) collective-permute-start(bf16[1,8,32,16,128]{4,3,2,1,0:T(8,128)(2,1)} %get-tuple-element.29.refs_4_), channel_id=1, source_target_pairs={{4,8},{8,4},{12,16},{16,12},{20,24},{24,20},{28,32},{32,28},{36,40... | collective-permute-start | bytes 3145736 | tf_op jit(solution)/shard_map/ppermute | solution.py:337
  33.7 0.9 collective-permute-start.7
  34.6 6.9 %shard_map.69.far = bf16[4,8,32,16,128]{4,3,2,1,0:T(8,128)(2,1)} custom-call(bf16[512,512]{1,0:T(8,128)(2,1)} %constant_dynamic-slice_fusion.refs_1_.refs_0_, bf16[128,32,512]{2,1,0:T(8,128)(2,1)} %collective-permute-done.4.refs_1_), custom_call_target="tpu_custom_call" | custom-call | flops 24000000000 | bytes 72000000 | tf_op jit(solution)/shard_map/pallas_call | solution.py:88
  41.6 28.2 %collective-permute-start.5 = (bf16[1,8,32,16,128]{4,3,2,1,0:T(8,128)(2,1)S(1)}, bf16[1,8,32,16,128]{4,3,2,1,0:T(8,128)(2,1)}, u32[]{:S(2)}, u32[]{:S(2)}) collective-permute-start(bf16[1,8,32,16,128]{4,3,2,1,0:T(8,128)(2,1)S(1)} %copy-done.5), channel_id=1, source_target_pairs={{0,4},{4,0},{8,12},{12,8},{16,20},{20,16},{24,28},{28,24},{32,36},... | collective-permute-start | bytes 3145736 | tf_op jit(solution)/shard_map/ppermute | solution.py:334
  69.7 9.9 %shard_map.70 = (bf16[128,64,512]{2,1,0:T(8,128)(2,1)}, bf16[4,128,32,128]{3,2,1,0:T(8,128)(2,1)}) custom-call(bf16[128,384]{1,0:T(8,128)(2,1)} %maximum_select_fusion.metric_ref.refs_0_, bf16[4,8,32,16,128]{4,3,2,1,0:T(8,128)(2,1)} %shard_map.69.far, bf16[4,8,32,16,128]{4,3,2,1,0:T(8,128)(2,1)} %get-tuple-element.27.own, ...), custom_call_target="tpu_custom_call" | custom-call | flops 24000000000 | bytes 72000000 | tf_op jit(solution)/shard_map/pallas_call | solution.py:172
  79.7 0.3 collective-permute-start.8
  79.9 1.5 %collective-permute-start.9 = (bf16[1,8,16,16,128]{4,3,2,1,0:T(8,128)(2,1)S(1)}, bf16[1,8,16,16,128]{4,3,2,1,0:T(8,128)(2,1)}, u32[]{:S(2)}, u32[]{:S(2)}) collective-permute-start(bf16[1,8,16,16,128]{4,3,2,1,0:T(8,128)(2,1)S(1)} %copy-done.7), channel_id=1, source_target_pairs={{4,8},{8,4},{12,16},{16,12},{20,24},{24,20},{28,32},{32,28},{36,40... | collective-permute-start | bytes 1572872 | tf_op jit(solution)/shard_map/ppermute | solution.py:337
  81.4 0.6 broadcast_in_dim.16.refs_2_
  82.1 6.4 %shard_map.71 = (bf16[128,64,512]{2,1,0:T(8,128)(2,1)}, f32[64,64]{1,0:T(8,128)}) custom-call(bf16[128,384]{1,0:T(8,128)(2,1)} %maximum_select_fusion.metric_ref.refs_0_, f32[2,1,512]{2,1,0:T(1,128)} %convert_element_type.36.refs_0_.refs_1_, f32[64,64]{1,0:T(8,128)} %broadcast_in_dim.16.refs_2_, ...), custom_call_target="tpu_custom_call", output_to_operand_aliasing={{0}: (8, {})} | custom-call | flops 20000000000 | bytes 60000000 | tf_op jit(solution)/shard_map/pallas_call | solution.py:272
  88.5 0.7 collective-permute-start.11
  89.2 4.0 %collective-permute-start.10 = (bf16[1,8,16,16,128]{4,3,2,1,0:T(8,128)(2,1)S(1)}, bf16[1,8,16,16,128]{4,3,2,1,0:T(8,128)(2,1)}, u32[]{:S(2)}, u32[]{:S(2)}) collective-permute-start(bf16[1,8,16,16,128]{4,3,2,1,0:T(8,128)(2,1)S(1)} %copy-done.7), channel_id=1, source_target_pairs={{0,4},{4,0},{8,12},{12,8},{16,20},{20,16},{24,28},{28,24},{32,36},... | collective-permute-start | bytes 1572872 | tf_op jit(solution)/shard_map/ppermute | solution.py:334
  93.2 1.4 copy-done.3
  94.6 0.6 copy-done.4
  95.2 8.4 %shard_map.72 = (bf16[128,64,512]{2,1,0:T(8,128)(2,1)}, f32[64,64]{1,0:T(8,128)}) custom-call(bf16[128,384]{1,0:T(8,128)(2,1)} %maximum_select_fusion.metric_ref.refs_0_, f32[2,1,512]{2,1,0:T(1,128)} %convert_element_type.36.refs_0_.refs_1_, f32[64,64]{1,0:T(8,128)} %get-tuple-element.32.refs_2_, ...), custom_call_target="tpu_custom_call", output_to_operand_aliasing={{0}: (8, {})} | custom-call | flops 28000000000 | bytes 84000000 | tf_op jit(solution)/shard_map/pallas_call | solution.py:272
  103.7 3.2 %collective-permute-start.12 = (bf16[1,8,16,16,128]{4,3,2,1,0:T(8,128)(2,1)S(1)}, bf16[1,8,16,16,128]{4,3,2,1,0:T(8,128)(2,1)S(1)}, u32[]{:S(2)}, u32[]{:S(2)}) collective-permute-start(bf16[1,8,16,16,128]{4,3,2,1,0:T(8,128)(2,1)S(1)} %copy-done.6), channel_id=1, source_target_pairs={{0,4},{4,0},{8,12},{12,8},{16,20},{20,16},{24,28},{28,24},{32,36},... | collective-permute-start | bytes 1572872 | tf_op jit(solution)/shard_map/ppermute | solution.py:334
  106.8 5.7 %shard_map.73 = (bf16[128,64,512]{2,1,0:T(8,128)(2,1)}, f32[64,64]{1,0:T(8,128)}) custom-call(bf16[128,384]{1,0:T(8,128)(2,1)} %maximum_select_fusion.metric_ref.refs_0_, f32[2,1,512]{2,1,0:T(1,128)} %convert_element_type.36.refs_0_.refs_1_, f32[64,64]{1,0:T(8,128)} %get-tuple-element.36.refs_2_, ...), custom_call_target="tpu_custom_call", output_to_operand_aliasing={{0}: (8, {})} | custom-call | flops 16000000000 | bytes 48000000 | tf_op jit(solution)/shard_map/pallas_call | solution.py:272
  112.6 0.8 copy-done.8
  113.3 0.2 copy-done.9
  113.5 5.3 %shard_map.74 = (bf16[128,64,512]{2,1,0:T(8,128)(2,1)}, f32[64,64]{1,0:T(8,128)}) custom-call(bf16[128,384]{1,0:T(8,128)(2,1)} %maximum_select_fusion.metric_ref.refs_0_, f32[2,1,512]{2,1,0:T(1,128)} %convert_element_type.36.refs_0_.refs_1_, f32[64,64]{1,0:T(8,128)} %get-tuple-element.41.refs_2_, ...), custom_call_target="tpu_custom_call", output_to_operand_aliasing={{0}: (7, {})} | custom-call | flops 16000000000 | bytes 48000000 | tf_op jit(solution)/shard_map/pallas_call | solution.py:272
  118.8 0.1 collective-permute-start.13
  118.9 1.4 collective-permute-done.13
  120.3 0.8 add.34
  121.1 3.3 %collective-permute-start.14 = (f32[64,64]{1,0:T(8,128)S(1)}, f32[64,64]{1,0:T(8,128)S(1)}, u32[]{:S(2)}, u32[]{:S(2)}) collective-permute-start(f32[64,64]{1,0:T(8,128)S(1)} %add.34), channel_id=1, source_target_pairs={{0,16},{4,20},{8,24},{12,28},{16,0},{20,4},{24,8},{28,12},{32,48},... | collective-permute-start | bytes 49160 | tf_op jit(solution)/shard_map/ppermute | solution.py:312
  124.4 1.5 %collective-permute-start.15 = (f32[64,64]{1,0:T(8,128)S(1)}, f32[64,64]{1,0:T(8,128)S(1)}, u32[]{:S(2)}, u32[]{:S(2)}) collective-permute-start(f32[64,64]{1,0:T(8,128)S(1)} %add.34), channel_id=1, source_target_pairs={{0,8},{4,12},{8,16},{12,20},{16,24},{20,28},{24,0},{28,4},{32,40},... | collective-permute-start | bytes 49160 | tf_op jit(solution)/shard_map/ppermute | solution.py:312
  125.9 1.7 %collective-permute-start.16 = (f32[64,64]{1,0:T(8,128)S(1)}, f32[64,64]{1,0:T(8,128)S(1)}, u32[]{:S(2)}, u32[]{:S(2)}) collective-permute-start(f32[64,64]{1,0:T(8,128)S(1)} %add.34), channel_id=1, source_target_pairs={{0,24},{4,28},{8,0},{12,4},{16,8},{20,12},{24,16},{28,20},{32,56},... | collective-permute-start | bytes 49160 | tf_op jit(solution)/shard_map/ppermute | solution.py:312
  127.6 1.9 %collective-permute-done.15 = f32[64,64]{1,0:T(8,128)S(1)} collective-permute-done((f32[64,64]{1,0:T(8,128)S(1)}, f32[64,64]{1,0:T(8,128)S(1)}, u32[]{:S(2)}, u32[]{:S(2)}) %collective-permute-start.15) | collective-permute-done | bytes 16416 | tf_op jit(solution)/shard_map/ppermute | solution.py:312
  129.5 0.3 collective-permute-done.16
  129.8 3.3 %collective-permute-start.17 = (f32[64,64]{1,0:T(8,128)S(1)}, f32[64,64]{1,0:T(8,128)S(1)}, u32[]{:S(2)}, u32[]{:S(2)}) collective-permute-start(f32[64,64]{1,0:T(8,128)S(1)} %add_add_fusion), channel_id=1, source_target_pairs={{0,64},{4,68},{8,72},{12,76},{16,80},{20,84},{24,88},{28,92},{32,9... | collective-permute-start | bytes 49160 | tf_op jit(solution)/shard_map/ppermute | solution.py:312
  133.1 0.4 collective-permute-start.18
  133.5 2.9 %collective-permute-start.19 = (f32[64,64]{1,0:T(8,128)S(1)}, f32[64,64]{1,0:T(8,128)S(1)}, u32[]{:S(2)}, u32[]{:S(2)}) collective-permute-start(f32[64,64]{1,0:T(8,128)S(1)} %add_add_fusion), channel_id=1, source_target_pairs={{0,96},{4,100},{8,104},{12,108},{16,112},{20,116},{24,120},{28,124... | collective-permute-start | bytes 49160 | tf_op jit(solution)/shard_map/ppermute | solution.py:312
  136.3 1.9 %collective-permute-done.18 = f32[64,64]{1,0:T(8,128)S(1)} collective-permute-done((f32[64,64]{1,0:T(8,128)S(1)}, f32[64,64]{1,0:T(8,128)S(1)}, u32[]{:S(2)}, u32[]{:S(2)}) %collective-permute-start.18) | collective-permute-done | bytes 16416 | tf_op jit(solution)/shard_map/ppermute | solution.py:312
  138.2 0.6 add_multiply_fusion
  (49 shorter events, 0.7 us)
Async XLA Ops:
  2.6 4.6 %copy-start.1 = (bf16[128,512]{1,0:T(8,128)(2,1)S(1)}, bf16[128,512]{1,0:T(8,128)(2,1)}, u32[]{:S(2)}) copy-start(bf16[128,512]{1,0:T(8,128)(2,1)} %param.7) | copy-start | bytes 393220
  7.3 9.8 %collective-permute-start = (bf16[128,512]{1,0:T(8,128)(2,1)S(1)}, bf16[128,512]{1,0:T(8,128)(2,1)S(1)}, u32[]{:S(2)}, u32[]{:S(2)}) collective-permute-start(bf16[128,512]{1,0:T(8,128)(2,1)S(1)} %mul.25), channel_id=1, source_target_pairs={{1,0},{2,1},{3,2},{0,3},{5,4},{6,5},{7,6},{4,7},{9,8},{10,9},{11,1... | collective-permute-start | bytes 393224 | tf_op jit(solution)/shard_map/ppermute | solution.py:299
  11.4 7.9 %collective-permute-start.1 = (bf16[128,512]{1,0:T(8,128)(2,1)S(1)}, bf16[128,512]{1,0:T(8,128)(2,1)S(1)}, u32[]{:S(2)}, u32[]{:S(2)}) collective-permute-start(bf16[128,512]{1,0:T(8,128)(2,1)S(1)} %mul.25), channel_id=1, source_target_pairs={{2,0},{3,1},{0,2},{1,3},{6,4},{7,5},{4,6},{5,7},{10,8},{11,9},{8,1... | collective-permute-start | bytes 393224 | tf_op jit(solution)/shard_map/ppermute | solution.py:299
  11.4 9.0 %collective-permute-start.2 = (bf16[128,512]{1,0:T(8,128)(2,1)S(1)}, bf16[128,512]{1,0:T(8,128)(2,1)S(1)}, u32[]{:S(2)}, u32[]{:S(2)}) collective-permute-start(bf16[128,512]{1,0:T(8,128)(2,1)S(1)} %mul.25), channel_id=1, source_target_pairs={{3,0},{0,1},{1,2},{2,3},{7,4},{4,5},{5,6},{6,7},{11,8},{8,9},{9,10... | collective-permute-start | bytes 393224 | tf_op jit(solution)/shard_map/ppermute | solution.py:299
  12.7 21.9 %collective-permute-start.4 = (bf16[128,32,512]{2,1,0:T(8,128)(2,1)}, bf16[128,32,512]{2,1,0:T(8,128)(2,1)}, u32[]{:S(2)}, u32[]{:S(2)}) collective-permute-start(bf16[128,32,512]{2,1,0:T(8,128)(2,1)} %slice_multiply_fusion), channel_id=1, source_target_pairs={{4,8},{8,4},{12,16},{16,12},{20,24},{24,20},{28,32},{32,28},{36,40... | collective-permute-start | bytes 12582920 | tf_op jit(solution)/shard_map/ppermute | solution.py:337
  21.4 10.0 %copy-start = (bf16[128,384]{1,0:T(8,128)(2,1)S(1)}, bf16[128,384]{1,0:T(8,128)(2,1)}, u32[]{:S(2)}) copy-start(bf16[128,384]{1,0:T(8,128)(2,1)} %param.9) | copy-start | bytes 294916
  31.2 38.5 %collective-permute-start.6 = (bf16[4,8,32,16,128]{4,3,2,1,0:T(8,128)(2,1)}, bf16[4,8,32,16,128]{4,3,2,1,0:T(8,128)(2,1)}, u32[]{:S(2)}, u32[]{:S(2)}) collective-permute-start(bf16[4,8,32,16,128]{4,3,2,1,0:T(8,128)(2,1)} %get-tuple-element.27.own), channel_id=1, source_target_pairs={{0,4},{4,0},{8,12},{12,8},{16,20},{20,16},{24,28},{28,24},{32,36},... | collective-permute-start | bytes 12582920 | tf_op jit(solution)/shard_map/ppermute | solution.py:334
  32.1 49.4 %collective-permute-start.3 = (bf16[1,8,32,16,128]{4,3,2,1,0:T(8,128)(2,1)}, bf16[1,8,32,16,128]{4,3,2,1,0:T(8,128)(2,1)}, u32[]{:S(2)}, u32[]{:S(2)}) collective-permute-start(bf16[1,8,32,16,128]{4,3,2,1,0:T(8,128)(2,1)} %get-tuple-element.29.refs_4_), channel_id=1, source_target_pairs={{4,8},{8,4},{12,16},{16,12},{20,24},{24,20},{28,32},{32,28},{36,40... | collective-permute-start | bytes 3145736 | tf_op jit(solution)/shard_map/ppermute | solution.py:337
  33.7 7.9 %copy-start.5 = (bf16[1,8,32,16,128]{4,3,2,1,0:T(8,128)(2,1)S(1)}, bf16[1,8,32,16,128]{4,3,2,1,0:T(8,128)(2,1)}, u32[]{:S(2)}) copy-start(bf16[1,8,32,16,128]{4,3,2,1,0:T(8,128)(2,1)} %get-tuple-element.29.refs_4_) | copy-start | bytes 3145732
  33.7 59.5 %collective-permute-start.7 = (bf16[2,8,32,16,128]{4,3,2,1,0:T(8,128)(2,1)}, bf16[2,8,32,16,128]{4,3,2,1,0:T(8,128)(2,1)S(1)}, u32[]{:S(2)}, u32[]{:S(2)}) collective-permute-start(bf16[2,8,32,16,128]{4,3,2,1,0:T(8,128)(2,1)} %get-tuple-element.34.refs_4_), channel_id=1, source_target_pairs={{4,8},{8,4},{12,16},{16,12},{20,24},{24,20},{28,32},{32,28},{36,40... | collective-permute-start | bytes 6291464 | tf_op jit(solution)/shard_map/ppermute | solution.py:337
  41.6 38.1 %copy-start.2 = (bf16[2,8,32,16,128]{4,3,2,1,0:T(8,128)(2,1)S(1)}, bf16[2,8,32,16,128]{4,3,2,1,0:T(8,128)(2,1)}, u32[]{:S(2)}) copy-start(bf16[2,8,32,16,128]{4,3,2,1,0:T(8,128)(2,1)} %get-tuple-element.34.refs_4_) | copy-start | bytes 6291460
  41.6 38.4 %copy-start.7 = (bf16[1,8,16,16,128]{4,3,2,1,0:T(8,128)(2,1)S(1)}, bf16[1,8,16,16,128]{4,3,2,1,0:T(8,128)(2,1)}, u32[]{:S(2)}) copy-start(bf16[1,8,16,16,128]{4,3,2,1,0:T(8,128)(2,1)} %get-tuple-element.39.refs_4_) | copy-start | bytes 1572868
  41.6 39.9 %collective-permute-start.5 = (bf16[1,8,32,16,128]{4,3,2,1,0:T(8,128)(2,1)S(1)}, bf16[1,8,32,16,128]{4,3,2,1,0:T(8,128)(2,1)}, u32[]{:S(2)}, u32[]{:S(2)}) collective-permute-start(bf16[1,8,32,16,128]{4,3,2,1,0:T(8,128)(2,1)S(1)} %copy-done.5), channel_id=1, source_target_pairs={{0,4},{4,0},{8,12},{12,8},{16,20},{20,16},{24,28},{28,24},{32,36},... | collective-permute-start | bytes 3145736 | tf_op jit(solution)/shard_map/ppermute | solution.py:334
  79.7 13.5 %collective-permute-start.8 = (bf16[2,8,32,16,128]{4,3,2,1,0:T(8,128)(2,1)S(1)}, bf16[2,8,32,16,128]{4,3,2,1,0:T(8,128)(2,1)S(1)}, u32[]{:S(2)}, u32[]{:S(2)}) collective-permute-start(bf16[2,8,32,16,128]{4,3,2,1,0:T(8,128)(2,1)S(1)} %copy-done.2), channel_id=1, source_target_pairs={{0,4},{4,0},{8,12},{12,8},{16,20},{20,16},{24,28},{28,24},{32,36},... | collective-permute-start | bytes 6291464 | tf_op jit(solution)/shard_map/ppermute | solution.py:334
  79.9 26.9 %collective-permute-start.9 = (bf16[1,8,16,16,128]{4,3,2,1,0:T(8,128)(2,1)S(1)}, bf16[1,8,16,16,128]{4,3,2,1,0:T(8,128)(2,1)}, u32[]{:S(2)}, u32[]{:S(2)}) collective-permute-start(bf16[1,8,16,16,128]{4,3,2,1,0:T(8,128)(2,1)S(1)} %copy-done.7), channel_id=1, source_target_pairs={{4,8},{8,4},{12,16},{16,12},{20,24},{24,20},{28,32},{32,28},{36,40... | collective-permute-start | bytes 1572872 | tf_op jit(solution)/shard_map/ppermute | solution.py:337
  82.1 6.4 %copy-start.6 = (bf16[1,8,16,16,128]{4,3,2,1,0:T(8,128)(2,1)S(1)}, bf16[1,8,16,16,128]{4,3,2,1,0:T(8,128)(2,1)}, u32[]{:S(2)}) copy-start(bf16[1,8,16,16,128]{4,3,2,1,0:T(8,128)(2,1)} %get-tuple-element.44.refs_4_) | copy-start | bytes 1572868
  88.5 24.0 %collective-permute-start.11 = (bf16[1,8,16,16,128]{4,3,2,1,0:T(8,128)(2,1)S(1)}, bf16[1,8,16,16,128]{4,3,2,1,0:T(8,128)(2,1)S(1)}, u32[]{:S(2)}, u32[]{:S(2)}) collective-permute-start(bf16[1,8,16,16,128]{4,3,2,1,0:T(8,128)(2,1)S(1)} %copy-done.6), channel_id=1, source_target_pairs={{4,8},{8,4},{12,16},{16,12},{20,24},{24,20},{28,32},{32,28},{36,40... | collective-permute-start | bytes 1572872 | tf_op jit(solution)/shard_map/ppermute | solution.py:337
  89.2 17.7 %collective-permute-start.10 = (bf16[1,8,16,16,128]{4,3,2,1,0:T(8,128)(2,1)S(1)}, bf16[1,8,16,16,128]{4,3,2,1,0:T(8,128)(2,1)}, u32[]{:S(2)}, u32[]{:S(2)}) collective-permute-start(bf16[1,8,16,16,128]{4,3,2,1,0:T(8,128)(2,1)S(1)} %copy-done.7), channel_id=1, source_target_pairs={{0,4},{4,0},{8,12},{12,8},{16,20},{20,16},{24,28},{28,24},{32,36},... | collective-permute-start | bytes 1572872 | tf_op jit(solution)/shard_map/ppermute | solution.py:334
  93.2 1.4 copy-start.3
  93.2 2.0 %copy-start.4 = (bf16[2,8,32,16,128]{4,3,2,1,0:T(8,128)(2,1)}, bf16[2,8,32,16,128]{4,3,2,1,0:T(8,128)(2,1)S(1)}, u32[]{:S(2)}) copy-start(bf16[2,8,32,16,128]{4,3,2,1,0:T(8,128)(2,1)S(1)} %collective-permute-done.8.refs_5_) | copy-start | bytes 6291460
  103.7 8.9 %collective-permute-start.12 = (bf16[1,8,16,16,128]{4,3,2,1,0:T(8,128)(2,1)S(1)}, bf16[1,8,16,16,128]{4,3,2,1,0:T(8,128)(2,1)S(1)}, u32[]{:S(2)}, u32[]{:S(2)}) collective-permute-start(bf16[1,8,16,16,128]{4,3,2,1,0:T(8,128)(2,1)S(1)} %copy-done.6), channel_id=1, source_target_pairs={{0,4},{4,0},{8,12},{12,8},{16,20},{20,16},{24,28},{28,24},{32,36},... | collective-permute-start | bytes 1572872 | tf_op jit(solution)/shard_map/ppermute | solution.py:334
  112.5 0.8 copy-start.8
  112.5 1.0 copy-start.9
  118.8 1.5 %collective-permute-start.13 = (f32[64,64]{1,0:T(8,128)}, f32[64,64]{1,0:T(8,128)S(1)}, u32[]{:S(2)}, u32[]{:S(2)}) collective-permute-start(f32[64,64]{1,0:T(8,128)} %get-tuple-element.47), channel_id=1, source_target_pairs={{0,4},{4,0},{8,12},{12,8},{16,20},{20,16},{24,28},{28,24},{32,36},... | collective-permute-start | bytes 49160 | tf_op jit(solution)/shard_map/ppermute | solution.py:312
  121.1 6.6 %collective-permute-start.14 = (f32[64,64]{1,0:T(8,128)S(1)}, f32[64,64]{1,0:T(8,128)S(1)}, u32[]{:S(2)}, u32[]{:S(2)}) collective-permute-start(f32[64,64]{1,0:T(8,128)S(1)} %add.34), channel_id=1, source_target_pairs={{0,16},{4,20},{8,24},{12,28},{16,0},{20,4},{24,8},{28,12},{32,48},... | collective-permute-start | bytes 49160 | tf_op jit(solution)/shard_map/ppermute | solution.py:312
  124.4 5.1 %collective-permute-start.15 = (f32[64,64]{1,0:T(8,128)S(1)}, f32[64,64]{1,0:T(8,128)S(1)}, u32[]{:S(2)}, u32[]{:S(2)}) collective-permute-start(f32[64,64]{1,0:T(8,128)S(1)} %add.34), channel_id=1, source_target_pairs={{0,8},{4,12},{8,16},{12,20},{16,24},{20,28},{24,0},{28,4},{32,40},... | collective-permute-start | bytes 49160 | tf_op jit(solution)/shard_map/ppermute | solution.py:312
  125.9 3.9 %collective-permute-start.16 = (f32[64,64]{1,0:T(8,128)S(1)}, f32[64,64]{1,0:T(8,128)S(1)}, u32[]{:S(2)}, u32[]{:S(2)}) collective-permute-start(f32[64,64]{1,0:T(8,128)S(1)} %add.34), channel_id=1, source_target_pairs={{0,24},{4,28},{8,0},{12,4},{16,8},{20,12},{24,16},{28,20},{32,56},... | collective-permute-start | bytes 49160 | tf_op jit(solution)/shard_map/ppermute | solution.py:312
  129.8 6.5 %collective-permute-start.17 = (f32[64,64]{1,0:T(8,128)S(1)}, f32[64,64]{1,0:T(8,128)S(1)}, u32[]{:S(2)}, u32[]{:S(2)}) collective-permute-start(f32[64,64]{1,0:T(8,128)S(1)} %add_add_fusion), channel_id=1, source_target_pairs={{0,64},{4,68},{8,72},{12,76},{16,80},{20,84},{24,88},{28,92},{32,9... | collective-permute-start | bytes 49160 | tf_op jit(solution)/shard_map/ppermute | solution.py:312
  133.1 5.1 %collective-permute-start.18 = (f32[64,64]{1,0:T(8,128)S(1)}, f32[64,64]{1,0:T(8,128)S(1)}, u32[]{:S(2)}, u32[]{:S(2)}) collective-permute-start(f32[64,64]{1,0:T(8,128)S(1)} %add_add_fusion), channel_id=1, source_target_pairs={{0,32},{4,36},{8,40},{12,44},{16,48},{20,52},{24,56},{28,60},{32,6... | collective-permute-start | bytes 49160 | tf_op jit(solution)/shard_map/ppermute | solution.py:312
  133.5 4.8 %collective-permute-start.19 = (f32[64,64]{1,0:T(8,128)S(1)}, f32[64,64]{1,0:T(8,128)S(1)}, u32[]{:S(2)}, u32[]{:S(2)}) collective-permute-start(f32[64,64]{1,0:T(8,128)S(1)} %add_add_fusion), channel_id=1, source_target_pairs={{0,96},{4,100},{8,104},{12,108},{16,112},{20,116},{24,120},{28,124... | collective-permute-start | bytes 49160 | tf_op jit(solution)/shard_map/ppermute | solution.py:312

commit v4 on v0

v4 whole, which is shorter than its diff:
```python
import math

import jax
import jax.numpy as jnp
from jax import lax
from jax.experimental import pallas as pl
from jax.experimental.pallas import tpu as pltpu
from jax.sharding import PartitionSpec as P

BS = 64
SIG = 128
PB = 16
QB = 16
MIB = 2**20

RAW_MU = 32
RAW_STEP = 32
CHUNKS = ((0, 0, 32), (128, 0, 32), (256, 0, 32), (384, 0, 16), (384, 16, 16))
WITH_RAW = (True, True, True, True, False)
HALF_MIB = 56
HALF_COST = 1
FIT_MIB = 24
FAR_COST = 20
FIT_COST = 0.3
ANY = pl.BlockSpec(memory_space=pl.ANY)
WHOLE = pl.BlockSpec(memory_space=pltpu.VMEM)


def cost(us):
    return pl.CostEstimate(
        flops=int(us * 4e9), bytes_accessed=int(us * 12e6), transcendentals=0
    )


def params(mib):
    return pltpu.CompilerParams(vmem_limit_bytes=mib * MIB)


def half_rows(x, dens, scratch, cols):
    flat = jnp.dot(x.reshape(PB * cols, x.shape[2]), dens, preferred_element_type=jnp.float32)
    pitch = cols + 1
    for t in range(scratch.shape[0]):
        for p in range(PB):
            scratch[t, p * pitch:p * pitch + cols] = flat[
                p * cols:(p + 1) * cols, t * SIG:(t + 1) * SIG
            ]


def turned(scratch, t, m, cols):
    return scratch[t, pl.ds(m, PB, stride=cols + 1), :].astype(jnp.bfloat16)


def half_kernel(mask_ref, *refs):
    parts, tc_hbm = refs[:4], refs[4]
    dens_ref, all_hbm, chunk_hbm = refs[5], refs[6], refs[7:-5]
    tc_buf, staged, scratch, in_sem, out_sem = refs[-5:]
    rows, cols, width = tc_buf.shape
    blocks = rows // PB

    def fetch(b):
        rows_b = pl.ds(b * PB, PB)
        return pltpu.make_async_copy(tc_hbm.at[rows_b], tc_buf.at[rows_b], in_sem.at[b])

    for b in range(blocks):
        fetch(b).start()
    me = lax.axis_index("mu")
    depth = parts[0].shape[0]
    for k, part in enumerate(parts):
        at = lax.rem(me + k, len(parts)) * depth
        dens_ref[pl.ds(pl.multiple_of(at, depth), depth), :] = part[...]

    def step(b, carry):
        fetch(b).wait()
        x = tc_buf[pl.ds(b * PB, PB)] * mask_ref[(b * PB) // BS].astype(jnp.bfloat16)
        half_rows(x, dens_ref[...], scratch, cols)
        for t in range(width // SIG):
            for m in range(cols):
                staged[t, b, m] = turned(scratch, t, m, cols)
        for k, (s, mu0, count) in enumerate(CHUNKS):
            part = staged.at[s // SIG, b, pl.ds(mu0, count)]
            pltpu.make_async_copy(part, chunk_hbm[k].at[b], out_sem.at[k]).start()
        pltpu.make_async_copy(staged.at[:, b], all_hbm.at[:, b], out_sem.at[len(CHUNKS)]).start()
        return carry

    lax.fori_loop(0, blocks, step, 0)
    for k, (s, mu0, count) in enumerate(CHUNKS):
        part = staged.at[s // SIG, :, pl.ds(mu0, count)]
        pltpu.make_async_copy(part, chunk_hbm[k], out_sem.at[k]).wait()
    pltpu.make_async_copy(staged, all_hbm, out_sem.at[len(CHUNKS)]).wait()


def half_call(tc, mask, parts):
    rows, cols, width = tc.shape
    whole = (width // SIG, rows // PB, cols, PB, SIG)
    shapes = [(width, width), whole] + [(rows // PB, n, PB, SIG) for _, _, n in CHUNKS]
    return pl.pallas_call(
        half_kernel,
        in_specs=[WHOLE] * (1 + len(parts)) + [ANY],
        out_specs=[WHOLE] + [ANY] * (len(CHUNKS) + 1),
        out_shape=[jax.ShapeDtypeStruct(shape, jnp.bfloat16) for shape in shapes],
        scratch_shapes=[
            pltpu.VMEM(tc.shape, jnp.bfloat16),
            pltpu.VMEM(whole, jnp.bfloat16),
            pltpu.VMEM((width // SIG, PB * (cols + 1) + 8, SIG), jnp.float32),
            pltpu.SemaphoreType.DMA((rows // PB,)),
            pltpu.SemaphoreType.DMA((len(CHUNKS) + 1,)),
        ],
        compiler_params=params(HALF_MIB),
        cost_estimate=cost(HALF_COST),
    )(mask, *parts, tc)


def far_half_kernel(dens_ref, raw_ref, out_ref, scratch):
    def step(b, carry):
        half_block(dens_ref, raw_ref, out_ref, scratch, b)
        return carry

    lax.fori_loop(0, raw_ref.shape[0] // PB, step, 0)


def half_block(dens_ref, raw_ref, out_ref, scratch, b):
    cols = raw_ref.shape[1]
    half_rows(raw_ref[pl.ds(b * PB, PB)], dens_ref[...], scratch, cols)
    for t in range(scratch.shape[0]):
        for m in range(cols):
            out_ref[t, b, m] = turned(scratch, t, m, cols)


def far_half_call(raw_far, dens):
    rows, count, width = raw_far.shape
    return pl.pallas_call(
        far_half_kernel,
        in_specs=[WHOLE, WHOLE],
        out_specs=WHOLE,
        out_shape=jax.ShapeDtypeStruct(
            (width // SIG, rows // PB, count, PB, SIG), jnp.bfloat16
        ),
        scratch_shapes=[pltpu.VMEM((width // SIG, PB * (count + 1) + 8, SIG), jnp.float32)],
        compiler_params=params(16),
        cost_estimate=cost(FAR_COST),
    )(dens, raw_far)


def fit_tile(pieces, metric_ref, scratch, pitch, count):
    metric = metric_ref[...]
    rows = metric.shape[0]

    def fit(pair, carry):
        columns = [jnp.concatenate(pieces(m), axis=0) for m in (2 * pair, 2 * pair + 1)]
        y = jnp.dot(metric, jnp.concatenate(columns, axis=1), preferred_element_type=jnp.float32)
        scratch[pl.ds(2 * pair, rows, stride=pitch), :] = y[:, :SIG]
        scratch[pl.ds(2 * pair + 1, rows, stride=pitch), :] = y[:, SIG:]
        return carry

    lax.fori_loop(0, count // 2, fit, 0, unroll=8)


def raw_kernel(metric_ref, far_ref, own, near, fitted, rows_ref, *refs):
    own_buf, near_buf, scratch, in_sem, out_sem = refs
    tiles, rows, count, _ = rows_ref.shape
    pitch = count + 1
    part = pl.ds(RAW_MU, count)

    def fetch(t):
        return [
            pltpu.make_async_copy(src.at[t, :, part], buf.at[t], in_sem.at[k, t])
            for k, (src, buf) in enumerate(((own, own_buf), (near, near_buf)))
        ]

    def put(t):
        lanes = pl.ds(pl.multiple_of(t * SIG, SIG), SIG)
        return pltpu.make_async_copy(rows_ref.at[t], fitted.at[:, part, lanes], out_sem.at[t])

    for t in range(tiles):
        for copy in fetch(t):
            copy.start()

    def tile(t, carry):
        for copy in fetch(t):
            copy.wait()

        def pieces(m):
            return [buf[t, :, m].reshape(rows, SIG) for buf in (far_ref, own_buf, near_buf)]

        fit_tile(pieces, metric_ref, scratch, pitch, count)

        def store(block, inner):
            for q in range(QB):
                row = block * QB + q
                rows_ref[t, row] = scratch[pl.ds(row * pitch, count), :].astype(jnp.bfloat16)
            return inner

        lax.fori_loop(0, rows // QB, store, 0)
        put(t).start()
        return carry

    lax.fori_loop(0, tiles, tile, 0)
    for t in range(tiles):
        put(t).wait()


def raw_call(far, own, near, metric, shape):
    rows, _, width = shape
    count = RAW_STEP
    tiles = width // SIG
    buf = pltpu.VMEM((tiles, rows // PB, count, PB, SIG), jnp.bfloat16)
    return pl.pallas_call(
        raw_kernel,
        in_specs=[WHOLE, WHOLE, ANY, ANY],
        out_specs=[ANY, WHOLE],
        out_shape=[
            jax.ShapeDtypeStruct(shape, jnp.bfloat16),
            jax.ShapeDtypeStruct((tiles, rows, count, SIG), jnp.bfloat16),
        ],
        scratch_shapes=[
            buf,
            buf,
            pltpu.VMEM((rows * (count + 1), SIG), jnp.float32),
            pltpu.SemaphoreType.DMA((2, tiles)),
            pltpu.SemaphoreType.DMA((tiles,)),
        ],
        compiler_params=params(FIT_MIB),
        cost_estimate=cost(FIT_COST),
    )(metric, far, own, near)


def fit_kernel(chunk, raws, metric_ref, mask_ref, acc_ref, far_ref, *refs):
    s, mu0, count = chunk
    raw_refs, refs = refs[:raws], refs[raws:]
    own, near, tc, _, fitted, exch_ref, own_buf, near_buf, tc_buf, staged, scratch = refs[:11]
    in_sem, out_sem = refs[11:]
    rows = metric_ref.shape[0]
    pitch = count + 1
    tile = s // SIG
    part = pl.ds(mu0, count)
    lanes = pl.ds(s, SIG)
    copies = [
        pltpu.make_async_copy(src, buf, in_sem.at[k])
        for k, (src, buf) in enumerate((
            (own.at[tile, :, part], own_buf),
            (near.at[tile, :, part], near_buf),
            (tc.at[:, :, lanes], tc_buf),
        ))
    ]
    for copy in copies:
        copy.start()
    for copy in copies[:2]:
        copy.wait()

    def pieces(m):
        return [buf[:, m].reshape(rows, SIG) for buf in (far_ref, own_buf, near_buf)]

    fit_tile(pieces, metric_ref, scratch, pitch, count)
    copies[2].wait()

    def contract(block, total):
        first = pl.multiple_of(block * QB, QB)
        mask = mask_ref[(block * QB) // BS, :, s:s + SIG].astype(jnp.bfloat16)
        left = []
        for q in range(QB):
            f = scratch[pl.ds((first + q) * pitch, count), :].astype(jnp.bfloat16)
            staged[first + q] = f
            if raws:
                f = jnp.concatenate([f] + [r[tile, first + q] for r in raw_refs], axis=0)
            left.append(f * mask)
        right = [tc_buf[first + q] for q in range(QB)]
        return total + lax.dot_general(
            jnp.concatenate(left, axis=1),
            jnp.concatenate(right, axis=1),
            (((1,), (1,)), ((), ())),
            preferred_element_type=jnp.float32,
        )

    lines = count + raws * RAW_STEP
    total = lax.fori_loop(
        0, rows // QB, contract, jnp.zeros((lines, acc_ref.shape[1]), jnp.float32), unroll=2
    )
    store = pltpu.make_async_copy(staged, fitted.at[:, part, lanes], out_sem)
    store.start()
    exch_ref[...] = acc_ref[...]
    exch_ref[mu0:mu0 + count, :] += total[:count]
    if raws:
        exch_ref[RAW_MU:, :] += total[count:]
    store.wait()


def fit_call(chunk, far, own, near, metric, tc, mask, acc, raw_rows, fitted):
    _, _, count = chunk
    rows, cols, _ = tc.shape
    raws = len(raw_rows)
    args = [metric, mask, acc, far, *raw_rows, own, near, tc, fitted]
    buf = pltpu.VMEM((rows // PB, count, PB, SIG), jnp.bfloat16)
    return pl.pallas_call(
        lambda *refs: fit_kernel(chunk, raws, *refs),
        in_specs=[WHOLE] * (4 + raws) + [ANY] * 4,
        out_specs=[ANY, WHOLE],
        out_shape=[
            jax.ShapeDtypeStruct(tc.shape, jnp.bfloat16),
            jax.ShapeDtypeStruct(acc.shape, jnp.float32),
        ],
        scratch_shapes=[
            buf,
            buf,
            pltpu.VMEM((rows, cols, SIG), jnp.bfloat16),
            pltpu.VMEM((rows, count, SIG), jnp.bfloat16),
            pltpu.VMEM((rows * (count + 1), SIG), jnp.float32),
            pltpu.SemaphoreType.DMA((3,)),
            pltpu.SemaphoreType.DMA,
        ],
        input_output_aliases={len(args) - 1: 0},
        compiler_params=params(FIT_MIB),
        cost_estimate=cost(FIT_COST),
    )(*args)


def rotate(value, stride, count, k):
    size = lax.axis_size("pa")
    span = stride * count
    pairs = [
        (i, (i // span) * span + ((i // stride + k) % count) * stride + i % stride)
        for i in range(size)
    ]
    return lax.ppermute(value, "pa", pairs)


def sum_pa(value):
    value = value + rotate(value, 1, 2, 1)
    for stride in (2, 8):
        parts = [rotate(value, stride, 4, k) for k in (1, 2, 3)]
        value = (value + parts[1]) + (parts[0] + parts[2])
    return value


def after(value, *earlier):
    return lax.optimization_barrier((value,) + earlier)[0]


def on_device(three_center, center_mask, density, density_mask, metric_band):
    rows, cols, width = three_center.shape
    size = lax.axis_size("pa")
    near_pairs = [(i, i ^ 1) for i in range(size)]
    far_pairs = [(i, i + 1 if i % 2 else i - 1) for i in range(1, size - 1)]

    def to_far(value, *earlier):
        return lax.ppermute(after(value, *earlier), "pa", far_pairs)

    mask = jnp.repeat(center_mask, BS, axis=2).astype(jnp.float32)

    def masked(mu0, lane_mask):
        piece = three_center[:, mu0:mu0 + RAW_STEP, :].reshape(rows // BS, BS, RAW_STEP, width)
        piece = piece * lane_mask.astype(jnp.bfloat16)[:, None]
        return piece.reshape(rows, RAW_STEP, width)

    raw = masked(RAW_MU, mask)
    raw_far = to_far(raw)
    block_mask = jnp.repeat(jnp.repeat(density_mask, BS, axis=0), BS, axis=1)
    local = after(density * block_mask.astype(jnp.bfloat16), raw)
    count = lax.axis_size("mu")
    parts = [local] + [
        lax.ppermute(local, "mu", [((i + k) % count, i) for i in range(count)])
        for k in range(1, count)
    ]
    low, middle, high = jnp.split(metric_band, 3, axis=1)
    metric = jnp.where(
        lax.axis_index("pa") % 2 == 0,
        metric_band,
        jnp.concatenate([high, middle, low], axis=1),
    )

    dens, own, *chunks = half_call(three_center, mask, parts)
    far = [to_far(chunks[0])]
    near = lax.ppermute(own, "pa", near_pairs)
    half_far = far_half_call(raw_far, dens)
    far.append(to_far(chunks[1], half_far))
    fitted, raw_rows = raw_call(half_far, own, near, metric, three_center.shape)
    far += [to_far(chunks[2], raw_rows), to_far(chunks[3], raw_rows)]
    acc = jnp.zeros((cols, cols), jnp.float32)
    for c, chunk in enumerate(CHUNKS):
        fitted, acc = fit_call(
            chunk, far[c], own, near, metric, three_center, mask, acc,
            [raw_rows] if WITH_RAW[c] else [], fitted,
        )
        if len(far) < len(CHUNKS):
            far.append(to_far(chunks[len(far)], acc))
    scale = 1.0 / math.sqrt(rows * size * width)
    return (fitted, sum_pa(acc) * scale)


def solution(mesh):
    placed = (P("pa", "mu", None), P("pa", "mu", None), P("mu", None), P("mu", None), P("pa", None))
    return jax.shard_map(
        on_device,
        mesh=mesh,
        in_specs=placed,
        out_specs=(P("pa", "mu", None), P("mu", None)),
        check_vma=False,
    )
```

time: 340 us -> 129 us (0.38)
  blocking collectives: 214 us -> 0 us
  local copies, waits for them, and re-layouts: 80.8 us -> 3.72 us
  starting transfers between devices: 5.78 us -> 57.1 us
  Pallas kernels: 0 us -> 42.9 us
  matrix products: 30.2 us -> 0 us
  waiting for transfers between devices: 0.01 us -> 17.4 us
    psum x1 -> x0, blocking collectives: 199 us -> none  [on_device(): total = lax.psum(partial_block, 'pa')]
    ppermute x2 -> x17, starting transfers between devices: 5.78 us -> 57.1 us  [the longest x7 43.8 us: rotate(): return lax.ppermute(value, 'pa', pairs)]
    pallas_call x0 -> x8, Pallas kernels: none -> 42.9 us  [the longest x5 19.2 us: fit_call(): pl.pallas_call(lambda *refs: fit_kernel(chunk, raws, *refs), in_specs=[WH...]
    unnamed x10 -> x33, local copies, waits for them, and re-layouts: 37.9 us -> 2.38 us
    dot_general x3 -> x0, matrix products: 30.2 us -> none  [the longest x1 15.4 us: on_device(): jnp.dot(metric_band, wide_half.reshape(3 * rows, cols * width), preferred...]
    mul x6 -> x1, local copies, waits for them, and re-layouts: 29.4 us -> 0.02 us  [masked(): piece = piece * lane_mask.astype(jnp.bfloat16)[:, None]]
    ppermute x2 -> x17, waiting for transfers between devices: 0.01 us -> 17.4 us  [the longest x7 7.78 us: rotate(): return lax.ppermute(value, 'pa', pairs)]
    all_gather x1 -> x0, blocking collectives: 14.1 us -> none  [on_device(): dens = lax.all_gather(local_dens, 'mu', axis=0, tiled=True)]
  transfers between devices with their start and end apart: 2 -> 17, of which waited for: 0 -> 8; matrix products, arithmetic and copies ran while one was open for 8% -> 1% of each run, Pallas kernels for 0% -> 31%
where the time goes in v4:
time: 129 us; the launch traced here: 128 us
  starting transfers between devices  57.1 us (44%)
  Pallas kernels  42.9 us (33%)
  waiting for transfers between devices  17.4 us (13%)
  other arithmetic  5.91 us (5%)
  local copies, waits for them, and re-layouts  3.72 us (3%)
    ppermute x7, starting transfers between devices, rotate(): return lax.ppermute(value, 'pa', pairs)  43.8 us
    pallas_call x5, Pallas kernels, fit_call(): pl.pallas_call(lambda *refs: fit_kernel(chunk, raws, *refs), in_specs=[WH...  19.2 us
    pallas_call x1, Pallas kernels, half_call(): pl.pallas_call(half_kernel, in_specs=[WHOLE] * (1 + len(parts)) + [ANY],...  10.9 us
    ppermute x7, waiting for transfers between devices, rotate(): return lax.ppermute(value, 'pa', pairs)  7.78 us
    ppermute x3, starting transfers between devices, on_device(): lax.ppermute(local, 'mu', [((i + k) % count, i) for i in range(count)])  6.66 us
    ppermute x6, starting transfers between devices, to_far(): return lax.ppermute(after(value, *earlier), 'pa', far_pairs)  6.52 us
    pallas_call x1, Pallas kernels, raw_call(): pl.pallas_call(raw_kernel, in_specs=[WHOLE, WHOLE, ANY, ANY], out_specs=[...  6.48 us
    pallas_call x1, Pallas kernels, far_half_call(): pl.pallas_call(far_half_kernel, in_specs=[WHOLE, WHOLE], out_specs=WHOLE,...  6.32 us
  transfers between devices with their start and end apart: 17, of which 8 were waited for; matrix products, arithmetic and copies ran while one was open for 1% of the time, Pallas kernels for 31%

profile of v4, /device:TPU:0, one launch (start us, length us, event | category | flops | bytes accessed | tf_op | source)
XLA Modules:
  0.0 128.0 jit_solution(3046645587748374142)
XLA Ops:
  0.7 0.7 convert_convert_fusion
  1.4 0.1 broadcast_in_dim.19
  1.5 0.1 convert_element_type.42
  1.6 4.5 %slice_multiply_fusion = bf16[128,32,512]{2,1,0:T(8,128)(2,1)} fusion(bf16[128,64,512]{2,1,0:T(8,128)(2,1)} %refs_6_.1, bf16[128,512]{1,0:T(8,128)(2,1)S(1)} %bitcast.10), kind=kLoop, calls=%fused_computation | loop fusion | flops 2097152 | bytes 8519680 | tf_op jit(solution)/shard_map/mul | solution.py:351
  6.0 2.8 %collective-permute-start.4 = (bf16[128,32,512]{2,1,0:T(8,128)(2,1)}, bf16[128,32,512]{2,1,0:T(8,128)(2,1)}, u32[]{:S(2)}, u32[]{:S(2)}) collective-permute-start(bf16[128,32,512]{2,1,0:T(8,128)(2,1)} %slice_multiply_fusion), channel_id=1, source_target_pairs={{4,8},{8,4},{12,16},{16,12},{20,24},{24,20},{28,32},{32,28},{36,40... | collective-permute-start | bytes 12582920 | tf_op jit(solution)/shard_map/ppermute | solution.py:345
  8.9 0.1 copy.12
  9.0 0.1 broadcast_in_dim.17
  9.0 0.1 convert_element_type.38
  9.2 0.1 copy.13
  9.3 2.1 %collective-permute-start.2 = (bf16[128,512]{1,0:T(8,128)(2,1)S(1)}, bf16[128,512]{1,0:T(8,128)(2,1)S(1)}, u32[]{:S(2)}, u32[]{:S(2)}) collective-permute-start(bf16[128,512]{1,0:T(8,128)(2,1)S(1)} %mul.22.refs_0_), channel_id=1, source_target_pairs={{3,0},{0,1},{1,2},{2,3},{7,4},{4,5},{5,6},{6,7},{11,8},{8,9},{9,10... | collective-permute-start | bytes 393224 | tf_op jit(solution)/shard_map/ppermute | solution.py:360
  11.4 3.6 %collective-permute-start.1 = (bf16[128,512]{1,0:T(8,128)(2,1)S(1)}, bf16[128,512]{1,0:T(8,128)(2,1)S(1)}, u32[]{:S(2)}, u32[]{:S(2)}) collective-permute-start(bf16[128,512]{1,0:T(8,128)(2,1)S(1)} %mul.22.refs_0_), channel_id=1, source_target_pairs={{2,0},{3,1},{0,2},{1,3},{6,4},{7,5},{4,6},{5,7},{10,8},{11,9},{8,1... | collective-permute-start | bytes 393224 | tf_op jit(solution)/shard_map/ppermute | solution.py:360
  15.0 1.0 collective-permute-start
  16.0 0.1 broadcast_in_dim.15
  16.1 0.7 convert_element_type.36.mask_ref.refs_1_
  16.7 1.0 collective-permute-done.2.refs_3_
  17.7 4.3 %collective-permute-done.1.refs_2_ = bf16[128,512]{1,0:T(8,128)(2,1)S(1)} collective-permute-done((bf16[128,512]{1,0:T(8,128)(2,1)S(1)}, bf16[128,512]{1,0:T(8,128)(2,1)S(1)}, u32[]{:S(2)}, u32[]{:S(2)}) %collective-permute-start.1) | collective-permute-done | bytes 131104 | tf_op jit(solution)/shard_map/ppermute | solution.py:360
  22.0 0.6 copy-done.11
  22.7 0.6 copy-done.12
  23.3 10.9 %shard_map.68 = (bf16[512,512]{1,0:T(8,128)(2,1)}, bf16[4,8,64,16,128]{4,3,2,1,0:T(8,128)(2,1)}, bf16[8,32,16,128]{3,2,1,0:T(8,128)(2,1)}, bf16[8,32,16,128]{3,2...) custom-call(f32[2,1,512]{2,1,0:T(1,128)} %convert_element_type.36.ma, ...), custom_call_target="tpu_custom_call" | custom-call | flops 4000000000 | bytes 12000000 | tf_op jit(solution)/shard_map/pallas_call | solution.py:96
  34.2 0.1 collective-permute-start.5
  34.4 0.7 collective-permute-start.3
  35.2 0.0 collective-permute-done.4.raw_ref
  35.2 1.0 copy-done.2
  36.2 6.3 %shard_map.69.far_ref = bf16[4,8,32,16,128]{4,3,2,1,0:T(8,128)(2,1)S(1)} custom-call(bf16[512,512]{1,0:T(8,128)(2,1)S(1)} %copy-done.2, bf16[128,32,512]{2,1,0:T(8,128)(2,1)} %collective-permute-done.4.raw_ref), custom_call_target="tpu_custom_call" | custom-call | flops 80000000000 | bytes 240000000 | tf_op jit(solution)/shard_map/pallas_call | solution.py:131
  42.5 0.0 slice-start
  42.6 0.0 copy-start.1
  42.6 0.9 collective-permute-start.6
  43.5 4.3 %collective-permute-done.5.near.refs_6_.refs_5_ = bf16[4,8,64,16,128]{4,3,2,1,0:T(8,128)(2,1)} collective-permute-done((bf16[4,8,64,16,128]{4,3,2,1,0:T(8,128)(2,1)}, bf16[4,8,64,16,128]{4,3,2,1,0:T(8,128)(2,1)}, u32[]{:S(2)}, u32[]{:S(2)}) %collective-permute-start.5) | collective-permute-done | bytes 8388640 | tf_op jit(solution)/shard_map/ppermute | solution.py:372
  47.8 6.5 %shard_map.70 = (bf16[128,64,512]{2,1,0:T(8,128)(2,1)}, bf16[4,128,32,128]{3,2,1,0:T(8,128)(2,1)S(1)}) custom-call(bf16[128,384]{1,0:T(8,128)(2,1)S(1)} %maximum_select_fusion.metric_ref.refs_0_, bf16[4,8,32,16,128]{4,3,2,1,0:T(8,128)(2,1)S(1)} %shard_map.69.far_ref, bf16[4,8,64,16,128]{4,3,2,1,0:T(8,128)(2,1)S(1)} %copy-done, ...), custom_call_target="tpu_custom_call" | custom-call | flops 1200000000 | bytes 3600000 | tf_op jit(solution)/shard_map/pallas_call | solution.py:207
  54.3 0.7 collective-permute-start.7
  55.1 0.7 collective-permute-start.8
  55.8 4.3 %shard_map.71 = (bf16[128,64,512]{2,1,0:T(8,128)(2,1)}, f32[64,64]{1,0:T(8,128)S(1)}) custom-call(bf16[128,384]{1,0:T(8,128)(2,1)S(1)} %maximum_select_fusion.metric_ref.refs_0_, f32[2,1,512]{2,1,0:T(1,128)S(1)} %copy-done.1, f32[64,64]{1,0:T(8,128)S(1)} %broadcast_in_dim.16.refs_2_, ...), custom_call_target="tpu_custom_call", output_to_operand_aliasing={{0}: (8, {})} | custom-call | flops 1200000000 | bytes 3600000 | tf_op jit(solution)/shard_map/pallas_call | solution.py:293
  60.1 0.7 collective-permute-start.9
  60.8 4.2 %shard_map.72 = (bf16[128,64,512]{2,1,0:T(8,128)(2,1)}, f32[64,64]{1,0:T(8,128)S(1)}) custom-call(bf16[128,384]{1,0:T(8,128)(2,1)S(1)} %maximum_select_fusion.metric_ref.refs_0_, f32[2,1,512]{2,1,0:T(1,128)S(1)} %copy-done.1, f32[64,64]{1,0:T(8,128)S(1)} %get-tuple-element.32.refs_2_, ...), custom_call_target="tpu_custom_call", output_to_operand_aliasing={{0}: (8, {})} | custom-call | flops 1200000000 | bytes 3600000 | tf_op jit(solution)/shard_map/pallas_call | solution.py:293
  65.0 4.2 %shard_map.73 = (bf16[128,64,512]{2,1,0:T(8,128)(2,1)}, f32[64,64]{1,0:T(8,128)S(1)}) custom-call(bf16[128,384]{1,0:T(8,128)(2,1)S(1)} %maximum_select_fusion.metric_ref.refs_0_, f32[2,1,512]{2,1,0:T(1,128)S(1)} %copy-done.1, f32[64,64]{1,0:T(8,128)S(1)} %get-tuple-element.36.refs_2_, ...), custom_call_target="tpu_custom_call", output_to_operand_aliasing={{0}: (8, {})} | custom-call | flops 1200000000 | bytes 3600000 | tf_op jit(solution)/shard_map/pallas_call | solution.py:293
  69.3 3.3 %shard_map.74 = (bf16[128,64,512]{2,1,0:T(8,128)(2,1)}, f32[64,64]{1,0:T(8,128)S(1)}) custom-call(bf16[128,384]{1,0:T(8,128)(2,1)S(1)} %maximum_select_fusion.metric_ref.refs_0_, f32[2,1,512]{2,1,0:T(1,128)S(1)} %copy-done.1, f32[64,64]{1,0:T(8,128)S(1)} %get-tuple-element.40.refs_2_, ...), custom_call_target="tpu_custom_call", output_to_operand_aliasing={{0}: (8, {})} | custom-call | flops 1200000000 | bytes 3600000 | tf_op jit(solution)/shard_map/pallas_call | solution.py:293
  72.6 3.2 %shard_map.75 = (bf16[128,64,512]{2,1,0:T(8,128)(2,1)}, f32[64,64]{1,0:T(8,128)S(1)}) custom-call(bf16[128,384]{1,0:T(8,128)(2,1)S(1)} %maximum_select_fusion.metric_ref.refs_0_, f32[2,1,512]{2,1,0:T(1,128)S(1)} %copy-done.1, f32[64,64]{1,0:T(8,128)S(1)} %get-tuple-element.44.refs_2_, ...), custom_call_target="tpu_custom_call", output_to_operand_aliasing={{0}: (7, {})} | custom-call | flops 1200000000 | bytes 3600000 | tf_op jit(solution)/shard_map/pallas_call | solution.py:293
  75.8 30.1 %collective-permute-start.10 = (f32[64,64]{1,0:T(8,128)S(1)}, f32[64,64]{1,0:T(8,128)S(1)}, u32[]{:S(2)}, u32[]{:S(2)}) collective-permute-start(f32[64,64]{1,0:T(8,128)S(1)} %get-tuple-element.49), channel_id=1, source_target_pairs={{0,4},{4,0},{8,12},{12,8},{16,20},{20,16},{24,28},{28,24},{32,36},... | collective-permute-start | bytes 49160 | tf_op jit(solution)/shard_map/ppermute | solution.py:323
  106.0 0.9 collective-permute-done.10
  106.8 6.8 %collective-permute-start.13 = (f32[64,64]{1,0:T(8,128)S(1)}, f32[64,64]{1,0:T(8,128)S(1)}, u32[]{:S(2)}, u32[]{:S(2)}) collective-permute-start(f32[64,64]{1,0:T(8,128)S(1)} %add.26), channel_id=1, source_target_pairs={{0,24},{4,28},{8,0},{12,4},{16,8},{20,12},{24,16},{28,20},{32,56},... | collective-permute-start | bytes 49160 | tf_op jit(solution)/shard_map/ppermute | solution.py:323
  113.6 1.5 %collective-permute-start.11 = (f32[64,64]{1,0:T(8,128)S(1)}, f32[64,64]{1,0:T(8,128)S(1)}, u32[]{:S(2)}, u32[]{:S(2)}) collective-permute-start(f32[64,64]{1,0:T(8,128)S(1)} %add.26), channel_id=1, source_target_pairs={{0,16},{4,20},{8,24},{12,28},{16,0},{20,4},{24,8},{28,12},{32,48},... | collective-permute-start | bytes 49160 | tf_op jit(solution)/shard_map/ppermute | solution.py:323
  115.2 0.1 collective-permute-done.13
  115.2 3.9 %collective-permute-done.12 = f32[64,64]{1,0:T(8,128)S(1)} collective-permute-done((f32[64,64]{1,0:T(8,128)S(1)}, f32[64,64]{1,0:T(8,128)S(1)}, u32[]{:S(2)}, u32[]{:S(2)}) %collective-permute-start.12) | collective-permute-done | bytes 16416 | tf_op jit(solution)/shard_map/ppermute | solution.py:323
  119.1 2.8 %collective-permute-start.16 = (f32[64,64]{1,0:T(8,128)S(1)}, f32[64,64]{1,0:T(8,128)S(1)}, u32[]{:S(2)}, u32[]{:S(2)}) collective-permute-start(f32[64,64]{1,0:T(8,128)S(1)} %add_add_fusion), channel_id=1, source_target_pairs={{0,96},{4,100},{8,104},{12,108},{16,112},{20,116},{24,120},{28,124... | collective-permute-start | bytes 49160 | tf_op jit(solution)/shard_map/ppermute | solution.py:323
  121.9 2.5 %collective-permute-start.14 = (f32[64,64]{1,0:T(8,128)S(1)}, f32[64,64]{1,0:T(8,128)S(1)}, u32[]{:S(2)}, u32[]{:S(2)}) collective-permute-start(f32[64,64]{1,0:T(8,128)S(1)} %add_add_fusion), channel_id=1, source_target_pairs={{0,64},{4,68},{8,72},{12,76},{16,80},{20,84},{24,88},{28,92},{32,9... | collective-permute-start | bytes 49160 | tf_op jit(solution)/shard_map/ppermute | solution.py:323
  124.4 2.6 %collective-permute-done.15 = f32[64,64]{1,0:T(8,128)S(1)} collective-permute-done((f32[64,64]{1,0:T(8,128)S(1)}, f32[64,64]{1,0:T(8,128)S(1)}, u32[]{:S(2)}, u32[]{:S(2)}) %collective-permute-start.15) | collective-permute-done | bytes 16416 | tf_op jit(solution)/shard_map/ppermute | solution.py:323
  127.1 0.3 collective-permute-done.14
  127.4 0.6 add_multiply_fusion
  (48 shorter events, 0.2 us)
Async XLA Ops:
  0.6 8.2 %copy-start.13 = (s32[2,8]{1,0:T(2,128)S(1)}, s32[2,8]{1,0:T(2,128)}, u32[]{:S(2)}) copy-start(s32[2,8]{1,0:T(2,128)} %param.8) | copy-start | bytes 196
  0.6 8.6 %copy-start.4 = (bf16[128,512]{1,0:T(8,128)(2,1)S(1)}, bf16[128,512]{1,0:T(8,128)(2,1)}, u32[]{:S(2)}) copy-start(bf16[128,512]{1,0:T(8,128)(2,1)} %param.7) | copy-start | bytes 393220
  6.0 28.3 %copy-start.3 = (bf16[128,384]{1,0:T(8,128)(2,1)S(1)}, bf16[128,384]{1,0:T(8,128)(2,1)}, u32[]{:S(2)}) copy-start(bf16[128,384]{1,0:T(8,128)(2,1)} %param.9) | copy-start | bytes 294916
  6.0 29.1 %collective-permute-start.4 = (bf16[128,32,512]{2,1,0:T(8,128)(2,1)}, bf16[128,32,512]{2,1,0:T(8,128)(2,1)}, u32[]{:S(2)}, u32[]{:S(2)}) collective-permute-start(bf16[128,32,512]{2,1,0:T(8,128)(2,1)} %slice_multiply_fusion), channel_id=1, source_target_pairs={{4,8},{8,4},{12,16},{16,12},{20,24},{24,20},{28,32},{32,28},{36,40... | collective-permute-start | bytes 12582920 | tf_op jit(solution)/shard_map/ppermute | solution.py:345
  9.3 12.7 %copy-start.5 = (bf16[128,512]{1,0:T(8,128)(2,1)}, bf16[128,512]{1,0:T(8,128)(2,1)S(1)}, u32[]{:S(2)}) copy-start(bf16[128,512]{1,0:T(8,128)(2,1)S(1)} %mul.22.refs_0_) | copy-start | bytes 393220
  9.3 8.4 %collective-permute-start.2 = (bf16[128,512]{1,0:T(8,128)(2,1)S(1)}, bf16[128,512]{1,0:T(8,128)(2,1)S(1)}, u32[]{:S(2)}, u32[]{:S(2)}) collective-permute-start(bf16[128,512]{1,0:T(8,128)(2,1)S(1)} %mul.22.refs_0_), channel_id=1, source_target_pairs={{3,0},{0,1},{1,2},{2,3},{7,4},{4,5},{5,6},{6,7},{11,8},{8,9},{9,10... | collective-permute-start | bytes 393224 | tf_op jit(solution)/shard_map/ppermute | solution.py:360
  11.4 10.6 %collective-permute-start.1 = (bf16[128,512]{1,0:T(8,128)(2,1)S(1)}, bf16[128,512]{1,0:T(8,128)(2,1)S(1)}, u32[]{:S(2)}, u32[]{:S(2)}) collective-permute-start(bf16[128,512]{1,0:T(8,128)(2,1)S(1)} %mul.22.refs_0_), channel_id=1, source_target_pairs={{2,0},{3,1},{0,2},{1,3},{6,4},{7,5},{4,6},{5,7},{10,8},{11,9},{8,1... | collective-permute-start | bytes 393224 | tf_op jit(solution)/shard_map/ppermute | solution.py:360
  15.0 7.0 %collective-permute-start = (bf16[128,512]{1,0:T(8,128)(2,1)S(1)}, bf16[128,512]{1,0:T(8,128)(2,1)S(1)}, u32[]{:S(2)}, u32[]{:S(2)}) collective-permute-start(bf16[128,512]{1,0:T(8,128)(2,1)S(1)} %mul.22.refs_0_), channel_id=1, source_target_pairs={{1,0},{2,1},{3,2},{0,3},{5,4},{6,5},{7,6},{4,7},{9,8},{10,9},{11,1... | collective-permute-start | bytes 393224 | tf_op jit(solution)/shard_map/ppermute | solution.py:360
  17.7 4.3 %copy-start.10 = (bf16[128,512]{1,0:T(8,128)(2,1)}, bf16[128,512]{1,0:T(8,128)(2,1)S(1)}, u32[]{:S(2)}) copy-start(bf16[128,512]{1,0:T(8,128)(2,1)S(1)} %collective-permute-done.2.refs_3_) | copy-start | bytes 393220
  22.0 0.7 copy-start.11
  22.7 0.6 copy-start.12
  34.2 13.6 %collective-permute-start.5 = (bf16[4,8,64,16,128]{4,3,2,1,0:T(8,128)(2,1)}, bf16[4,8,64,16,128]{4,3,2,1,0:T(8,128)(2,1)}, u32[]{:S(2)}, u32[]{:S(2)}) collective-permute-start(bf16[4,8,64,16,128]{4,3,2,1,0:T(8,128)(2,1)} %get-tuple-element.29.own.refs_5_.refs_4_), channel_id=1, source_target_pairs={{0,4},{4,0},{8,12},{12,8},{16,20},{20,16},{24,28},{28,24},{32,36},... | collective-permute-start | bytes 25165832 | tf_op jit(solution)/shard_map/ppermute | solution.py:372
  34.4 21.4 %collective-permute-start.3 = (bf16[8,32,16,128]{3,2,1,0:T(8,128)(2,1)}, bf16[8,32,16,128]{3,2,1,0:T(8,128)(2,1)S(1)}, u32[]{:S(2)}, u32[]{:S(2)}) collective-permute-start(bf16[8,32,16,128]{3,2,1,0:T(8,128)(2,1)} %get-tuple-element.27), channel_id=1, source_target_pairs={{4,8},{8,4},{12,16},{16,12},{20,24},{24,20},{28,32},{32,28},{36,40... | collective-permute-start | bytes 3145736 | tf_op jit(solution)/shard_map/ppermute | solution.py:345
  35.2 1.0 copy-start.2
  36.2 6.3 %copy-start.7 = (bf16[8,32,16,128]{3,2,1,0:T(8,128)(2,1)S(1)}, bf16[8,32,16,128]{3,2,1,0:T(8,128)(2,1)}, u32[]{:S(2)}) copy-start(bf16[8,32,16,128]{3,2,1,0:T(8,128)(2,1)} %get-tuple-element.34) | copy-start | bytes 3145732
  36.2 11.6 %copy-start = (bf16[4,8,64,16,128]{4,3,2,1,0:T(8,128)(2,1)S(1)}, bf16[4,8,64,16,128]{4,3,2,1,0:T(8,128)(2,1)}, u32[]{:S(2)}) copy-start(bf16[4,8,64,16,128]{4,3,2,1,0:T(8,128)(2,1)} %get-tuple-element.29.own.refs_5_.refs_4_) | copy-start | bytes 25165828
  42.5 13.3 %slice-start = ((s8[8388608]{0:T(1024)(128)(4,1)}), s8[4194304]{0:T(1024)(128)(4,1)S(1)}, s32[]{:S(2)}) async-start(s8[8388608]{0:T(1024)(128)(4,1)} %bitcast.8), calls=%async_computation | async-start | bytes 8388608
  42.6 11.8 %copy-start.6 = (bf16[8,32,16,128]{3,2,1,0:T(8,128)(2,1)S(1)}, bf16[8,32,16,128]{3,2,1,0:T(8,128)(2,1)}, u32[]{:S(2)}) copy-start(bf16[8,32,16,128]{3,2,1,0:T(8,128)(2,1)} %get-tuple-element.38) | copy-start | bytes 3145732
  42.6 12.5 %copy-start.9 = (bf16[8,16,16,128]{3,2,1,0:T(8,128)(2,1)S(1)}, bf16[8,16,16,128]{3,2,1,0:T(8,128)(2,1)}, u32[]{:S(2)}) copy-start(bf16[8,16,16,128]{3,2,1,0:T(8,128)(2,1)} %get-tuple-element.42) | copy-start | bytes 1572868
  42.6 13.2 %slice-start.1 = ((s8[8388608]{0:T(1024)(128)(4,1)}), s8[4194304]{0:T(1024)(128)(4,1)S(1)}, s32[]{:S(2)}) async-start(s8[8388608]{0:T(1024)(128)(4,1)} %bitcast.8), calls=%async_computation.1 | async-start | bytes 8388608
  42.6 13.2 %copy-start.1 = (f32[2,1,512]{2,1,0:T(1,128)S(1)}, f32[2,1,512]{2,1,0:T(1,128)}, u32[]{:S(2)}) copy-start(f32[2,1,512]{2,1,0:T(1,128)} %convert_element_type.36.mask_ref.refs_1_) | copy-start | bytes 12292
  42.6 18.2 %collective-permute-start.6 = (bf16[8,32,16,128]{3,2,1,0:T(8,128)(2,1)S(1)}, bf16[8,32,16,128]{3,2,1,0:T(8,128)(2,1)S(1)}, u32[]{:S(2)}, u32[]{:S(2)}) collective-permute-start(bf16[8,32,16,128]{3,2,1,0:T(8,128)(2,1)S(1)} %copy-done.7), channel_id=1, source_target_pairs={{4,8},{8,4},{12,16},{16,12},{20,24},{24,20},{28,32},{32,28},{36,40... | collective-permute-start | bytes 3145736 | tf_op jit(solution)/shard_map/ppermute | solution.py:345
  54.3 10.7 %collective-permute-start.7 = (bf16[8,32,16,128]{3,2,1,0:T(8,128)(2,1)S(1)}, bf16[8,32,16,128]{3,2,1,0:T(8,128)(2,1)S(1)}, u32[]{:S(2)}, u32[]{:S(2)}) collective-permute-start(bf16[8,32,16,128]{3,2,1,0:T(8,128)(2,1)S(1)} %copy-done.6), channel_id=1, source_target_pairs={{4,8},{8,4},{12,16},{16,12},{20,24},{24,20},{28,32},{32,28},{36,40... | collective-permute-start | bytes 3145736 | tf_op jit(solution)/shard_map/ppermute | solution.py:345
  55.1 14.2 %collective-permute-start.8 = (bf16[8,16,16,128]{3,2,1,0:T(8,128)(2,1)S(1)}, bf16[8,16,16,128]{3,2,1,0:T(8,128)(2,1)S(1)}, u32[]{:S(2)}, u32[]{:S(2)}) collective-permute-start(bf16[8,16,16,128]{3,2,1,0:T(8,128)(2,1)S(1)} %copy-done.9), channel_id=1, source_target_pairs={{4,8},{8,4},{12,16},{16,12},{20,24},{24,20},{28,32},{32,28},{36,40... | collective-permute-start | bytes 1572872 | tf_op jit(solution)/shard_map/ppermute | solution.py:345
  55.8 4.3 %copy-start.8 = (bf16[8,16,16,128]{3,2,1,0:T(8,128)(2,1)S(1)}, bf16[8,16,16,128]{3,2,1,0:T(8,128)(2,1)}, u32[]{:S(2)}) copy-start(bf16[8,16,16,128]{3,2,1,0:T(8,128)(2,1)} %get-tuple-element.46) | copy-start | bytes 1572868
  60.1 12.5 %collective-permute-start.9 = (bf16[8,16,16,128]{3,2,1,0:T(8,128)(2,1)S(1)}, bf16[8,16,16,128]{3,2,1,0:T(8,128)(2,1)S(1)}, u32[]{:S(2)}, u32[]{:S(2)}) collective-permute-start(bf16[8,16,16,128]{3,2,1,0:T(8,128)(2,1)S(1)} %copy-done.8), channel_id=1, source_target_pairs={{4,8},{8,4},{12,16},{16,12},{20,24},{24,20},{28,32},{32,28},{36,40... | collective-permute-start | bytes 1572872 | tf_op jit(solution)/shard_map/ppermute | solution.py:345
  75.8 31.0 %collective-permute-start.10 = (f32[64,64]{1,0:T(8,128)S(1)}, f32[64,64]{1,0:T(8,128)S(1)}, u32[]{:S(2)}, u32[]{:S(2)}) collective-permute-start(f32[64,64]{1,0:T(8,128)S(1)} %get-tuple-element.49), channel_id=1, source_target_pairs={{0,4},{4,0},{8,12},{12,8},{16,20},{20,16},{24,28},{28,24},{32,36},... | collective-permute-start | bytes 49160 | tf_op jit(solution)/shard_map/ppermute | solution.py:323
  106.8 8.4 %collective-permute-start.13 = (f32[64,64]{1,0:T(8,128)S(1)}, f32[64,64]{1,0:T(8,128)S(1)}, u32[]{:S(2)}, u32[]{:S(2)}) collective-permute-start(f32[64,64]{1,0:T(8,128)S(1)} %add.26), channel_id=1, source_target_pairs={{0,24},{4,28},{8,0},{12,4},{16,8},{20,12},{24,16},{28,20},{32,56},... | collective-permute-start | bytes 49160 | tf_op jit(solution)/shard_map/ppermute | solution.py:323
  113.6 5.5 %collective-permute-start.12 = (f32[64,64]{1,0:T(8,128)S(1)}, f32[64,64]{1,0:T(8,128)S(1)}, u32[]{:S(2)}, u32[]{:S(2)}) collective-permute-start(f32[64,64]{1,0:T(8,128)S(1)} %add.26), channel_id=1, source_target_pairs={{0,8},{4,12},{8,16},{12,20},{16,24},{20,28},{24,0},{28,4},{32,40},... | collective-permute-start | bytes 49160 | tf_op jit(solution)/shard_map/ppermute | solution.py:323
  113.6 5.5 %collective-permute-start.11 = (f32[64,64]{1,0:T(8,128)S(1)}, f32[64,64]{1,0:T(8,128)S(1)}, u32[]{:S(2)}, u32[]{:S(2)}) collective-permute-start(f32[64,64]{1,0:T(8,128)S(1)} %add.26), channel_id=1, source_target_pairs={{0,16},{4,20},{8,24},{12,28},{16,0},{20,4},{24,8},{28,12},{32,48},... | collective-permute-start | bytes 49160 | tf_op jit(solution)/shard_map/ppermute | solution.py:323
  119.1 5.3 %collective-permute-start.16 = (f32[64,64]{1,0:T(8,128)S(1)}, f32[64,64]{1,0:T(8,128)S(1)}, u32[]{:S(2)}, u32[]{:S(2)}) collective-permute-start(f32[64,64]{1,0:T(8,128)S(1)} %add_add_fusion), channel_id=1, source_target_pairs={{0,96},{4,100},{8,104},{12,108},{16,112},{20,116},{24,120},{28,124... | collective-permute-start | bytes 49160 | tf_op jit(solution)/shard_map/ppermute | solution.py:323
  121.9 5.1 %collective-permute-start.15 = (f32[64,64]{1,0:T(8,128)S(1)}, f32[64,64]{1,0:T(8,128)S(1)}, u32[]{:S(2)}, u32[]{:S(2)}) collective-permute-start(f32[64,64]{1,0:T(8,128)S(1)} %add_add_fusion), channel_id=1, source_target_pairs={{0,32},{4,36},{8,40},{12,44},{16,48},{20,52},{24,56},{28,60},{32,6... | collective-permute-start | bytes 49160 | tf_op jit(solution)/shard_map/ppermute | solution.py:323
  121.9 5.5 %collective-permute-start.14 = (f32[64,64]{1,0:T(8,128)S(1)}, f32[64,64]{1,0:T(8,128)S(1)}, u32[]{:S(2)}, u32[]{:S(2)}) collective-permute-start(f32[64,64]{1,0:T(8,128)S(1)} %add_add_fusion), channel_id=1, source_target_pairs={{0,64},{4,68},{8,72},{12,76},{16,80},{20,84},{24,88},{28,92},{32,9... | collective-permute-start | bytes 49160 | tf_op jit(solution)/shard_map/ppermute | solution.py:323

commit v5 on v0

v5 whole, which is shorter than its diff:
```python
import math

import jax
import jax.numpy as jnp
from jax import lax
from jax.experimental import pallas as pl
from jax.experimental.pallas import tpu as pltpu
from jax.sharding import PartitionSpec as P

BS = 64
SIG = 128
PB = 16
QB = 16
MIB = 2**20

RAW_MU = 32
RAW_STEP = 32
LOW = (0, 4, 0, 32)
RAW_HALVES = ((0, 2, 32, 32), (256, 2, 32, 32))
CHUNKS = ((0, 2, 0, 32), (256, 1, 0, 32), (384, 1, 0, 16), (384, 1, 16, 16))
PIECES = (LOW,) + RAW_HALVES + CHUNKS
HALF_MIB = 56
HALF_COST = 1
FIT_MIB = 40
RAW_MIB = 32
FIT_COST = 0.3
HBM = pl.BlockSpec(memory_space=pltpu.HBM)
WHOLE = pl.BlockSpec(memory_space=pltpu.VMEM)


def cost(us):
    return pl.CostEstimate(
        flops=int(us * 4e9), bytes_accessed=int(us * 12e6), transcendentals=0
    )


def params(mib):
    return pltpu.CompilerParams(vmem_limit_bytes=mib * MIB)


def half_rows(x, dens, scratch, cols):
    flat = jnp.dot(x.reshape(PB * cols, x.shape[2]), dens, preferred_element_type=jnp.float32)
    pitch = cols + 1
    for t in range(scratch.shape[0]):
        for p in range(PB):
            scratch[t, p * pitch:p * pitch + cols] = flat[
                p * cols:(p + 1) * cols, t * SIG:(t + 1) * SIG
            ]


def turned(scratch, t, m, cols):
    return scratch[t, pl.ds(m, PB, stride=cols + 1), :].astype(jnp.bfloat16)


def half_kernel(mask_ref, *refs):
    parts, tc_hbm = refs[:4], refs[4]
    dens_ref, outs = refs[5], refs[6:-5]
    tc_buf, staged, scratch, in_sem, out_sem = refs[-5:]
    rows, cols, width = tc_buf.shape
    blocks = rows // PB

    def fetch(b):
        rows_b = pl.ds(b * PB, PB)
        return pltpu.make_async_copy(tc_hbm.at[rows_b], tc_buf.at[rows_b], in_sem.at[b])

    for b in range(blocks):
        fetch(b).start()
    me = lax.axis_index("mu")
    depth = parts[0].shape[0]
    for k, part in enumerate(parts):
        at = lax.rem(me + k, len(parts)) * depth
        dens_ref[pl.ds(pl.multiple_of(at, depth), depth), :] = part[...]

    def step(b, carry):
        fetch(b).wait()
        x = tc_buf[pl.ds(b * PB, PB)] * mask_ref[(b * PB) // BS].astype(jnp.bfloat16)
        half_rows(x, dens_ref[...], scratch, cols)
        for t in range(width // SIG):
            for m in range(cols):
                staged[t, b, m] = turned(scratch, t, m, cols)
        for k, (s, tiles, mu0, count) in enumerate(PIECES):
            part = staged.at[pl.ds(s // SIG, tiles), b, pl.ds(mu0, count)]
            pltpu.make_async_copy(part, outs[k].at[:, b], out_sem.at[k]).start()
        return carry

    lax.fori_loop(0, blocks, step, 0)
    for k, (s, tiles, mu0, count) in enumerate(PIECES):
        part = staged.at[pl.ds(s // SIG, tiles), :, pl.ds(mu0, count)]
        pltpu.make_async_copy(part, outs[k], out_sem.at[k]).wait()


def half_call(tc, mask, parts):
    rows, cols, width = tc.shape
    whole = (width // SIG, rows // PB, cols, PB, SIG)
    shapes = [(width, width)] + [(t, rows // PB, n, PB, SIG) for _, t, _, n in PIECES]
    return pl.pallas_call(
        half_kernel,
        in_specs=[WHOLE] * (1 + len(parts)) + [HBM],
        out_specs=[WHOLE] + [HBM] * len(PIECES),
        out_shape=[jax.ShapeDtypeStruct(shape, jnp.bfloat16) for shape in shapes],
        scratch_shapes=[
            pltpu.VMEM(tc.shape, jnp.bfloat16),
            pltpu.VMEM(whole, jnp.bfloat16),
            pltpu.VMEM((width // SIG, PB * (cols + 1) + 8, SIG), jnp.float32),
            pltpu.SemaphoreType.DMA((rows // PB,)),
            pltpu.SemaphoreType.DMA((len(PIECES),)),
        ],
        compiler_params=params(HALF_MIB),
        cost_estimate=cost(HALF_COST),
    )(mask, *parts, tc)


def raw_kernel_send(mask_ref, tc, out, bufs, in_sem, out_sem):
    rows, count, width = bufs.shape
    step = rows // in_sem.shape[0]

    def fetch(b):
        part = pl.ds(b * step, step)
        source = tc.at[part, pl.ds(RAW_MU, RAW_STEP)]
        return pltpu.make_async_copy(source, bufs.at[part], in_sem.at[b])

    def put(b):
        part = pl.ds(b * step, step)
        return pltpu.make_async_copy(bufs.at[part], out.at[part], out_sem.at[b])

    pieces = rows // step
    for b in range(pieces):
        fetch(b).start()
    block = lax.broadcasted_iota(jnp.int32, (1, width), 1) // BS
    masks = []
    for p in range(mask_ref.shape[0]):
        lanes = jnp.zeros((1, width), jnp.float32)
        for k in range(mask_ref.shape[2]):
            lanes = jnp.where(block == k, mask_ref[p, 0, k].astype(jnp.float32), lanes)
        masks.append(lanes.astype(jnp.bfloat16))
    for b in range(pieces):
        fetch(b).wait()
        mask = masks[(b * step) // BS]

        def scale(i, carry, mask=mask, b=b):
            row = b * step + i
            bufs[row] = bufs[row] * mask
            return carry

        lax.fori_loop(0, step, scale, 0, unroll=4)
        put(b).start()
    for b in range(pieces):
        put(b).wait()


def raw_slice(tc, center_mask):
    rows, _, width = tc.shape
    pieces = 8
    return pl.pallas_call(
        raw_kernel_send,
        in_specs=[pl.BlockSpec(memory_space=pltpu.SMEM), HBM],
        out_specs=HBM,
        out_shape=jax.ShapeDtypeStruct((rows, RAW_STEP, width), tc.dtype),
        scratch_shapes=[
            pltpu.VMEM((rows, RAW_STEP, width), tc.dtype),
            pltpu.SemaphoreType.DMA((pieces,)),
            pltpu.SemaphoreType.DMA((pieces,)),
        ],
        compiler_params=params(HALF_MIB),
        cost_estimate=cost(FIT_COST),
    )(center_mask, tc)


def fit_tile(pieces, metric_ref, scratch, pitch, count):
    metric = metric_ref[...]
    rows = metric.shape[0]

    def fit(pair, carry):
        columns = [jnp.concatenate(pieces(m), axis=0) for m in (2 * pair, 2 * pair + 1)]
        y = jnp.dot(metric, jnp.concatenate(columns, axis=1), preferred_element_type=jnp.float32)
        scratch[pl.ds(2 * pair, rows, stride=pitch), :] = y[:, :SIG]
        scratch[pl.ds(2 * pair + 1, rows, stride=pitch), :] = y[:, SIG:]
        return carry

    lax.fori_loop(0, count // 2, fit, 0, unroll=8)


def raw_kernel(metric_ref, dens_ref, raw, *refs):
    own, near, refs = refs[:2], refs[2:4], refs[4:]
    fitted, zero_ref, raw_buf, far_buf, own_buf, near_buf, staged, half_scratch, scratch = refs[:9]
    raw_sem, in_sem, out_sem = refs[9:]
    tiles, rows, count, _ = staged.shape
    pitch = count + 1
    blocks = rows // PB

    def fetch_raw(b):
        part = pl.ds(b * PB, PB)
        return pltpu.make_async_copy(raw.at[part], raw_buf.at[part], raw_sem.at[b])

    def fetch(t):
        k, at = t // 2, t % 2
        return [
            pltpu.make_async_copy(own[k].at[at], own_buf.at[t], in_sem.at[0, t]),
            pltpu.make_async_copy(near[k].at[at], near_buf.at[t], in_sem.at[1, t]),
        ]

    def put(t):
        lanes = pl.ds(t * SIG, SIG)
        return pltpu.make_async_copy(
            staged.at[t], fitted.at[:, pl.ds(RAW_MU, count), lanes], out_sem.at[t]
        )

    for b in range(blocks):
        fetch_raw(b).start()
    for t in range(tiles):
        for copy in fetch(t):
            copy.start()
    zero_ref[...] = jnp.zeros(zero_ref.shape, jnp.float32)

    def step(b, carry):
        fetch_raw(b).wait()
        half_rows(raw_buf[pl.ds(b * PB, PB)], dens_ref[...], half_scratch, count)
        for t in range(tiles):
            for m in range(count):
                far_buf[t, b, m] = turned(half_scratch, t, m, count)
        return carry

    lax.fori_loop(0, blocks, step, 0)
    for t in range(tiles):
        for copy in fetch(t):
            copy.wait()

        def pieces(m, t=t):
            return [buf[t, :, m].reshape(rows, SIG) for buf in (far_buf, own_buf, near_buf)]

        fit_tile(pieces, metric_ref, scratch, pitch, count)

        def store(block, inner, t=t):
            for q in range(QB):
                row = block * QB + q
                staged[t, row] = scratch[pl.ds(row * pitch, count), :].astype(jnp.bfloat16)
            return inner

        lax.fori_loop(0, rows // QB, store, 0)
        put(t).start()
    for t in range(tiles):
        put(t).wait()


def raw_call(raw_far, own, near, dens, metric, tc, cols):
    rows, count, width = raw_far.shape
    tiles = width // SIG
    buf = pltpu.VMEM((tiles, rows // PB, count, PB, SIG), jnp.bfloat16)
    return pl.pallas_call(
        raw_kernel,
        in_specs=[WHOLE, WHOLE] + [HBM] * 5,
        out_specs=[HBM, WHOLE],
        out_shape=[
            jax.ShapeDtypeStruct(tc.shape, jnp.bfloat16),
            jax.ShapeDtypeStruct((cols, cols), jnp.float32),
        ],
        scratch_shapes=[
            pltpu.VMEM(raw_far.shape, jnp.bfloat16),
            buf,
            buf,
            buf,
            pltpu.VMEM((tiles, rows, count, SIG), jnp.bfloat16),
            pltpu.VMEM((tiles, PB * (count + 1) + 8, SIG), jnp.float32),
            pltpu.VMEM((rows * (count + 1), SIG), jnp.float32),
            pltpu.SemaphoreType.DMA((rows // PB,)),
            pltpu.SemaphoreType.DMA((2, tiles)),
            pltpu.SemaphoreType.DMA((tiles,)),
        ],
        compiler_params=params(RAW_MIB),
        cost_estimate=cost(FIT_COST),
    )(metric, dens, raw_far, *own, *near)


def fit_kernel(chunk, raws, role, metric_ref, mask_ref, acc_ref, far, *refs):
    s, tiles, mu0, count = chunk
    (own, near, tc, _, fitted, exch_ref), refs = refs[:6], refs[6:]
    if role == "second":
        own_buf, near_buf, tc_buf = own, near, tc
        base = mu0
        far_buf, raw_buf, staged, scratch, out_sem, in_sem = refs
    else:
        own_buf, near_buf, tc_buf, far_buf, raw_buf, staged, scratch, out_sem, in_sem = refs
        base = 0
    rows = metric_ref.shape[0]
    pitch = count + 1
    wide = own_buf.shape[2]

    def fetch(t):
        part = pl.ds(mu0, wide)
        lanes = pl.ds(s + t * SIG, SIG)
        tile = s // SIG + t
        copies = [pltpu.make_async_copy(far.at[t], far_buf.at[t], in_sem.at[0, t])]
        if raws:
            source = fitted.at[:, pl.ds(RAW_MU, RAW_STEP), lanes]
            copies.append(pltpu.make_async_copy(source, raw_buf.at[t], in_sem.at[4, t]))
        if role == "second":
            return copies
        return copies + [
            pltpu.make_async_copy(own.at[tile, :, part], own_buf.at[t], in_sem.at[1, t]),
            pltpu.make_async_copy(near.at[tile, :, part], near_buf.at[t], in_sem.at[2, t]),
            pltpu.make_async_copy(tc.at[:, :, lanes], tc_buf.at[t], in_sem.at[3, t]),
        ]

    def put(t):
        lanes = pl.ds(s + t * SIG, SIG)
        return pltpu.make_async_copy(
            staged.at[t], fitted.at[:, pl.ds(mu0, count), lanes], out_sem.at[t]
        )

    for t in range(tiles):
        for copy in fetch(t):
            copy.start()
    exch_ref[...] = acc_ref[...]
    for t in range(tiles):
        for copy in fetch(t):
            copy.wait()

        def pieces(m, t=t):
            bufs = (far_buf[t, :, m], own_buf[t, :, base + m], near_buf[t, :, base + m])
            return [piece.reshape(rows, SIG) for piece in bufs]

        fit_tile(pieces, metric_ref, scratch, pitch, count)
        def contract(block, total, t=t):
            first = pl.multiple_of(block * QB, QB)
            lanes = slice(s + t * SIG, s + (t + 1) * SIG)
            mask = mask_ref[(block * QB) // BS, :, lanes].astype(jnp.bfloat16)
            left = []
            for q in range(QB):
                f = scratch[pl.ds((first + q) * pitch, count), :].astype(jnp.bfloat16)
                staged[t, first + q] = f
                if raws:
                    f = jnp.concatenate([f, raw_buf[t, first + q]], axis=0)
                left.append(f * mask)
            right = [tc_buf[t, first + q] for q in range(QB)]
            return total + lax.dot_general(
                jnp.concatenate(left, axis=1),
                jnp.concatenate(right, axis=1),
                (((1,), (1,)), ((), ())),
                preferred_element_type=jnp.float32,
            )

        lines = count + raws * RAW_STEP
        total = lax.fori_loop(
            0, rows // QB, contract, jnp.zeros((lines, acc_ref.shape[1]), jnp.float32), unroll=2
        )
        put(t).start()
        exch_ref[mu0:mu0 + count, :] += total[:count]
        if raws:
            exch_ref[RAW_MU:, :] += total[count:]
    for t in range(tiles):
        put(t).wait()


def fit_call(chunk, role, far, own, near, metric, tc, mask, acc, fitted):
    _, tiles, _, count = chunk
    rows, cols = metric.shape[0], acc.shape[1]
    raws = 0 if role == "second" else 1
    args = [metric, mask, acc, far, own, near, tc, fitted]
    operand = WHOLE if role == "second" else HBM
    wide = 2 * count if role == "first" else count
    fetched = [
        (tiles, rows // PB, wide, PB, SIG),
        (tiles, rows // PB, wide, PB, SIG),
        (tiles, rows, cols, SIG),
    ]
    handed = fetched if role == "first" else []
    kept = fetched if role == "" else []
    return pl.pallas_call(
        lambda *refs: fit_kernel(chunk, raws, role, *refs),
        in_specs=[WHOLE] * 3 + [HBM] + [operand] * 3 + [HBM],
        out_specs=[HBM, WHOLE] + [WHOLE] * len(handed),
        out_shape=[
            jax.ShapeDtypeStruct(fitted.shape, jnp.bfloat16),
            jax.ShapeDtypeStruct(acc.shape, jnp.float32),
        ] + [jax.ShapeDtypeStruct(shape, jnp.bfloat16) for shape in handed],
        scratch_shapes=[pltpu.VMEM(shape, jnp.bfloat16) for shape in kept] + [
            pltpu.VMEM(far.shape, jnp.bfloat16),
            pltpu.VMEM((tiles, rows, RAW_STEP if raws else 16, SIG), jnp.bfloat16),
            pltpu.VMEM((tiles, rows, count, SIG), jnp.bfloat16),
            pltpu.VMEM((rows * (count + 1), SIG), jnp.float32),
            pltpu.SemaphoreType.DMA((tiles,)),
            pltpu.SemaphoreType.DMA((5, tiles)),
        ],
        input_output_aliases={len(args) - 1: 0},
        compiler_params=params(FIT_MIB),
        cost_estimate=cost(FIT_COST),
    )(*args)


def sum_pa(value):
    size = lax.axis_size("pa")

    for stride, mask in ((1, 1), (2, 1), (2, 3), (8, 1), (8, 3)):
        pairs = [(i, i ^ (mask * stride)) for i in range(size)]
        value = value + lax.ppermute(value, "pa", pairs)
    return value


def after(value, *earlier):
    return lax.optimization_barrier((value,) + earlier)[0]


def on_device(three_center, center_mask, density, density_mask, metric_band):
    rows, cols, width = three_center.shape
    size = lax.axis_size("pa")
    near_pairs = [(i, i ^ 1) for i in range(size)]
    far_pairs = [(i, i + 1 if i % 2 else i - 1) for i in range(1, size - 1)]

    def to_far(value, *earlier):
        return lax.ppermute(after(value, *earlier), "pa", far_pairs)

    raw = raw_slice(three_center, center_mask)
    raw_far = to_far(raw)
    mask = jnp.repeat(center_mask, BS, axis=2).astype(jnp.float32)
    block_mask = jnp.repeat(jnp.repeat(density_mask, BS, axis=0), BS, axis=1)
    local = after(density * block_mask.astype(jnp.bfloat16), raw)
    count = lax.axis_size("mu")
    parts = [local] + [
        lax.ppermute(local, "mu", [((i + k) % count, i) for i in range(count)])
        for k in range(1, count)
    ]
    left, middle, right = jnp.split(metric_band, 3, axis=1)
    metric = jnp.where(
        lax.axis_index("pa") % 2 == 0,
        metric_band,
        jnp.concatenate([right, middle, left], axis=1),
    )

    def to_near(value):
        return lax.ppermute(value, "pa", near_pairs)

    dens, low, *rest = half_call(three_center, mask, parts)
    own_raw, chunks = rest[:2], rest[2:]
    far = [to_far(chunks[0])]
    near_raw = [to_near(piece) for piece in own_raw]
    near_low = to_near(low)
    fitted, acc = raw_call(raw_far, own_raw, near_raw, dens, metric, three_center, cols)
    far += [to_far(chunks[1], acc), to_far(chunks[2], acc)]
    handed = (low, near_low, three_center)
    for c, chunk in enumerate(CHUNKS):
        role = {len(CHUNKS) - 2: "first", len(CHUNKS) - 1: "second"}.get(c, "")
        fitted, acc, *rest = fit_call(
            chunk, role, far[c], *handed[:2], metric, handed[2], mask, acc, fitted
        )
        handed = tuple(rest) or handed
        if len(far) < len(CHUNKS):
            far.append(to_far(chunks[len(far)], acc))
    scale = 1.0 / math.sqrt(rows * size * width)
    return (fitted, sum_pa(acc) * scale)


def solution(mesh):
    placed = (P("pa", "mu", None), P("pa", "mu", None), P("mu", None), P("mu", None), P("pa", None))
    return jax.shard_map(
        on_device,
        mesh=mesh,
        in_specs=placed,
        out_specs=(P("pa", "mu", None), P("mu", None)),
        check_vma=False,
    )
```

time: 340 us -> 125 us (0.37)
  blocking collectives: 214 us -> 0 us
  local copies, waits for them, and re-layouts: 80.8 us -> 6.73 us
  Pallas kernels: 0 us -> 45.2 us
  starting transfers between devices: 5.78 us -> 44.7 us
  matrix products: 30.2 us -> 0 us
  waiting for transfers between devices: 0.01 us -> 25.8 us
  other arithmetic: 7.73 us -> 0.71 us
    psum x1 -> x0, blocking collectives: 199 us -> none  [on_device(): total = lax.psum(partial_block, 'pa')]
    pallas_call x0 -> x7, Pallas kernels: none -> 45.2 us  [the longest x4 19.4 us: fit_call(): pl.pallas_call(lambda *refs: fit_kernel(chunk, raws, role, *refs), in_spe...]
    ppermute x2 -> x16, starting transfers between devices: 5.78 us -> 44.7 us  [the longest x5 31.9 us: sum_pa(): value = value + lax.ppermute(value, 'pa', pairs)]
    unnamed x10 -> x32, local copies, waits for them, and re-layouts: 37.9 us -> 5.57 us
    dot_general x3 -> x0, matrix products: 30.2 us -> none  [the longest x1 15.4 us: on_device(): jnp.dot(metric_band, wide_half.reshape(3 * rows, cols * width), preferred...]
    mul x6 -> x0, local copies, waits for them, and re-layouts: 29.4 us -> none  [the longest x4 29.1 us: on_device(): blocks * center_mask.astype(jnp.bfloat16)[:, None, :, None, :, None]]
    ppermute x2 -> x16, waiting for transfers between devices: 0.01 us -> 25.8 us  [the longest x3 12 us: to_near(): return lax.ppermute(value, 'pa', near_pairs)]
    all_gather x1 -> x0, blocking collectives: 14.1 us -> none  [on_device(): dens = lax.all_gather(local_dens, 'mu', axis=0, tiled=True)]
  transfers between devices with their start and end apart: 2 -> 16, of which waited for: 0 -> 9; matrix products, arithmetic and copies ran while one was open for 8% -> 1% of each run, Pallas kernels for 0% -> 31%
where the time goes in v5:
time: 125 us; the launch traced here: 124 us
  Pallas kernels  45.2 us (36%)
  starting transfers between devices  44.7 us (36%)
  waiting for transfers between devices  25.8 us (21%)
  local copies, waits for them, and re-layouts  6.73 us (5%)
    ppermute x5, starting transfers between devices, sum_pa(): value = value + lax.ppermute(value, 'pa', pairs)  31.9 us
    pallas_call x4, Pallas kernels, fit_call(): pl.pallas_call(lambda *refs: fit_kernel(chunk, raws, role, *refs), in_spe...  19.4 us
    ppermute x3, waiting for transfers between devices, to_near(): return lax.ppermute(value, 'pa', near_pairs)  12 us
    pallas_call x1, Pallas kernels, half_call(): pl.pallas_call(half_kernel, in_specs=[WHOLE] * (1 + len(parts)) + [HBM],...  11 us
    pallas_call x1, Pallas kernels, raw_call(): pl.pallas_call(raw_kernel, in_specs=[WHOLE, WHOLE] + [HBM] * 5, out_specs...  10.5 us
    ppermute x5, waiting for transfers between devices, sum_pa(): value = value + lax.ppermute(value, 'pa', pairs)  8.49 us
    ppermute x3, starting transfers between devices, on_device(): lax.ppermute(local, 'mu', [((i + k) % count, i) for i in range(count)])  6.66 us
    unnamed x32, local copies, waits for them, and re-layouts  5.57 us
  transfers between devices with their start and end apart: 16, of which 9 were waited for; matrix products, arithmetic and copies ran while one was open for 1% of the time, Pallas kernels for 31%

profile of v5, /device:TPU:0, one launch (start us, length us, event | category | flops | bytes accessed | tf_op | source)
XLA Modules:
  0.0 124.2 jit_solution(10388749280245692479)
XLA Ops:
  0.7 4.3 %shard_map.68 = bf16[128,32,512]{2,1,0:T(8,128)(2,1)} custom-call(s32[2,1,8]{2,1,0:T(1,128)} %mask_ref.1, bf16[128,64,512]{2,1,0:T(8,128)(2,1)} %refs_6_.5), custom_call_target="tpu_custom_call" | custom-call | flops 1200000000 | bytes 3600000 | tf_op jit(solution)/shard_map/pallas_call | solution.py:154
  5.0 2.6 %collective-permute-start.3 = (bf16[128,32,512]{2,1,0:T(8,128)(2,1)}, bf16[128,32,512]{2,1,0:T(8,128)(2,1)}, u32[]{:S(2)}, u32[]{:S(2)}) collective-permute-start(bf16[128,32,512]{2,1,0:T(8,128)(2,1)} %shard_map.68), channel_id=1, source_target_pairs={{4,8},{8,4},{12,16},{16,12},{20,24},{24,20},{28,32},{32,28},{36,40... | collective-permute-start | bytes 12582920 | tf_op jit(solution)/shard_map/ppermute | solution.py:410
  7.7 0.1 copy.11
  7.8 0.1 broadcast_in_dim.10
  7.8 0.1 convert_element_type.22
  8.0 0.1 copy.12
  8.1 2.1 %collective-permute-start.2 = (bf16[128,512]{1,0:T(8,128)(2,1)S(1)}, bf16[128,512]{1,0:T(8,128)(2,1)S(1)}, u32[]{:S(2)}, u32[]{:S(2)}) collective-permute-start(bf16[128,512]{1,0:T(8,128)(2,1)S(1)} %mul.9.refs_0_), channel_id=1, source_target_pairs={{3,0},{0,1},{1,2},{2,3},{7,4},{4,5},{5,6},{6,7},{11,8},{8,9},{9,10... | collective-permute-start | bytes 393224 | tf_op jit(solution)/shard_map/ppermute | solution.py:419
  10.2 3.6 %collective-permute-start.1 = (bf16[128,512]{1,0:T(8,128)(2,1)S(1)}, bf16[128,512]{1,0:T(8,128)(2,1)S(1)}, u32[]{:S(2)}, u32[]{:S(2)}) collective-permute-start(bf16[128,512]{1,0:T(8,128)(2,1)S(1)} %mul.9.refs_0_), channel_id=1, source_target_pairs={{2,0},{3,1},{0,2},{1,3},{6,4},{7,5},{4,6},{5,7},{10,8},{11,9},{8,1... | collective-permute-start | bytes 393224 | tf_op jit(solution)/shard_map/ppermute | solution.py:419
  13.8 1.0 collective-permute-start
  14.8 0.1 broadcast_in_dim.9
  14.9 0.7 convert_element_type.20.mask_ref.refs_1_
  15.6 0.9 collective-permute-done.2.refs_3_
  16.5 4.4 %collective-permute-done.1.refs_2_ = bf16[128,512]{1,0:T(8,128)(2,1)S(1)} collective-permute-done((bf16[128,512]{1,0:T(8,128)(2,1)S(1)}, bf16[128,512]{1,0:T(8,128)(2,1)S(1)}, u32[]{:S(2)}, u32[]{:S(2)}) %collective-permute-start.1) | collective-permute-done | bytes 131104 | tf_op jit(solution)/shard_map/ppermute | solution.py:419
  20.9 0.0 collective-permute-done.refs_1_
  20.9 0.6 copy-done.13
  21.5 0.7 copy-done.14
  22.2 11.0 %shard_map.69 = (bf16[512,512]{1,0:T(8,128)(2,1)}, bf16[4,8,32,16,128]{4,3,2,1,0:T(8,128)(2,1)}, bf16[2,8,32,16,128]{4,3,2,1,0:T(8,128)(2,1)}, bf16[2,8,32,16,12...) custom-call(f32[2,1,512]{2,1,0:T(1,128)} %convert_element_type.20.ma, ...), custom_call_target="tpu_custom_call" | custom-call | flops 4000000000 | bytes 12000000 | tf_op jit(solution)/shard_map/pallas_call | solution.py:96
  33.2 0.1 collective-permute-start.7
  33.3 0.5 collective-permute-start.4
  33.8 0.1 collective-permute-start.5
  33.9 0.8 collective-permute-start.6
  34.8 9.0 %collective-permute-done.4.refs_2_ = bf16[2,8,32,16,128]{4,3,2,1,0:T(8,128)(2,1)} collective-permute-done((bf16[2,8,32,16,128]{4,3,2,1,0:T(8,128)(2,1)}, bf16[2,8,32,16,128]{4,3,2,1,0:T(8,128)(2,1)}, u32[]{:S(2)}, u32[]{:S(2)}) %collective-permute-start.4) | collective-permute-done | bytes 2097184 | tf_op jit(solution)/shard_map/ppermute | solution.py:430
  43.8 3.0 %collective-permute-done.5.refs_3_ = bf16[2,8,32,16,128]{4,3,2,1,0:T(8,128)(2,1)} collective-permute-done((bf16[2,8,32,16,128]{4,3,2,1,0:T(8,128)(2,1)}, bf16[2,8,32,16,128]{4,3,2,1,0:T(8,128)(2,1)}, u32[]{:S(2)}, u32[]{:S(2)}) %collective-permute-start.5) | collective-permute-done | bytes 2097184 | tf_op jit(solution)/shard_map/ppermute | solution.py:430
  46.8 1.6 %copy-done.1 = bf16[2,8,32,16,128]{4,3,2,1,0:T(8,128)(2,1)S(1)} copy-done((bf16[2,8,32,16,128]{4,3,2,1,0:T(8,128)(2,1)S(1)}, bf16[2,8,32,16,128]{4,3,2,1,0:T(8,128)(2,1)}, u32[]{:S(2)}) %copy-start.1) | copy-done | bytes 2097176
  48.4 1.6 %copy-done.2 = bf16[2,8,32,16,128]{4,3,2,1,0:T(8,128)(2,1)S(1)} copy-done((bf16[2,8,32,16,128]{4,3,2,1,0:T(8,128)(2,1)S(1)}, bf16[2,8,32,16,128]{4,3,2,1,0:T(8,128)(2,1)}, u32[]{:S(2)}) %copy-start.2) | copy-done | bytes 2097176
  50.0 1.0 copy-done.3
  51.0 10.5 %shard_map.70 = (bf16[128,64,512]{2,1,0:T(8,128)(2,1)}, f32[64,64]{1,0:T(8,128)S(1)}) custom-call(bf16[128,384]{1,0:T(8,128)(2,1)S(1)} %maximum_select_fusion.metric_ref.refs_0_, bf16[512,512]{1,0:T(8,128)(2,1)S(1)} %copy-done.3, bf16[128,32,512]{2,1,0:T(8,128)(2,1)} %collective-permute-done.3.raw, bf16[2,8,32,16,128]{4,3,2,1,0:T(8,128)(2,1)S(1)} %copy-done.1, ...), custom_call_target="tpu_custom_call" | custom-call | flops 1200000000 | bytes 3600000 | tf_op jit(solution)/shard_map/pallas_call | solution.py:249
  61.5 0.7 collective-permute-start.8
  62.3 0.7 collective-permute-start.9
  63.0 0.0 collective-permute-done.7.refs_5_
  63.0 7.4 %shard_map.71 = (bf16[128,64,512]{2,1,0:T(8,128)(2,1)}, f32[64,64]{1,0:T(8,128)S(1)}) custom-call(bf16[128,384]{1,0:T(8,128)(2,1)S(1)} %maximum_select_fusion.metric_ref.refs_0_, f32[2,1,512]{2,1,0:T(1,128)S(1)} %copy-done.4, f32[64,64]{1,0:T(8,128)S(1)} %get-tuple-element.31.refs_2_, ...), custom_call_target="tpu_custom_call", output_to_operand_aliasing={{0}: (7, {})} | custom-call | flops 1200000000 | bytes 3600000 | tf_op jit(solution)/shard_map/pallas_call | solution.py:368
  70.4 0.7 collective-permute-start.10
  71.1 0.0 collective-permute-done.8.refs_3_
  71.1 5.2 %shard_map.72 = (bf16[128,64,512]{2,1,0:T(8,128)(2,1)}, f32[64,64]{1,0:T(8,128)S(1)}) custom-call(bf16[128,384]{1,0:T(8,128)(2,1)S(1)} %maximum_select_fusion.metric_ref.refs_0_, f32[2,1,512]{2,1,0:T(1,128)S(1)} %copy-done.4, f32[64,64]{1,0:T(8,128)S(1)} %get-tuple-element.35.refs_2_, ...), custom_call_target="tpu_custom_call", output_to_operand_aliasing={{0}: (7, {})} | custom-call | flops 1200000000 | bytes 3600000 | tf_op jit(solution)/shard_map/pallas_call | solution.py:368
  76.4 4.6 %shard_map.73 = (bf16[128,64,512]{2,1,0:T(8,128)(2,1)}, f32[64,64]{1,0:T(8,128)S(1)}, bf16[1,8,32,16,128]{4,3,2,1,0:T(8,128)(2,1)S(1)}, bf16[1,8,32,16,128]{4,3,...) custom-call(bf16[128,384]{1,0:T(8,128)(2,1)S(1)} %maximum_select_fusion.metric_ref.refs_0_, ...), custom_call_target="tpu_custom_call", output_to_operand_aliasing={{0}: (7, {})} | custom-call | flops 1200000000 | bytes 3600000 | tf_op jit(solution)/shard_map/pallas_call | solution.py:368
  81.0 0.0 collective-permute-done.10.refs_3_
  81.0 2.2 %shard_map.74 = (bf16[128,64,512]{2,1,0:T(8,128)(2,1)}, f32[64,64]{1,0:T(8,128)S(1)}) custom-call(bf16[128,384]{1,0:T(8,128)(2,1)S(1)} %maximum_select_fusion.metric_ref.refs_0_, f32[2,1,512]{2,1,0:T(1,128)S(1)} %copy-done.4, f32[64,64]{1,0:T(8,128)S(1)} %get-tuple-element.43.refs_2_, ...), custom_call_target="tpu_custom_call", output_to_operand_aliasing={{0}: (7, {})} | custom-call | flops 1200000000 | bytes 3600000 | tf_op jit(solution)/shard_map/pallas_call | solution.py:368
  83.2 19.1 %collective-permute-start.11 = (f32[64,64]{1,0:T(8,128)S(1)}, f32[64,64]{1,0:T(8,128)S(1)}, u32[]{:S(2)}, u32[]{:S(2)}) collective-permute-start(f32[64,64]{1,0:T(8,128)S(1)} %get-tuple-element.51), channel_id=1, source_target_pairs={{0,4},{4,0},{8,12},{12,8},{16,20},{20,16},{24,28},{28,24},{32,36},... | collective-permute-start | bytes 49160 | tf_op jit(solution)/shard_map/ppermute | solution.py:395
  102.2 0.9 collective-permute-done.11
  103.1 2.0 %collective-permute-start.12 = (f32[64,64]{1,0:T(8,128)S(1)}, f32[64,64]{1,0:T(8,128)S(1)}, u32[]{:S(2)}, u32[]{:S(2)}) collective-permute-start(f32[64,64]{1,0:T(8,128)S(1)} %add.20), channel_id=1, source_target_pairs={{0,8},{4,12},{8,0},{12,4},{16,24},{20,28},{24,16},{28,20},{32,40},... | collective-permute-start | bytes 49160 | tf_op jit(solution)/shard_map/ppermute | solution.py:395
  105.1 2.0 %collective-permute-done.12 = f32[64,64]{1,0:T(8,128)S(1)} collective-permute-done((f32[64,64]{1,0:T(8,128)S(1)}, f32[64,64]{1,0:T(8,128)S(1)}, u32[]{:S(2)}, u32[]{:S(2)}) %collective-permute-start.12) | collective-permute-done | bytes 16416 | tf_op jit(solution)/shard_map/ppermute | solution.py:395
  107.0 4.8 %collective-permute-start.13 = (f32[64,64]{1,0:T(8,128)S(1)}, f32[64,64]{1,0:T(8,128)S(1)}, u32[]{:S(2)}, u32[]{:S(2)}) collective-permute-start(f32[64,64]{1,0:T(8,128)S(1)} %add.21), channel_id=1, source_target_pairs={{0,24},{4,28},{8,16},{12,20},{16,8},{20,12},{24,0},{28,4},{32,56},... | collective-permute-start | bytes 49160 | tf_op jit(solution)/shard_map/ppermute | solution.py:395
  111.8 1.9 %collective-permute-done.13 = f32[64,64]{1,0:T(8,128)S(1)} collective-permute-done((f32[64,64]{1,0:T(8,128)S(1)}, f32[64,64]{1,0:T(8,128)S(1)}, u32[]{:S(2)}, u32[]{:S(2)}) %collective-permute-start.13) | collective-permute-done | bytes 16416 | tf_op jit(solution)/shard_map/ppermute | solution.py:395
  113.7 2.6 %collective-permute-start.14 = (f32[64,64]{1,0:T(8,128)S(1)}, f32[64,64]{1,0:T(8,128)S(1)}, u32[]{:S(2)}, u32[]{:S(2)}) collective-permute-start(f32[64,64]{1,0:T(8,128)S(1)} %add.22), channel_id=1, source_target_pairs={{0,32},{4,36},{8,40},{12,44},{16,48},{20,52},{24,56},{28,60},{32,0... | collective-permute-start | bytes 49160 | tf_op jit(solution)/shard_map/ppermute | solution.py:395
  116.3 1.9 %collective-permute-done.14 = f32[64,64]{1,0:T(8,128)S(1)} collective-permute-done((f32[64,64]{1,0:T(8,128)S(1)}, f32[64,64]{1,0:T(8,128)S(1)}, u32[]{:S(2)}, u32[]{:S(2)}) %collective-permute-start.14) | collective-permute-done | bytes 16416 | tf_op jit(solution)/shard_map/ppermute | solution.py:395
  118.2 3.5 %collective-permute-start.15 = (f32[64,64]{1,0:T(8,128)S(1)}, f32[64,64]{1,0:T(8,128)S(1)}, u32[]{:S(2)}, u32[]{:S(2)}) collective-permute-start(f32[64,64]{1,0:T(8,128)S(1)} %add.23), channel_id=1, source_target_pairs={{0,96},{4,100},{8,104},{12,108},{16,112},{20,116},{24,120},{28,124... | collective-permute-start | bytes 49160 | tf_op jit(solution)/shard_map/ppermute | solution.py:395
  121.7 1.9 %collective-permute-done.15 = f32[64,64]{1,0:T(8,128)S(1)} collective-permute-done((f32[64,64]{1,0:T(8,128)S(1)}, f32[64,64]{1,0:T(8,128)S(1)}, u32[]{:S(2)}, u32[]{:S(2)}) %collective-permute-start.15) | collective-permute-done | bytes 16416 | tf_op jit(solution)/shard_map/ppermute | solution.py:395
  123.6 0.6 add_multiply_fusion
  (40 shorter events, 0.2 us)
Async XLA Ops:
  0.6 14.2 %copy-start.8 = (s32[2,1,8]{2,1,0:T(1,128)S(1)}, s32[2,1,8]{2,1,0:T(1,128)}, u32[]{:S(2)}) copy-start(s32[2,1,8]{2,1,0:T(1,128)} %mask_ref.1) | copy-start | bytes 196
  0.6 7.0 %copy-start.15 = (s32[2,8]{1,0:T(2,128)S(1)}, s32[2,8]{1,0:T(2,128)}, u32[]{:S(2)}) copy-start(s32[2,8]{1,0:T(2,128)} %param.8) | copy-start | bytes 196
  0.7 7.4 %copy-start.6 = (bf16[128,512]{1,0:T(8,128)(2,1)S(1)}, bf16[128,512]{1,0:T(8,128)(2,1)}, u32[]{:S(2)}) copy-start(bf16[128,512]{1,0:T(8,128)(2,1)} %param.7) | copy-start | bytes 393220
  5.0 41.8 %collective-permute-start.3 = (bf16[128,32,512]{2,1,0:T(8,128)(2,1)}, bf16[128,32,512]{2,1,0:T(8,128)(2,1)}, u32[]{:S(2)}, u32[]{:S(2)}) collective-permute-start(bf16[128,32,512]{2,1,0:T(8,128)(2,1)} %shard_map.68), channel_id=1, source_target_pairs={{4,8},{8,4},{12,16},{16,12},{20,24},{24,20},{28,32},{32,28},{36,40... | collective-permute-start | bytes 12582920 | tf_op jit(solution)/shard_map/ppermute | solution.py:410
  8.1 12.8 %copy-start.7 = (bf16[128,512]{1,0:T(8,128)(2,1)}, bf16[128,512]{1,0:T(8,128)(2,1)S(1)}, u32[]{:S(2)}) copy-start(bf16[128,512]{1,0:T(8,128)(2,1)S(1)} %mul.9.refs_0_) | copy-start | bytes 393220
  8.1 8.3 %collective-permute-start.2 = (bf16[128,512]{1,0:T(8,128)(2,1)S(1)}, bf16[128,512]{1,0:T(8,128)(2,1)S(1)}, u32[]{:S(2)}, u32[]{:S(2)}) collective-permute-start(bf16[128,512]{1,0:T(8,128)(2,1)S(1)} %mul.9.refs_0_), channel_id=1, source_target_pairs={{3,0},{0,1},{1,2},{2,3},{7,4},{4,5},{5,6},{6,7},{11,8},{8,9},{9,10... | collective-permute-start | bytes 393224 | tf_op jit(solution)/shard_map/ppermute | solution.py:419
  10.2 10.7 %collective-permute-start.1 = (bf16[128,512]{1,0:T(8,128)(2,1)S(1)}, bf16[128,512]{1,0:T(8,128)(2,1)S(1)}, u32[]{:S(2)}, u32[]{:S(2)}) collective-permute-start(bf16[128,512]{1,0:T(8,128)(2,1)S(1)} %mul.9.refs_0_), channel_id=1, source_target_pairs={{2,0},{3,1},{0,2},{1,3},{6,4},{7,5},{4,6},{5,7},{10,8},{11,9},{8,1... | collective-permute-start | bytes 393224 | tf_op jit(solution)/shard_map/ppermute | solution.py:419
  13.8 7.1 %collective-permute-start = (bf16[128,512]{1,0:T(8,128)(2,1)S(1)}, bf16[128,512]{1,0:T(8,128)(2,1)S(1)}, u32[]{:S(2)}, u32[]{:S(2)}) collective-permute-start(bf16[128,512]{1,0:T(8,128)(2,1)S(1)} %mul.9.refs_0_), channel_id=1, source_target_pairs={{1,0},{2,1},{3,2},{0,3},{5,4},{6,5},{7,6},{4,7},{9,8},{10,9},{11,1... | collective-permute-start | bytes 393224 | tf_op jit(solution)/shard_map/ppermute | solution.py:419
  15.6 19.1 %copy-start.5 = (bf16[128,384]{1,0:T(8,128)(2,1)S(1)}, bf16[128,384]{1,0:T(8,128)(2,1)}, u32[]{:S(2)}) copy-start(bf16[128,384]{1,0:T(8,128)(2,1)} %param.9) | copy-start | bytes 294916
  16.5 4.4 %copy-start.12 = (bf16[128,512]{1,0:T(8,128)(2,1)}, bf16[128,512]{1,0:T(8,128)(2,1)S(1)}, u32[]{:S(2)}) copy-start(bf16[128,512]{1,0:T(8,128)(2,1)S(1)} %collective-permute-done.2.refs_3_) | copy-start | bytes 393220
  20.9 0.7 copy-start.13
  21.5 0.7 copy-start.14
  33.2 29.8 %collective-permute-start.7 = (bf16[4,8,32,16,128]{4,3,2,1,0:T(8,128)(2,1)}, bf16[4,8,32,16,128]{4,3,2,1,0:T(8,128)(2,1)}, u32[]{:S(2)}, u32[]{:S(2)}) collective-permute-start(bf16[4,8,32,16,128]{4,3,2,1,0:T(8,128)(2,1)} %get-tuple-element.33.refs_4_), channel_id=1, source_target_pairs={{0,4},{4,0},{8,12},{12,8},{16,20},{20,16},{24,28},{28,24},{32,36},... | collective-permute-start | bytes 12582920 | tf_op jit(solution)/shard_map/ppermute | solution.py:430
  33.3 10.5 %collective-permute-start.4 = (bf16[2,8,32,16,128]{4,3,2,1,0:T(8,128)(2,1)}, bf16[2,8,32,16,128]{4,3,2,1,0:T(8,128)(2,1)}, u32[]{:S(2)}, u32[]{:S(2)}) collective-permute-start(bf16[2,8,32,16,128]{4,3,2,1,0:T(8,128)(2,1)} %get-tuple-element.29.refs_0_), channel_id=1, source_target_pairs={{0,4},{4,0},{8,12},{12,8},{16,20},{20,16},{24,28},{28,24},{32,36},... | collective-permute-start | bytes 6291464 | tf_op jit(solution)/shard_map/ppermute | solution.py:430
  33.8 13.0 %collective-permute-start.5 = (bf16[2,8,32,16,128]{4,3,2,1,0:T(8,128)(2,1)}, bf16[2,8,32,16,128]{4,3,2,1,0:T(8,128)(2,1)}, u32[]{:S(2)}, u32[]{:S(2)}) collective-permute-start(bf16[2,8,32,16,128]{4,3,2,1,0:T(8,128)(2,1)} %get-tuple-element.30.refs_1_), channel_id=1, source_target_pairs={{0,4},{4,0},{8,12},{12,8},{16,20},{20,16},{24,28},{28,24},{32,36},... | collective-permute-start | bytes 6291464 | tf_op jit(solution)/shard_map/ppermute | solution.py:430
  33.9 29.1 %collective-permute-start.6 = (bf16[2,8,32,16,128]{4,3,2,1,0:T(8,128)(2,1)}, bf16[2,8,32,16,128]{4,3,2,1,0:T(8,128)(2,1)S(1)}, u32[]{:S(2)}, u32[]{:S(2)}) collective-permute-start(bf16[2,8,32,16,128]{4,3,2,1,0:T(8,128)(2,1)} %get-tuple-element.32), channel_id=1, source_target_pairs={{4,8},{8,4},{12,16},{16,12},{20,24},{24,20},{28,32},{32,28},{36,40... | collective-permute-start | bytes 6291464 | tf_op jit(solution)/shard_map/ppermute | solution.py:410
  46.8 1.6 %copy-start.1 = (bf16[2,8,32,16,128]{4,3,2,1,0:T(8,128)(2,1)S(1)}, bf16[2,8,32,16,128]{4,3,2,1,0:T(8,128)(2,1)}, u32[]{:S(2)}) copy-start(bf16[2,8,32,16,128]{4,3,2,1,0:T(8,128)(2,1)} %get-tuple-element.29.refs_0_) | copy-start | bytes 6291460
  48.4 1.6 %copy-start.2 = (bf16[2,8,32,16,128]{4,3,2,1,0:T(8,128)(2,1)S(1)}, bf16[2,8,32,16,128]{4,3,2,1,0:T(8,128)(2,1)}, u32[]{:S(2)}) copy-start(bf16[2,8,32,16,128]{4,3,2,1,0:T(8,128)(2,1)} %get-tuple-element.30.refs_1_) | copy-start | bytes 6291460
  50.0 1.0 copy-start.3
  51.0 10.5 %copy-start.9 = (bf16[1,8,32,16,128]{4,3,2,1,0:T(8,128)(2,1)S(1)}, bf16[1,8,32,16,128]{4,3,2,1,0:T(8,128)(2,1)}, u32[]{:S(2)}) copy-start(bf16[1,8,32,16,128]{4,3,2,1,0:T(8,128)(2,1)} %get-tuple-element.37) | copy-start | bytes 3145732
  51.0 11.3 %copy-start.11 = (bf16[1,8,16,16,128]{4,3,2,1,0:T(8,128)(2,1)S(1)}, bf16[1,8,16,16,128]{4,3,2,1,0:T(8,128)(2,1)}, u32[]{:S(2)}) copy-start(bf16[1,8,16,16,128]{4,3,2,1,0:T(8,128)(2,1)} %get-tuple-element.41) | copy-start | bytes 1572868
  51.0 12.0 %copy-start = (bf16[4,8,32,16,128]{4,3,2,1,0:T(8,128)(2,1)S(1)}, bf16[4,8,32,16,128]{4,3,2,1,0:T(8,128)(2,1)}, u32[]{:S(2)}) copy-start(bf16[4,8,32,16,128]{4,3,2,1,0:T(8,128)(2,1)} %get-tuple-element.33.refs_4_) | copy-start | bytes 12582916
  51.0 12.0 %copy-start.4 = (f32[2,1,512]{2,1,0:T(1,128)S(1)}, f32[2,1,512]{2,1,0:T(1,128)}, u32[]{:S(2)}) copy-start(f32[2,1,512]{2,1,0:T(1,128)} %convert_element_type.20.mask_ref.refs_1_) | copy-start | bytes 12292
  61.5 9.6 %collective-permute-start.8 = (bf16[1,8,32,16,128]{4,3,2,1,0:T(8,128)(2,1)S(1)}, bf16[1,8,32,16,128]{4,3,2,1,0:T(8,128)(2,1)S(1)}, u32[]{:S(2)}, u32[]{:S(2)}) collective-permute-start(bf16[1,8,32,16,128]{4,3,2,1,0:T(8,128)(2,1)S(1)} %copy-done.9), channel_id=1, source_target_pairs={{4,8},{8,4},{12,16},{16,12},{20,24},{24,20},{28,32},{32,28},{36,40... | collective-permute-start | bytes 3145736 | tf_op jit(solution)/shard_map/ppermute | solution.py:410
  62.3 14.1 %collective-permute-start.9 = (bf16[1,8,16,16,128]{4,3,2,1,0:T(8,128)(2,1)S(1)}, bf16[1,8,16,16,128]{4,3,2,1,0:T(8,128)(2,1)S(1)}, u32[]{:S(2)}, u32[]{:S(2)}) collective-permute-start(bf16[1,8,16,16,128]{4,3,2,1,0:T(8,128)(2,1)S(1)} %copy-done.11), channel_id=1, source_target_pairs={{4,8},{8,4},{12,16},{16,12},{20,24},{24,20},{28,32},{32,28},{36,40... | collective-permute-start | bytes 1572872 | tf_op jit(solution)/shard_map/ppermute | solution.py:410
  63.0 7.4 %copy-start.10 = (bf16[1,8,16,16,128]{4,3,2,1,0:T(8,128)(2,1)S(1)}, bf16[1,8,16,16,128]{4,3,2,1,0:T(8,128)(2,1)}, u32[]{:S(2)}) copy-start(bf16[1,8,16,16,128]{4,3,2,1,0:T(8,128)(2,1)} %get-tuple-element.45) | copy-start | bytes 1572868
  70.4 10.5 %collective-permute-start.10 = (bf16[1,8,16,16,128]{4,3,2,1,0:T(8,128)(2,1)S(1)}, bf16[1,8,16,16,128]{4,3,2,1,0:T(8,128)(2,1)S(1)}, u32[]{:S(2)}, u32[]{:S(2)}) collective-permute-start(bf16[1,8,16,16,128]{4,3,2,1,0:T(8,128)(2,1)S(1)} %copy-done.10), channel_id=1, source_target_pairs={{4,8},{8,4},{12,16},{16,12},{20,24},{24,20},{28,32},{32,28},{36,40... | collective-permute-start | bytes 1572872 | tf_op jit(solution)/shard_map/ppermute | solution.py:410
  83.2 19.9 %collective-permute-start.11 = (f32[64,64]{1,0:T(8,128)S(1)}, f32[64,64]{1,0:T(8,128)S(1)}, u32[]{:S(2)}, u32[]{:S(2)}) collective-permute-start(f32[64,64]{1,0:T(8,128)S(1)} %get-tuple-element.51), channel_id=1, source_target_pairs={{0,4},{4,0},{8,12},{12,8},{16,20},{20,16},{24,28},{28,24},{32,36},... | collective-permute-start | bytes 49160 | tf_op jit(solution)/shard_map/ppermute | solution.py:395
  103.1 3.9 %collective-permute-start.12 = (f32[64,64]{1,0:T(8,128)S(1)}, f32[64,64]{1,0:T(8,128)S(1)}, u32[]{:S(2)}, u32[]{:S(2)}) collective-permute-start(f32[64,64]{1,0:T(8,128)S(1)} %add.20), channel_id=1, source_target_pairs={{0,8},{4,12},{8,0},{12,4},{16,24},{20,28},{24,16},{28,20},{32,40},... | collective-permute-start | bytes 49160 | tf_op jit(solution)/shard_map/ppermute | solution.py:395
  107.0 6.7 %collective-permute-start.13 = (f32[64,64]{1,0:T(8,128)S(1)}, f32[64,64]{1,0:T(8,128)S(1)}, u32[]{:S(2)}, u32[]{:S(2)}) collective-permute-start(f32[64,64]{1,0:T(8,128)S(1)} %add.21), channel_id=1, source_target_pairs={{0,24},{4,28},{8,16},{12,20},{16,8},{20,12},{24,0},{28,4},{32,56},... | collective-permute-start | bytes 49160 | tf_op jit(solution)/shard_map/ppermute | solution.py:395
  113.7 4.5 %collective-permute-start.14 = (f32[64,64]{1,0:T(8,128)S(1)}, f32[64,64]{1,0:T(8,128)S(1)}, u32[]{:S(2)}, u32[]{:S(2)}) collective-permute-start(f32[64,64]{1,0:T(8,128)S(1)} %add.22), channel_id=1, source_target_pairs={{0,32},{4,36},{8,40},{12,44},{16,48},{20,52},{24,56},{28,60},{32,0... | collective-permute-start | bytes 49160 | tf_op jit(solution)/shard_map/ppermute | solution.py:395
  118.2 5.3 %collective-permute-start.15 = (f32[64,64]{1,0:T(8,128)S(1)}, f32[64,64]{1,0:T(8,128)S(1)}, u32[]{:S(2)}, u32[]{:S(2)}) collective-permute-start(f32[64,64]{1,0:T(8,128)S(1)} %add.23), channel_id=1, source_target_pairs={{0,96},{4,100},{8,104},{12,108},{16,112},{20,116},{24,120},{28,124... | collective-permute-start | bytes 49160 | tf_op jit(solution)/shard_map/ppermute | solution.py:395

commit v6 on v5

--- a/solution.py
+++ b/solution.py
@@ -101,7 +101,7 @@
         scratch_shapes=[
             pltpu.VMEM(tc.shape, jnp.bfloat16),
             pltpu.VMEM(whole, jnp.bfloat16),
-            pltpu.VMEM((width // SIG, PB * (cols + 1) + 8, SIG), jnp.float32),
+            pltpu.VMEM((width // SIG, (PB + 1) * (cols + 1) + 8, SIG), jnp.float32),
             pltpu.SemaphoreType.DMA((rows // PB,)),
             pltpu.SemaphoreType.DMA((len(PIECES),)),
         ],
@@ -150,7 +150,7 @@
 
 def raw_slice(tc, center_mask):
     rows, _, width = tc.shape
-    pieces = 8
+    pieces = 4
     return pl.pallas_call(
         raw_kernel_send,
         in_specs=[pl.BlockSpec(memory_space=pltpu.SMEM), HBM],
@@ -260,8 +260,8 @@
             buf,
             buf,
             pltpu.VMEM((tiles, rows, count, SIG), jnp.bfloat16),
-            pltpu.VMEM((tiles, PB * (count + 1) + 8, SIG), jnp.float32),
-            pltpu.VMEM((rows * (count + 1), SIG), jnp.float32),
+            pltpu.VMEM((tiles, (PB + 1) * (count + 1) + 8, SIG), jnp.float32),
+            pltpu.VMEM(((rows + 1) * (count + 1) + 8, SIG), jnp.float32),
             pltpu.SemaphoreType.DMA((rows // PB,)),
             pltpu.SemaphoreType.DMA((2, tiles)),
             pltpu.SemaphoreType.DMA((tiles,)),
@@ -377,7 +377,7 @@
             pltpu.VMEM(far.shape, jnp.bfloat16),
             pltpu.VMEM((tiles, rows, RAW_STEP if raws else 16, SIG), jnp.bfloat16),
             pltpu.VMEM((tiles, rows, count, SIG), jnp.bfloat16),
-            pltpu.VMEM((rows * (count + 1), SIG), jnp.float32),
+            pltpu.VMEM(((rows + 1) * (count + 1) + 8, SIG), jnp.float32),
             pltpu.SemaphoreType.DMA((tiles,)),
             pltpu.SemaphoreType.DMA((5, tiles)),
         ],

time: 125 us -> 125 us (level)
  no operation moved by 1% of the time
where the time goes in v6:
time: 125 us; the launch traced here: 124 us
  Pallas kernels  45.3 us (36%)
  starting transfers between devices  44.5 us (36%)
  waiting for transfers between devices  25.8 us (21%)
  local copies, waits for them, and re-layouts  6.73 us (5%)
    ppermute x5, starting transfers between devices, sum_pa(): value = value + lax.ppermute(value, 'pa', pairs)  31.7 us
    pallas_call x4, Pallas kernels, fit_call(): pl.pallas_call(lambda *refs: fit_kernel(chunk, raws, role, *refs), in_spe...  19.4 us
    ppermute x3, waiting for transfers between devices, to_near(): return lax.ppermute(value, 'pa', near_pairs)  12 us
    pallas_call x1, Pallas kernels, half_call(): pl.pallas_call(half_kernel, in_specs=[WHOLE] * (1 + len(parts)) + [HBM],...  11.2 us
    pallas_call x1, Pallas kernels, raw_call(): pl.pallas_call(raw_kernel, in_specs=[WHOLE, WHOLE] + [HBM] * 5, out_specs...  10.5 us
    ppermute x5, waiting for transfers between devices, sum_pa(): value = value + lax.ppermute(value, 'pa', pairs)  8.48 us
    ppermute x3, starting transfers between devices, on_device(): lax.ppermute(local, 'mu', [((i + k) % count, i) for i in range(count)])  6.66 us
    unnamed x32, local copies, waits for them, and re-layouts  5.57 us
  transfers between devices with their start and end apart: 16, of which 9 were waited for; matrix products, arithmetic and copies ran while one was open for 1% of the time, Pallas kernels for 31%

profile of v6, /device:TPU:0, one launch (start us, length us, event | category | flops | bytes accessed | tf_op | source)
XLA Modules:
  0.0 124.0 jit_solution(3985491504433016945)
XLA Ops:
  0.7 4.2 %shard_map.68 = bf16[128,32,512]{2,1,0:T(8,128)(2,1)} custom-call(s32[2,1,8]{2,1,0:T(1,128)} %mask_ref.1, bf16[128,64,512]{2,1,0:T(8,128)(2,1)} %refs_6_.5), custom_call_target="tpu_custom_call" | custom-call | flops 1200000000 | bytes 3600000 | tf_op jit(solution)/shard_map/pallas_call | solution.py:154
  4.9 2.6 %collective-permute-start.3 = (bf16[128,32,512]{2,1,0:T(8,128)(2,1)}, bf16[128,32,512]{2,1,0:T(8,128)(2,1)}, u32[]{:S(2)}, u32[]{:S(2)}) collective-permute-start(bf16[128,32,512]{2,1,0:T(8,128)(2,1)} %shard_map.68), channel_id=1, source_target_pairs={{4,8},{8,4},{12,16},{16,12},{20,24},{24,20},{28,32},{32,28},{36,40... | collective-permute-start | bytes 12582920 | tf_op jit(solution)/shard_map/ppermute | solution.py:410
  7.5 0.1 copy.11
  7.6 0.1 broadcast_in_dim.10
  7.7 0.1 convert_element_type.22
  7.8 0.1 copy.12
  8.0 2.1 %collective-permute-start.2 = (bf16[128,512]{1,0:T(8,128)(2,1)S(1)}, bf16[128,512]{1,0:T(8,128)(2,1)S(1)}, u32[]{:S(2)}, u32[]{:S(2)}) collective-permute-start(bf16[128,512]{1,0:T(8,128)(2,1)S(1)} %mul.9.refs_0_), channel_id=1, source_target_pairs={{3,0},{0,1},{1,2},{2,3},{7,4},{4,5},{5,6},{6,7},{11,8},{8,9},{9,10... | collective-permute-start | bytes 393224 | tf_op jit(solution)/shard_map/ppermute | solution.py:419
  10.1 3.6 %collective-permute-start.1 = (bf16[128,512]{1,0:T(8,128)(2,1)S(1)}, bf16[128,512]{1,0:T(8,128)(2,1)S(1)}, u32[]{:S(2)}, u32[]{:S(2)}) collective-permute-start(bf16[128,512]{1,0:T(8,128)(2,1)S(1)} %mul.9.refs_0_), channel_id=1, source_target_pairs={{2,0},{3,1},{0,2},{1,3},{6,4},{7,5},{4,6},{5,7},{10,8},{11,9},{8,1... | collective-permute-start | bytes 393224 | tf_op jit(solution)/shard_map/ppermute | solution.py:419
  13.6 1.0 collective-permute-start
  14.7 0.1 broadcast_in_dim.9
  14.7 0.7 convert_element_type.20.mask_ref.refs_1_
  15.4 0.9 collective-permute-done.2.refs_3_
  16.3 4.4 %collective-permute-done.1.refs_2_ = bf16[128,512]{1,0:T(8,128)(2,1)S(1)} collective-permute-done((bf16[128,512]{1,0:T(8,128)(2,1)S(1)}, bf16[128,512]{1,0:T(8,128)(2,1)S(1)}, u32[]{:S(2)}, u32[]{:S(2)}) %collective-permute-start.1) | collective-permute-done | bytes 131104 | tf_op jit(solution)/shard_map/ppermute | solution.py:419
  20.7 0.0 collective-permute-done.refs_1_
  20.7 0.6 copy-done.13
  21.4 0.7 copy-done.14
  22.1 11.2 %shard_map.69 = (bf16[512,512]{1,0:T(8,128)(2,1)}, bf16[4,8,32,16,128]{4,3,2,1,0:T(8,128)(2,1)}, bf16[2,8,32,16,128]{4,3,2,1,0:T(8,128)(2,1)}, bf16[2,8,32,16,12...) custom-call(f32[2,1,512]{2,1,0:T(1,128)} %convert_element_type.20.ma, ...), custom_call_target="tpu_custom_call" | custom-call | flops 4000000000 | bytes 12000000 | tf_op jit(solution)/shard_map/pallas_call | solution.py:96
  33.2 0.1 collective-permute-start.7
  33.3 0.5 collective-permute-start.4
  33.8 0.1 collective-permute-start.5
  33.9 0.8 collective-permute-start.6
  34.8 9.0 %collective-permute-done.4.refs_2_ = bf16[2,8,32,16,128]{4,3,2,1,0:T(8,128)(2,1)} collective-permute-done((bf16[2,8,32,16,128]{4,3,2,1,0:T(8,128)(2,1)}, bf16[2,8,32,16,128]{4,3,2,1,0:T(8,128)(2,1)}, u32[]{:S(2)}, u32[]{:S(2)}) %collective-permute-start.4) | collective-permute-done | bytes 2097184 | tf_op jit(solution)/shard_map/ppermute | solution.py:430
  43.8 3.0 %collective-permute-done.5.refs_3_ = bf16[2,8,32,16,128]{4,3,2,1,0:T(8,128)(2,1)} collective-permute-done((bf16[2,8,32,16,128]{4,3,2,1,0:T(8,128)(2,1)}, bf16[2,8,32,16,128]{4,3,2,1,0:T(8,128)(2,1)}, u32[]{:S(2)}, u32[]{:S(2)}) %collective-permute-start.5) | collective-permute-done | bytes 2097184 | tf_op jit(solution)/shard_map/ppermute | solution.py:430
  46.8 1.6 %copy-done.1 = bf16[2,8,32,16,128]{4,3,2,1,0:T(8,128)(2,1)S(1)} copy-done((bf16[2,8,32,16,128]{4,3,2,1,0:T(8,128)(2,1)S(1)}, bf16[2,8,32,16,128]{4,3,2,1,0:T(8,128)(2,1)}, u32[]{:S(2)}) %copy-start.1) | copy-done | bytes 2097176
  48.4 1.6 %copy-done.2 = bf16[2,8,32,16,128]{4,3,2,1,0:T(8,128)(2,1)S(1)} copy-done((bf16[2,8,32,16,128]{4,3,2,1,0:T(8,128)(2,1)S(1)}, bf16[2,8,32,16,128]{4,3,2,1,0:T(8,128)(2,1)}, u32[]{:S(2)}) %copy-start.2) | copy-done | bytes 2097176
  50.0 1.0 copy-done.3
  51.0 10.5 %shard_map.70 = (bf16[128,64,512]{2,1,0:T(8,128)(2,1)}, f32[64,64]{1,0:T(8,128)S(1)}) custom-call(bf16[128,384]{1,0:T(8,128)(2,1)S(1)} %maximum_select_fusion.metric_ref.refs_0_, bf16[512,512]{1,0:T(8,128)(2,1)S(1)} %copy-done.3, bf16[128,32,512]{2,1,0:T(8,128)(2,1)} %collective-permute-done.3.raw, bf16[2,8,32,16,128]{4,3,2,1,0:T(8,128)(2,1)S(1)} %copy-done.1, ...), custom_call_target="tpu_custom_call" | custom-call | flops 1200000000 | bytes 3600000 | tf_op jit(solution)/shard_map/pallas_call | solution.py:249
  61.6 0.7 collective-permute-start.8
  62.4 0.7 collective-permute-start.9
  63.1 0.0 collective-permute-done.6.refs_3_
  63.1 7.4 %shard_map.71 = (bf16[128,64,512]{2,1,0:T(8,128)(2,1)}, f32[64,64]{1,0:T(8,128)S(1)}) custom-call(bf16[128,384]{1,0:T(8,128)(2,1)S(1)} %maximum_select_fusion.metric_ref.refs_0_, f32[2,1,512]{2,1,0:T(1,128)S(1)} %copy-done.4, f32[64,64]{1,0:T(8,128)S(1)} %get-tuple-element.31.refs_2_, ...), custom_call_target="tpu_custom_call", output_to_operand_aliasing={{0}: (7, {})} | custom-call | flops 1200000000 | bytes 3600000 | tf_op jit(solution)/shard_map/pallas_call | solution.py:368
  70.5 0.7 collective-permute-start.10
  71.2 5.2 %shard_map.72 = (bf16[128,64,512]{2,1,0:T(8,128)(2,1)}, f32[64,64]{1,0:T(8,128)S(1)}) custom-call(bf16[128,384]{1,0:T(8,128)(2,1)S(1)} %maximum_select_fusion.metric_ref.refs_0_, f32[2,1,512]{2,1,0:T(1,128)S(1)} %copy-done.4, f32[64,64]{1,0:T(8,128)S(1)} %get-tuple-element.35.refs_2_, ...), custom_call_target="tpu_custom_call", output_to_operand_aliasing={{0}: (7, {})} | custom-call | flops 1200000000 | bytes 3600000 | tf_op jit(solution)/shard_map/pallas_call | solution.py:368
  76.4 0.0 collective-permute-done.9.refs_3_
  76.5 4.6 %shard_map.73 = (bf16[128,64,512]{2,1,0:T(8,128)(2,1)}, f32[64,64]{1,0:T(8,128)S(1)}, bf16[1,8,32,16,128]{4,3,2,1,0:T(8,128)(2,1)S(1)}, bf16[1,8,32,16,128]{4,3,...) custom-call(bf16[128,384]{1,0:T(8,128)(2,1)S(1)} %maximum_select_fusion.metric_ref.refs_0_, ...), custom_call_target="tpu_custom_call", output_to_operand_aliasing={{0}: (7, {})} | custom-call | flops 1200000000 | bytes 3600000 | tf_op jit(solution)/shard_map/pallas_call | solution.py:368
  81.0 0.0 collective-permute-done.10.refs_3_
  81.0 2.2 %shard_map.74 = (bf16[128,64,512]{2,1,0:T(8,128)(2,1)}, f32[64,64]{1,0:T(8,128)S(1)}) custom-call(bf16[128,384]{1,0:T(8,128)(2,1)S(1)} %maximum_select_fusion.metric_ref.refs_0_, f32[2,1,512]{2,1,0:T(1,128)S(1)} %copy-done.4, f32[64,64]{1,0:T(8,128)S(1)} %get-tuple-element.43.refs_2_, ...), custom_call_target="tpu_custom_call", output_to_operand_aliasing={{0}: (7, {})} | custom-call | flops 1200000000 | bytes 3600000 | tf_op jit(solution)/shard_map/pallas_call | solution.py:368
  83.3 18.8 %collective-permute-start.11 = (f32[64,64]{1,0:T(8,128)S(1)}, f32[64,64]{1,0:T(8,128)S(1)}, u32[]{:S(2)}, u32[]{:S(2)}) collective-permute-start(f32[64,64]{1,0:T(8,128)S(1)} %get-tuple-element.51), channel_id=1, source_target_pairs={{0,4},{4,0},{8,12},{12,8},{16,20},{20,16},{24,28},{28,24},{32,36},... | collective-permute-start | bytes 49160 | tf_op jit(solution)/shard_map/ppermute | solution.py:395
  102.1 0.9 collective-permute-done.11
  103.0 2.0 %collective-permute-start.12 = (f32[64,64]{1,0:T(8,128)S(1)}, f32[64,64]{1,0:T(8,128)S(1)}, u32[]{:S(2)}, u32[]{:S(2)}) collective-permute-start(f32[64,64]{1,0:T(8,128)S(1)} %add.20), channel_id=1, source_target_pairs={{0,8},{4,12},{8,0},{12,4},{16,24},{20,28},{24,16},{28,20},{32,40},... | collective-permute-start | bytes 49160 | tf_op jit(solution)/shard_map/ppermute | solution.py:395
  104.9 1.9 %collective-permute-done.12 = f32[64,64]{1,0:T(8,128)S(1)} collective-permute-done((f32[64,64]{1,0:T(8,128)S(1)}, f32[64,64]{1,0:T(8,128)S(1)}, u32[]{:S(2)}, u32[]{:S(2)}) %collective-permute-start.12) | collective-permute-done | bytes 16416 | tf_op jit(solution)/shard_map/ppermute | solution.py:395
  106.9 4.8 %collective-permute-start.13 = (f32[64,64]{1,0:T(8,128)S(1)}, f32[64,64]{1,0:T(8,128)S(1)}, u32[]{:S(2)}, u32[]{:S(2)}) collective-permute-start(f32[64,64]{1,0:T(8,128)S(1)} %add.21), channel_id=1, source_target_pairs={{0,24},{4,28},{8,16},{12,20},{16,8},{20,12},{24,0},{28,4},{32,56},... | collective-permute-start | bytes 49160 | tf_op jit(solution)/shard_map/ppermute | solution.py:395
  111.7 1.9 %collective-permute-done.13 = f32[64,64]{1,0:T(8,128)S(1)} collective-permute-done((f32[64,64]{1,0:T(8,128)S(1)}, f32[64,64]{1,0:T(8,128)S(1)}, u32[]{:S(2)}, u32[]{:S(2)}) %collective-permute-start.13) | collective-permute-done | bytes 16416 | tf_op jit(solution)/shard_map/ppermute | solution.py:395
  113.6 2.6 %collective-permute-start.14 = (f32[64,64]{1,0:T(8,128)S(1)}, f32[64,64]{1,0:T(8,128)S(1)}, u32[]{:S(2)}, u32[]{:S(2)}) collective-permute-start(f32[64,64]{1,0:T(8,128)S(1)} %add.22), channel_id=1, source_target_pairs={{0,32},{4,36},{8,40},{12,44},{16,48},{20,52},{24,56},{28,60},{32,0... | collective-permute-start | bytes 49160 | tf_op jit(solution)/shard_map/ppermute | solution.py:395
  116.2 1.9 %collective-permute-done.14 = f32[64,64]{1,0:T(8,128)S(1)} collective-permute-done((f32[64,64]{1,0:T(8,128)S(1)}, f32[64,64]{1,0:T(8,128)S(1)}, u32[]{:S(2)}, u32[]{:S(2)}) %collective-permute-start.14) | collective-permute-done | bytes 16416 | tf_op jit(solution)/shard_map/ppermute | solution.py:395
  118.1 3.5 %collective-permute-start.15 = (f32[64,64]{1,0:T(8,128)S(1)}, f32[64,64]{1,0:T(8,128)S(1)}, u32[]{:S(2)}, u32[]{:S(2)}) collective-permute-start(f32[64,64]{1,0:T(8,128)S(1)} %add.23), channel_id=1, source_target_pairs={{0,96},{4,100},{8,104},{12,108},{16,112},{20,116},{24,120},{28,124... | collective-permute-start | bytes 49160 | tf_op jit(solution)/shard_map/ppermute | solution.py:395
  121.5 1.9 %collective-permute-done.15 = f32[64,64]{1,0:T(8,128)S(1)} collective-permute-done((f32[64,64]{1,0:T(8,128)S(1)}, f32[64,64]{1,0:T(8,128)S(1)}, u32[]{:S(2)}, u32[]{:S(2)}) %collective-permute-start.15) | collective-permute-done | bytes 16416 | tf_op jit(solution)/shard_map/ppermute | solution.py:395
  123.4 0.6 add_multiply_fusion
  (40 shorter events, 0.2 us)
Async XLA Ops:
  0.6 14.0 %copy-start.8 = (s32[2,1,8]{2,1,0:T(1,128)S(1)}, s32[2,1,8]{2,1,0:T(1,128)}, u32[]{:S(2)}) copy-start(s32[2,1,8]{2,1,0:T(1,128)} %mask_ref.1) | copy-start | bytes 196
  0.6 6.9 %copy-start.15 = (s32[2,8]{1,0:T(2,128)S(1)}, s32[2,8]{1,0:T(2,128)}, u32[]{:S(2)}) copy-start(s32[2,8]{1,0:T(2,128)} %param.8) | copy-start | bytes 196
  0.7 7.3 %copy-start.6 = (bf16[128,512]{1,0:T(8,128)(2,1)S(1)}, bf16[128,512]{1,0:T(8,128)(2,1)}, u32[]{:S(2)}) copy-start(bf16[128,512]{1,0:T(8,128)(2,1)} %param.7) | copy-start | bytes 393220
  4.9 41.9 %collective-permute-start.3 = (bf16[128,32,512]{2,1,0:T(8,128)(2,1)}, bf16[128,32,512]{2,1,0:T(8,128)(2,1)}, u32[]{:S(2)}, u32[]{:S(2)}) collective-permute-start(bf16[128,32,512]{2,1,0:T(8,128)(2,1)} %shard_map.68), channel_id=1, source_target_pairs={{4,8},{8,4},{12,16},{16,12},{20,24},{24,20},{28,32},{32,28},{36,40... | collective-permute-start | bytes 12582920 | tf_op jit(solution)/shard_map/ppermute | solution.py:410
  8.0 12.8 %copy-start.7 = (bf16[128,512]{1,0:T(8,128)(2,1)}, bf16[128,512]{1,0:T(8,128)(2,1)S(1)}, u32[]{:S(2)}) copy-start(bf16[128,512]{1,0:T(8,128)(2,1)S(1)} %mul.9.refs_0_) | copy-start | bytes 393220
  8.0 8.3 %collective-permute-start.2 = (bf16[128,512]{1,0:T(8,128)(2,1)S(1)}, bf16[128,512]{1,0:T(8,128)(2,1)S(1)}, u32[]{:S(2)}, u32[]{:S(2)}) collective-permute-start(bf16[128,512]{1,0:T(8,128)(2,1)S(1)} %mul.9.refs_0_), channel_id=1, source_target_pairs={{3,0},{0,1},{1,2},{2,3},{7,4},{4,5},{5,6},{6,7},{11,8},{8,9},{9,10... | collective-permute-start | bytes 393224 | tf_op jit(solution)/shard_map/ppermute | solution.py:419
  10.1 10.7 %collective-permute-start.1 = (bf16[128,512]{1,0:T(8,128)(2,1)S(1)}, bf16[128,512]{1,0:T(8,128)(2,1)S(1)}, u32[]{:S(2)}, u32[]{:S(2)}) collective-permute-start(bf16[128,512]{1,0:T(8,128)(2,1)S(1)} %mul.9.refs_0_), channel_id=1, source_target_pairs={{2,0},{3,1},{0,2},{1,3},{6,4},{7,5},{4,6},{5,7},{10,8},{11,9},{8,1... | collective-permute-start | bytes 393224 | tf_op jit(solution)/shard_map/ppermute | solution.py:419
  13.6 7.1 %collective-permute-start = (bf16[128,512]{1,0:T(8,128)(2,1)S(1)}, bf16[128,512]{1,0:T(8,128)(2,1)S(1)}, u32[]{:S(2)}, u32[]{:S(2)}) collective-permute-start(bf16[128,512]{1,0:T(8,128)(2,1)S(1)} %mul.9.refs_0_), channel_id=1, source_target_pairs={{1,0},{2,1},{3,2},{0,3},{5,4},{6,5},{7,6},{4,7},{9,8},{10,9},{11,1... | collective-permute-start | bytes 393224 | tf_op jit(solution)/shard_map/ppermute | solution.py:419
  15.4 19.3 %copy-start.5 = (bf16[128,384]{1,0:T(8,128)(2,1)S(1)}, bf16[128,384]{1,0:T(8,128)(2,1)}, u32[]{:S(2)}) copy-start(bf16[128,384]{1,0:T(8,128)(2,1)} %param.9) | copy-start | bytes 294916
  16.3 4.4 %copy-start.12 = (bf16[128,512]{1,0:T(8,128)(2,1)}, bf16[128,512]{1,0:T(8,128)(2,1)S(1)}, u32[]{:S(2)}) copy-start(bf16[128,512]{1,0:T(8,128)(2,1)S(1)} %collective-permute-done.2.refs_3_) | copy-start | bytes 393220
  20.7 0.7 copy-start.13
  21.4 0.7 copy-start.14
  33.2 29.8 %collective-permute-start.7 = (bf16[4,8,32,16,128]{4,3,2,1,0:T(8,128)(2,1)}, bf16[4,8,32,16,128]{4,3,2,1,0:T(8,128)(2,1)}, u32[]{:S(2)}, u32[]{:S(2)}) collective-permute-start(bf16[4,8,32,16,128]{4,3,2,1,0:T(8,128)(2,1)} %get-tuple-element.33.refs_4_), channel_id=1, source_target_pairs={{0,4},{4,0},{8,12},{12,8},{16,20},{20,16},{24,28},{28,24},{32,36},... | collective-permute-start | bytes 12582920 | tf_op jit(solution)/shard_map/ppermute | solution.py:430
  33.3 10.5 %collective-permute-start.4 = (bf16[2,8,32,16,128]{4,3,2,1,0:T(8,128)(2,1)}, bf16[2,8,32,16,128]{4,3,2,1,0:T(8,128)(2,1)}, u32[]{:S(2)}, u32[]{:S(2)}) collective-permute-start(bf16[2,8,32,16,128]{4,3,2,1,0:T(8,128)(2,1)} %get-tuple-element.29.refs_0_), channel_id=1, source_target_pairs={{0,4},{4,0},{8,12},{12,8},{16,20},{20,16},{24,28},{28,24},{32,36},... | collective-permute-start | bytes 6291464 | tf_op jit(solution)/shard_map/ppermute | solution.py:430
  33.8 13.0 %collective-permute-start.5 = (bf16[2,8,32,16,128]{4,3,2,1,0:T(8,128)(2,1)}, bf16[2,8,32,16,128]{4,3,2,1,0:T(8,128)(2,1)}, u32[]{:S(2)}, u32[]{:S(2)}) collective-permute-start(bf16[2,8,32,16,128]{4,3,2,1,0:T(8,128)(2,1)} %get-tuple-element.30.refs_1_), channel_id=1, source_target_pairs={{0,4},{4,0},{8,12},{12,8},{16,20},{20,16},{24,28},{28,24},{32,36},... | collective-permute-start | bytes 6291464 | tf_op jit(solution)/shard_map/ppermute | solution.py:430
  33.9 29.1 %collective-permute-start.6 = (bf16[2,8,32,16,128]{4,3,2,1,0:T(8,128)(2,1)}, bf16[2,8,32,16,128]{4,3,2,1,0:T(8,128)(2,1)S(1)}, u32[]{:S(2)}, u32[]{:S(2)}) collective-permute-start(bf16[2,8,32,16,128]{4,3,2,1,0:T(8,128)(2,1)} %get-tuple-element.32), channel_id=1, source_target_pairs={{4,8},{8,4},{12,16},{16,12},{20,24},{24,20},{28,32},{32,28},{36,40... | collective-permute-start | bytes 6291464 | tf_op jit(solution)/shard_map/ppermute | solution.py:410
  46.8 1.6 %copy-start.1 = (bf16[2,8,32,16,128]{4,3,2,1,0:T(8,128)(2,1)S(1)}, bf16[2,8,32,16,128]{4,3,2,1,0:T(8,128)(2,1)}, u32[]{:S(2)}) copy-start(bf16[2,8,32,16,128]{4,3,2,1,0:T(8,128)(2,1)} %get-tuple-element.29.refs_0_) | copy-start | bytes 6291460
  48.4 1.6 %copy-start.2 = (bf16[2,8,32,16,128]{4,3,2,1,0:T(8,128)(2,1)S(1)}, bf16[2,8,32,16,128]{4,3,2,1,0:T(8,128)(2,1)}, u32[]{:S(2)}) copy-start(bf16[2,8,32,16,128]{4,3,2,1,0:T(8,128)(2,1)} %get-tuple-element.30.refs_1_) | copy-start | bytes 6291460
  50.0 1.0 copy-start.3
  51.0 10.6 %copy-start.9 = (bf16[1,8,32,16,128]{4,3,2,1,0:T(8,128)(2,1)S(1)}, bf16[1,8,32,16,128]{4,3,2,1,0:T(8,128)(2,1)}, u32[]{:S(2)}) copy-start(bf16[1,8,32,16,128]{4,3,2,1,0:T(8,128)(2,1)} %get-tuple-element.37) | copy-start | bytes 3145732
  51.0 11.3 %copy-start.11 = (bf16[1,8,16,16,128]{4,3,2,1,0:T(8,128)(2,1)S(1)}, bf16[1,8,16,16,128]{4,3,2,1,0:T(8,128)(2,1)}, u32[]{:S(2)}) copy-start(bf16[1,8,16,16,128]{4,3,2,1,0:T(8,128)(2,1)} %get-tuple-element.41) | copy-start | bytes 1572868
  51.0 12.0 %copy-start = (bf16[4,8,32,16,128]{4,3,2,1,0:T(8,128)(2,1)S(1)}, bf16[4,8,32,16,128]{4,3,2,1,0:T(8,128)(2,1)}, u32[]{:S(2)}) copy-start(bf16[4,8,32,16,128]{4,3,2,1,0:T(8,128)(2,1)} %get-tuple-element.33.refs_4_) | copy-start | bytes 12582916
  51.0 12.0 %copy-start.4 = (f32[2,1,512]{2,1,0:T(1,128)S(1)}, f32[2,1,512]{2,1,0:T(1,128)}, u32[]{:S(2)}) copy-start(f32[2,1,512]{2,1,0:T(1,128)} %convert_element_type.20.mask_ref.refs_1_) | copy-start | bytes 12292
  61.6 9.6 %collective-permute-start.8 = (bf16[1,8,32,16,128]{4,3,2,1,0:T(8,128)(2,1)S(1)}, bf16[1,8,32,16,128]{4,3,2,1,0:T(8,128)(2,1)S(1)}, u32[]{:S(2)}, u32[]{:S(2)}) collective-permute-start(bf16[1,8,32,16,128]{4,3,2,1,0:T(8,128)(2,1)S(1)} %copy-done.9), channel_id=1, source_target_pairs={{4,8},{8,4},{12,16},{16,12},{20,24},{24,20},{28,32},{32,28},{36,40... | collective-permute-start | bytes 3145736 | tf_op jit(solution)/shard_map/ppermute | solution.py:410
  62.4 14.1 %collective-permute-start.9 = (bf16[1,8,16,16,128]{4,3,2,1,0:T(8,128)(2,1)S(1)}, bf16[1,8,16,16,128]{4,3,2,1,0:T(8,128)(2,1)S(1)}, u32[]{:S(2)}, u32[]{:S(2)}) collective-permute-start(bf16[1,8,16,16,128]{4,3,2,1,0:T(8,128)(2,1)S(1)} %copy-done.11), channel_id=1, source_target_pairs={{4,8},{8,4},{12,16},{16,12},{20,24},{24,20},{28,32},{32,28},{36,40... | collective-permute-start | bytes 1572872 | tf_op jit(solution)/shard_map/ppermute | solution.py:410
  63.1 7.4 %copy-start.10 = (bf16[1,8,16,16,128]{4,3,2,1,0:T(8,128)(2,1)S(1)}, bf16[1,8,16,16,128]{4,3,2,1,0:T(8,128)(2,1)}, u32[]{:S(2)}) copy-start(bf16[1,8,16,16,128]{4,3,2,1,0:T(8,128)(2,1)} %get-tuple-element.45) | copy-start | bytes 1572868
  70.5 10.6 %collective-permute-start.10 = (bf16[1,8,16,16,128]{4,3,2,1,0:T(8,128)(2,1)S(1)}, bf16[1,8,16,16,128]{4,3,2,1,0:T(8,128)(2,1)S(1)}, u32[]{:S(2)}, u32[]{:S(2)}) collective-permute-start(bf16[1,8,16,16,128]{4,3,2,1,0:T(8,128)(2,1)S(1)} %copy-done.10), channel_id=1, source_target_pairs={{4,8},{8,4},{12,16},{16,12},{20,24},{24,20},{28,32},{32,28},{36,40... | collective-permute-start | bytes 1572872 | tf_op jit(solution)/shard_map/ppermute | solution.py:410
  83.3 19.7 %collective-permute-start.11 = (f32[64,64]{1,0:T(8,128)S(1)}, f32[64,64]{1,0:T(8,128)S(1)}, u32[]{:S(2)}, u32[]{:S(2)}) collective-permute-start(f32[64,64]{1,0:T(8,128)S(1)} %get-tuple-element.51), channel_id=1, source_target_pairs={{0,4},{4,0},{8,12},{12,8},{16,20},{20,16},{24,28},{28,24},{32,36},... | collective-permute-start | bytes 49160 | tf_op jit(solution)/shard_map/ppermute | solution.py:395
  103.0 3.9 %collective-permute-start.12 = (f32[64,64]{1,0:T(8,128)S(1)}, f32[64,64]{1,0:T(8,128)S(1)}, u32[]{:S(2)}, u32[]{:S(2)}) collective-permute-start(f32[64,64]{1,0:T(8,128)S(1)} %add.20), channel_id=1, source_target_pairs={{0,8},{4,12},{8,0},{12,4},{16,24},{20,28},{24,16},{28,20},{32,40},... | collective-permute-start | bytes 49160 | tf_op jit(solution)/shard_map/ppermute | solution.py:395
  106.9 6.7 %collective-permute-start.13 = (f32[64,64]{1,0:T(8,128)S(1)}, f32[64,64]{1,0:T(8,128)S(1)}, u32[]{:S(2)}, u32[]{:S(2)}) collective-permute-start(f32[64,64]{1,0:T(8,128)S(1)} %add.21), channel_id=1, source_target_pairs={{0,24},{4,28},{8,16},{12,20},{16,8},{20,12},{24,0},{28,4},{32,56},... | collective-permute-start | bytes 49160 | tf_op jit(solution)/shard_map/ppermute | solution.py:395
  113.6 4.5 %collective-permute-start.14 = (f32[64,64]{1,0:T(8,128)S(1)}, f32[64,64]{1,0:T(8,128)S(1)}, u32[]{:S(2)}, u32[]{:S(2)}) collective-permute-start(f32[64,64]{1,0:T(8,128)S(1)} %add.22), channel_id=1, source_target_pairs={{0,32},{4,36},{8,40},{12,44},{16,48},{20,52},{24,56},{28,60},{32,0... | collective-permute-start | bytes 49160 | tf_op jit(solution)/shard_map/ppermute | solution.py:395
  118.1 5.4 %collective-permute-start.15 = (f32[64,64]{1,0:T(8,128)S(1)}, f32[64,64]{1,0:T(8,128)S(1)}, u32[]{:S(2)}, u32[]{:S(2)}) collective-permute-start(f32[64,64]{1,0:T(8,128)S(1)} %add.23), channel_id=1, source_target_pairs={{0,96},{4,100},{8,104},{12,108},{16,112},{20,116},{24,120},{28,124... | collective-permute-start | bytes 49160 | tf_op jit(solution)/shard_map/ppermute | solution.py:395

commit v7 on v6

--- a/solution.py
+++ b/solution.py
@@ -390,9 +390,18 @@
 def sum_pa(value):
     size = lax.axis_size("pa")
 
-    for stride, mask in ((1, 1), (2, 1), (2, 3), (8, 1), (8, 3)):
-        pairs = [(i, i ^ (mask * stride)) for i in range(size)]
-        value = value + lax.ppermute(value, "pa", pairs)
+    def moved(value, stride, count, k):
+        span = stride * count
+        pairs = [
+            (i, (i // span) * span + ((i // stride + k) % count) * stride + i % stride)
+            for i in range(size)
+        ]
+        return lax.ppermute(value, "pa", pairs)
+
+    value = value + moved(value, 1, 2, 1)
+    for stride in (2, 8):
+        parts = [moved(value, stride, 4, k) for k in (1, 2, 3)]
+        value = (value + parts[1]) + (parts[0] + parts[2])
     return value
 
 

time: 125 us -> 123 us (0.984)
    ppermute x5 -> x7, starting transfers between devices: 31.7 us -> 30.4 us  [moved(): return lax.ppermute(value, 'pa', pairs)]
    ppermute x5 -> x7, waiting for transfers between devices: 8.48 us -> 7.8 us  [moved(): return lax.ppermute(value, 'pa', pairs)]
  transfers between devices with their start and end apart: 16 -> 18, of which waited for: 9 -> 9; matrix products, arithmetic and copies ran while one was open for 1% -> 1% of each run, Pallas kernels for 31% -> 32%
where the time goes in v7:
time: 123 us; the launch traced here: 122 us
  Pallas kernels  45.3 us (37%)
  starting transfers between devices  43.5 us (35%)
  waiting for transfers between devices  25 us (20%)
  local copies, waits for them, and re-layouts  6.73 us (5%)
    ppermute x7, starting transfers between devices, moved(): return lax.ppermute(value, 'pa', pairs)  30.4 us
    pallas_call x4, Pallas kernels, fit_call(): pl.pallas_call(lambda *refs: fit_kernel(chunk, raws, role, *refs), in_spe...  19.4 us
    ppermute x3, waiting for transfers between devices, to_near(): return lax.ppermute(value, 'pa', near_pairs)  11.9 us
    pallas_call x1, Pallas kernels, half_call(): pl.pallas_call(half_kernel, in_specs=[WHOLE] * (1 + len(parts)) + [HBM],...  11.2 us
    pallas_call x1, Pallas kernels, raw_call(): pl.pallas_call(raw_kernel, in_specs=[WHOLE, WHOLE] + [HBM] * 5, out_specs...  10.5 us
    ppermute x7, waiting for transfers between devices, moved(): return lax.ppermute(value, 'pa', pairs)  7.8 us
    ppermute x3, starting transfers between devices, on_device(): lax.ppermute(local, 'mu', [((i + k) % count, i) for i in range(count)])  6.66 us
    unnamed x32, local copies, waits for them, and re-layouts  5.57 us
  transfers between devices with their start and end apart: 18, of which 9 were waited for; matrix products, arithmetic and copies ran while one was open for 1% of the time, Pallas kernels for 32%

profile of v7, /device:TPU:0, one launch (start us, length us, event | category | flops | bytes accessed | tf_op | source)
XLA Modules:
  0.0 122.2 jit_solution(16268906999811421578)
XLA Ops:
  0.7 4.2 %shard_map.68 = bf16[128,32,512]{2,1,0:T(8,128)(2,1)} custom-call(s32[2,1,8]{2,1,0:T(1,128)} %mask_ref.1, bf16[128,64,512]{2,1,0:T(8,128)(2,1)} %refs_6_.5), custom_call_target="tpu_custom_call" | custom-call | flops 1200000000 | bytes 3600000 | tf_op jit(solution)/shard_map/pallas_call | solution.py:154
  4.9 2.6 %collective-permute-start.3 = (bf16[128,32,512]{2,1,0:T(8,128)(2,1)}, bf16[128,32,512]{2,1,0:T(8,128)(2,1)}, u32[]{:S(2)}, u32[]{:S(2)}) collective-permute-start(bf16[128,32,512]{2,1,0:T(8,128)(2,1)} %shard_map.68), channel_id=1, source_target_pairs={{4,8},{8,4},{12,16},{16,12},{20,24},{24,20},{28,32},{32,28},{36,40... | collective-permute-start | bytes 12582920 | tf_op jit(solution)/shard_map/ppermute | solution.py:419
  7.5 0.1 copy.11
  7.6 0.1 broadcast_in_dim.10
  7.7 0.1 convert_element_type.22
  7.8 0.1 copy.12
  8.0 2.1 %collective-permute-start.2 = (bf16[128,512]{1,0:T(8,128)(2,1)S(1)}, bf16[128,512]{1,0:T(8,128)(2,1)S(1)}, u32[]{:S(2)}, u32[]{:S(2)}) collective-permute-start(bf16[128,512]{1,0:T(8,128)(2,1)S(1)} %mul.9.refs_0_), channel_id=1, source_target_pairs={{3,0},{0,1},{1,2},{2,3},{7,4},{4,5},{5,6},{6,7},{11,8},{8,9},{9,10... | collective-permute-start | bytes 393224 | tf_op jit(solution)/shard_map/ppermute | solution.py:428
  10.1 3.6 %collective-permute-start.1 = (bf16[128,512]{1,0:T(8,128)(2,1)S(1)}, bf16[128,512]{1,0:T(8,128)(2,1)S(1)}, u32[]{:S(2)}, u32[]{:S(2)}) collective-permute-start(bf16[128,512]{1,0:T(8,128)(2,1)S(1)} %mul.9.refs_0_), channel_id=1, source_target_pairs={{2,0},{3,1},{0,2},{1,3},{6,4},{7,5},{4,6},{5,7},{10,8},{11,9},{8,1... | collective-permute-start | bytes 393224 | tf_op jit(solution)/shard_map/ppermute | solution.py:428
  13.7 1.0 collective-permute-start
  14.7 0.1 broadcast_in_dim.9
  14.7 0.7 convert_element_type.20.mask_ref.refs_1_
  15.4 0.9 collective-permute-done.2.refs_3_
  16.3 4.4 %collective-permute-done.1.refs_2_ = bf16[128,512]{1,0:T(8,128)(2,1)S(1)} collective-permute-done((bf16[128,512]{1,0:T(8,128)(2,1)S(1)}, bf16[128,512]{1,0:T(8,128)(2,1)S(1)}, u32[]{:S(2)}, u32[]{:S(2)}) %collective-permute-start.1) | collective-permute-done | bytes 131104 | tf_op jit(solution)/shard_map/ppermute | solution.py:428
  20.7 0.0 collective-permute-done.refs_1_
  20.7 0.6 copy-done.13
  21.4 0.7 copy-done.14
  22.1 11.2 %shard_map.69 = (bf16[512,512]{1,0:T(8,128)(2,1)}, bf16[4,8,32,16,128]{4,3,2,1,0:T(8,128)(2,1)}, bf16[2,8,32,16,128]{4,3,2,1,0:T(8,128)(2,1)}, bf16[2,8,32,16,12...) custom-call(f32[2,1,512]{2,1,0:T(1,128)} %convert_element_type.20.ma, ...), custom_call_target="tpu_custom_call" | custom-call | flops 4000000000 | bytes 12000000 | tf_op jit(solution)/shard_map/pallas_call | solution.py:96
  33.3 0.3 collective-permute-start.7
  33.6 0.3 collective-permute-start.4
  33.9 0.2 collective-permute-start.5
  34.1 0.8 collective-permute-start.6
  35.0 8.9 %collective-permute-done.4.refs_2_ = bf16[2,8,32,16,128]{4,3,2,1,0:T(8,128)(2,1)} collective-permute-done((bf16[2,8,32,16,128]{4,3,2,1,0:T(8,128)(2,1)}, bf16[2,8,32,16,128]{4,3,2,1,0:T(8,128)(2,1)}, u32[]{:S(2)}, u32[]{:S(2)}) %collective-permute-start.4) | collective-permute-done | bytes 2097184 | tf_op jit(solution)/shard_map/ppermute | solution.py:439
  43.8 3.0 %collective-permute-done.5.refs_3_ = bf16[2,8,32,16,128]{4,3,2,1,0:T(8,128)(2,1)} collective-permute-done((bf16[2,8,32,16,128]{4,3,2,1,0:T(8,128)(2,1)}, bf16[2,8,32,16,128]{4,3,2,1,0:T(8,128)(2,1)}, u32[]{:S(2)}, u32[]{:S(2)}) %collective-permute-start.5) | collective-permute-done | bytes 2097184 | tf_op jit(solution)/shard_map/ppermute | solution.py:439
  46.8 0.0 collective-permute-done.3.raw
  46.8 1.6 %copy-done.1 = bf16[2,8,32,16,128]{4,3,2,1,0:T(8,128)(2,1)S(1)} copy-done((bf16[2,8,32,16,128]{4,3,2,1,0:T(8,128)(2,1)S(1)}, bf16[2,8,32,16,128]{4,3,2,1,0:T(8,128)(2,1)}, u32[]{:S(2)}) %copy-start.1) | copy-done | bytes 2097176
  48.4 1.6 %copy-done.2 = bf16[2,8,32,16,128]{4,3,2,1,0:T(8,128)(2,1)S(1)} copy-done((bf16[2,8,32,16,128]{4,3,2,1,0:T(8,128)(2,1)S(1)}, bf16[2,8,32,16,128]{4,3,2,1,0:T(8,128)(2,1)}, u32[]{:S(2)}) %copy-start.2) | copy-done | bytes 2097176
  50.0 1.0 copy-done.3
  51.1 10.5 %shard_map.70 = (bf16[128,64,512]{2,1,0:T(8,128)(2,1)}, f32[64,64]{1,0:T(8,128)S(1)}) custom-call(bf16[128,384]{1,0:T(8,128)(2,1)S(1)} %maximum_select_fusion.metric_ref.refs_0_, bf16[512,512]{1,0:T(8,128)(2,1)S(1)} %copy-done.3, bf16[128,32,512]{2,1,0:T(8,128)(2,1)} %collective-permute-done.3.raw, bf16[2,8,32,16,128]{4,3,2,1,0:T(8,128)(2,1)S(1)} %copy-done.1, ...), custom_call_target="tpu_custom_call" | custom-call | flops 1200000000 | bytes 3600000 | tf_op jit(solution)/shard_map/pallas_call | solution.py:249
  61.6 0.7 collective-permute-start.8
  62.4 0.7 collective-permute-start.9
  63.1 7.4 %shard_map.71 = (bf16[128,64,512]{2,1,0:T(8,128)(2,1)}, f32[64,64]{1,0:T(8,128)S(1)}) custom-call(bf16[128,384]{1,0:T(8,128)(2,1)S(1)} %maximum_select_fusion.metric_ref.refs_0_, f32[2,1,512]{2,1,0:T(1,128)S(1)} %copy-done.4, f32[64,64]{1,0:T(8,128)S(1)} %get-tuple-element.31.refs_2_, ...), custom_call_target="tpu_custom_call", output_to_operand_aliasing={{0}: (7, {})} | custom-call | flops 1200000000 | bytes 3600000 | tf_op jit(solution)/shard_map/pallas_call | solution.py:368
  70.5 0.7 collective-permute-start.10
  71.2 5.2 %shard_map.72 = (bf16[128,64,512]{2,1,0:T(8,128)(2,1)}, f32[64,64]{1,0:T(8,128)S(1)}) custom-call(bf16[128,384]{1,0:T(8,128)(2,1)S(1)} %maximum_select_fusion.metric_ref.refs_0_, f32[2,1,512]{2,1,0:T(1,128)S(1)} %copy-done.4, f32[64,64]{1,0:T(8,128)S(1)} %get-tuple-element.35.refs_2_, ...), custom_call_target="tpu_custom_call", output_to_operand_aliasing={{0}: (7, {})} | custom-call | flops 1200000000 | bytes 3600000 | tf_op jit(solution)/shard_map/pallas_call | solution.py:368
  76.5 0.0 collective-permute-done.9.refs_3_
  76.5 4.6 %shard_map.73 = (bf16[128,64,512]{2,1,0:T(8,128)(2,1)}, f32[64,64]{1,0:T(8,128)S(1)}, bf16[1,8,32,16,128]{4,3,2,1,0:T(8,128)(2,1)S(1)}, bf16[1,8,32,16,128]{4,3,...) custom-call(bf16[128,384]{1,0:T(8,128)(2,1)S(1)} %maximum_select_fusion.metric_ref.refs_0_, ...), custom_call_target="tpu_custom_call", output_to_operand_aliasing={{0}: (7, {})} | custom-call | flops 1200000000 | bytes 3600000 | tf_op jit(solution)/shard_map/pallas_call | solution.py:368
  81.1 0.0 collective-permute-done.10.refs_3_
  81.1 2.2 %shard_map.74 = (bf16[128,64,512]{2,1,0:T(8,128)(2,1)}, f32[64,64]{1,0:T(8,128)S(1)}) custom-call(bf16[128,384]{1,0:T(8,128)(2,1)S(1)} %maximum_select_fusion.metric_ref.refs_0_, f32[2,1,512]{2,1,0:T(1,128)S(1)} %copy-done.4, f32[64,64]{1,0:T(8,128)S(1)} %get-tuple-element.43.refs_2_, ...), custom_call_target="tpu_custom_call", output_to_operand_aliasing={{0}: (7, {})} | custom-call | flops 1200000000 | bytes 3600000 | tf_op jit(solution)/shard_map/pallas_call | solution.py:368
  83.3 18.8 %collective-permute-start.11 = (f32[64,64]{1,0:T(8,128)S(1)}, f32[64,64]{1,0:T(8,128)S(1)}, u32[]{:S(2)}, u32[]{:S(2)}) collective-permute-start(f32[64,64]{1,0:T(8,128)S(1)} %get-tuple-element.51), channel_id=1, source_target_pairs={{0,4},{4,0},{8,12},{12,8},{16,20},{20,16},{24,28},{28,24},{32,36},... | collective-permute-start | bytes 49160 | tf_op jit(solution)/shard_map/ppermute | solution.py:399
  102.1 0.9 collective-permute-done.11
  103.0 4.8 %collective-permute-start.14 = (f32[64,64]{1,0:T(8,128)S(1)}, f32[64,64]{1,0:T(8,128)S(1)}, u32[]{:S(2)}, u32[]{:S(2)}) collective-permute-start(f32[64,64]{1,0:T(8,128)S(1)} %add.26), channel_id=1, source_target_pairs={{0,24},{4,28},{8,0},{12,4},{16,8},{20,12},{24,16},{28,20},{32,56},... | collective-permute-start | bytes 49160 | tf_op jit(solution)/shard_map/ppermute | solution.py:399
  107.8 1.5 %collective-permute-start.12 = (f32[64,64]{1,0:T(8,128)S(1)}, f32[64,64]{1,0:T(8,128)S(1)}, u32[]{:S(2)}, u32[]{:S(2)}) collective-permute-start(f32[64,64]{1,0:T(8,128)S(1)} %add.26), channel_id=1, source_target_pairs={{0,16},{4,20},{8,24},{12,28},{16,0},{20,4},{24,8},{28,12},{32,48},... | collective-permute-start | bytes 49160 | tf_op jit(solution)/shard_map/ppermute | solution.py:399
  109.3 0.1 collective-permute-done.14
  109.4 3.9 %collective-permute-done.13 = f32[64,64]{1,0:T(8,128)S(1)} collective-permute-done((f32[64,64]{1,0:T(8,128)S(1)}, f32[64,64]{1,0:T(8,128)S(1)}, u32[]{:S(2)}, u32[]{:S(2)}) %collective-permute-start.13) | collective-permute-done | bytes 16416 | tf_op jit(solution)/shard_map/ppermute | solution.py:399
  113.3 2.8 %collective-permute-start.17 = (f32[64,64]{1,0:T(8,128)S(1)}, f32[64,64]{1,0:T(8,128)S(1)}, u32[]{:S(2)}, u32[]{:S(2)}) collective-permute-start(f32[64,64]{1,0:T(8,128)S(1)} %add_add_fusion), channel_id=1, source_target_pairs={{0,96},{4,100},{8,104},{12,108},{16,112},{20,116},{24,120},{28,124... | collective-permute-start | bytes 49160 | tf_op jit(solution)/shard_map/ppermute | solution.py:399
  116.1 2.5 %collective-permute-start.15 = (f32[64,64]{1,0:T(8,128)S(1)}, f32[64,64]{1,0:T(8,128)S(1)}, u32[]{:S(2)}, u32[]{:S(2)}) collective-permute-start(f32[64,64]{1,0:T(8,128)S(1)} %add_add_fusion), channel_id=1, source_target_pairs={{0,64},{4,68},{8,72},{12,76},{16,80},{20,84},{24,88},{28,92},{32,9... | collective-permute-start | bytes 49160 | tf_op jit(solution)/shard_map/ppermute | solution.py:399
  118.6 2.7 %collective-permute-done.16 = f32[64,64]{1,0:T(8,128)S(1)} collective-permute-done((f32[64,64]{1,0:T(8,128)S(1)}, f32[64,64]{1,0:T(8,128)S(1)}, u32[]{:S(2)}, u32[]{:S(2)}) %collective-permute-start.16) | collective-permute-done | bytes 16416 | tf_op jit(solution)/shard_map/ppermute | solution.py:399
  121.2 0.3 collective-permute-done.15
  121.6 0.6 add_multiply_fusion
  (42 shorter events, 0.2 us)
Async XLA Ops:
  0.6 14.0 %copy-start.8 = (s32[2,1,8]{2,1,0:T(1,128)S(1)}, s32[2,1,8]{2,1,0:T(1,128)}, u32[]{:S(2)}) copy-start(s32[2,1,8]{2,1,0:T(1,128)} %mask_ref.1) | copy-start | bytes 196
  0.6 6.9 %copy-start.15 = (s32[2,8]{1,0:T(2,128)S(1)}, s32[2,8]{1,0:T(2,128)}, u32[]{:S(2)}) copy-start(s32[2,8]{1,0:T(2,128)} %param.8) | copy-start | bytes 196
  0.7 7.3 %copy-start.6 = (bf16[128,512]{1,0:T(8,128)(2,1)S(1)}, bf16[128,512]{1,0:T(8,128)(2,1)}, u32[]{:S(2)}) copy-start(bf16[128,512]{1,0:T(8,128)(2,1)} %param.7) | copy-start | bytes 393220
  4.9 42.0 %collective-permute-start.3 = (bf16[128,32,512]{2,1,0:T(8,128)(2,1)}, bf16[128,32,512]{2,1,0:T(8,128)(2,1)}, u32[]{:S(2)}, u32[]{:S(2)}) collective-permute-start(bf16[128,32,512]{2,1,0:T(8,128)(2,1)} %shard_map.68), channel_id=1, source_target_pairs={{4,8},{8,4},{12,16},{16,12},{20,24},{24,20},{28,32},{32,28},{36,40... | collective-permute-start | bytes 12582920 | tf_op jit(solution)/shard_map/ppermute | solution.py:419
  8.0 12.7 %copy-start.7 = (bf16[128,512]{1,0:T(8,128)(2,1)}, bf16[128,512]{1,0:T(8,128)(2,1)S(1)}, u32[]{:S(2)}) copy-start(bf16[128,512]{1,0:T(8,128)(2,1)S(1)} %mul.9.refs_0_) | copy-start | bytes 393220
  8.0 8.3 %collective-permute-start.2 = (bf16[128,512]{1,0:T(8,128)(2,1)S(1)}, bf16[128,512]{1,0:T(8,128)(2,1)S(1)}, u32[]{:S(2)}, u32[]{:S(2)}) collective-permute-start(bf16[128,512]{1,0:T(8,128)(2,1)S(1)} %mul.9.refs_0_), channel_id=1, source_target_pairs={{3,0},{0,1},{1,2},{2,3},{7,4},{4,5},{5,6},{6,7},{11,8},{8,9},{9,10... | collective-permute-start | bytes 393224 | tf_op jit(solution)/shard_map/ppermute | solution.py:428
  10.1 10.7 %collective-permute-start.1 = (bf16[128,512]{1,0:T(8,128)(2,1)S(1)}, bf16[128,512]{1,0:T(8,128)(2,1)S(1)}, u32[]{:S(2)}, u32[]{:S(2)}) collective-permute-start(bf16[128,512]{1,0:T(8,128)(2,1)S(1)} %mul.9.refs_0_), channel_id=1, source_target_pairs={{2,0},{3,1},{0,2},{1,3},{6,4},{7,5},{4,6},{5,7},{10,8},{11,9},{8,1... | collective-permute-start | bytes 393224 | tf_op jit(solution)/shard_map/ppermute | solution.py:428
  13.7 7.1 %collective-permute-start = (bf16[128,512]{1,0:T(8,128)(2,1)S(1)}, bf16[128,512]{1,0:T(8,128)(2,1)S(1)}, u32[]{:S(2)}, u32[]{:S(2)}) collective-permute-start(bf16[128,512]{1,0:T(8,128)(2,1)S(1)} %mul.9.refs_0_), channel_id=1, source_target_pairs={{1,0},{2,1},{3,2},{0,3},{5,4},{6,5},{7,6},{4,7},{9,8},{10,9},{11,1... | collective-permute-start | bytes 393224 | tf_op jit(solution)/shard_map/ppermute | solution.py:428
  15.4 19.5 %copy-start.5 = (bf16[128,384]{1,0:T(8,128)(2,1)S(1)}, bf16[128,384]{1,0:T(8,128)(2,1)}, u32[]{:S(2)}) copy-start(bf16[128,384]{1,0:T(8,128)(2,1)} %param.9) | copy-start | bytes 294916
  16.3 4.4 %copy-start.12 = (bf16[128,512]{1,0:T(8,128)(2,1)}, bf16[128,512]{1,0:T(8,128)(2,1)S(1)}, u32[]{:S(2)}) copy-start(bf16[128,512]{1,0:T(8,128)(2,1)S(1)} %collective-permute-done.2.refs_3_) | copy-start | bytes 393220
  20.7 0.7 copy-start.13
  21.4 0.7 copy-start.14
  33.3 29.8 %collective-permute-start.7 = (bf16[4,8,32,16,128]{4,3,2,1,0:T(8,128)(2,1)}, bf16[4,8,32,16,128]{4,3,2,1,0:T(8,128)(2,1)}, u32[]{:S(2)}, u32[]{:S(2)}) collective-permute-start(bf16[4,8,32,16,128]{4,3,2,1,0:T(8,128)(2,1)} %get-tuple-element.33.refs_4_), channel_id=1, source_target_pairs={{0,4},{4,0},{8,12},{12,8},{16,20},{20,16},{24,28},{28,24},{32,36},... | collective-permute-start | bytes 12582920 | tf_op jit(solution)/shard_map/ppermute | solution.py:439
  33.6 10.3 %collective-permute-start.4 = (bf16[2,8,32,16,128]{4,3,2,1,0:T(8,128)(2,1)}, bf16[2,8,32,16,128]{4,3,2,1,0:T(8,128)(2,1)}, u32[]{:S(2)}, u32[]{:S(2)}) collective-permute-start(bf16[2,8,32,16,128]{4,3,2,1,0:T(8,128)(2,1)} %get-tuple-element.29.refs_0_), channel_id=1, source_target_pairs={{0,4},{4,0},{8,12},{12,8},{16,20},{20,16},{24,28},{28,24},{32,36},... | collective-permute-start | bytes 6291464 | tf_op jit(solution)/shard_map/ppermute | solution.py:439
  33.9 13.0 %collective-permute-start.5 = (bf16[2,8,32,16,128]{4,3,2,1,0:T(8,128)(2,1)}, bf16[2,8,32,16,128]{4,3,2,1,0:T(8,128)(2,1)}, u32[]{:S(2)}, u32[]{:S(2)}) collective-permute-start(bf16[2,8,32,16,128]{4,3,2,1,0:T(8,128)(2,1)} %get-tuple-element.30.refs_1_), channel_id=1, source_target_pairs={{0,4},{4,0},{8,12},{12,8},{16,20},{20,16},{24,28},{28,24},{32,36},... | collective-permute-start | bytes 6291464 | tf_op jit(solution)/shard_map/ppermute | solution.py:439
  34.1 29.0 %collective-permute-start.6 = (bf16[2,8,32,16,128]{4,3,2,1,0:T(8,128)(2,1)}, bf16[2,8,32,16,128]{4,3,2,1,0:T(8,128)(2,1)S(1)}, u32[]{:S(2)}, u32[]{:S(2)}) collective-permute-start(bf16[2,8,32,16,128]{4,3,2,1,0:T(8,128)(2,1)} %get-tuple-element.32), channel_id=1, source_target_pairs={{4,8},{8,4},{12,16},{16,12},{20,24},{24,20},{28,32},{32,28},{36,40... | collective-permute-start | bytes 6291464 | tf_op jit(solution)/shard_map/ppermute | solution.py:419
  46.8 1.6 %copy-start.1 = (bf16[2,8,32,16,128]{4,3,2,1,0:T(8,128)(2,1)S(1)}, bf16[2,8,32,16,128]{4,3,2,1,0:T(8,128)(2,1)}, u32[]{:S(2)}) copy-start(bf16[2,8,32,16,128]{4,3,2,1,0:T(8,128)(2,1)} %get-tuple-element.29.refs_0_) | copy-start | bytes 6291460
  48.4 1.6 %copy-start.2 = (bf16[2,8,32,16,128]{4,3,2,1,0:T(8,128)(2,1)S(1)}, bf16[2,8,32,16,128]{4,3,2,1,0:T(8,128)(2,1)}, u32[]{:S(2)}) copy-start(bf16[2,8,32,16,128]{4,3,2,1,0:T(8,128)(2,1)} %get-tuple-element.30.refs_1_) | copy-start | bytes 6291460
  50.0 1.0 copy-start.3
  51.1 10.6 %copy-start.9 = (bf16[1,8,32,16,128]{4,3,2,1,0:T(8,128)(2,1)S(1)}, bf16[1,8,32,16,128]{4,3,2,1,0:T(8,128)(2,1)}, u32[]{:S(2)}) copy-start(bf16[1,8,32,16,128]{4,3,2,1,0:T(8,128)(2,1)} %get-tuple-element.37) | copy-start | bytes 3145732
  51.1 11.3 %copy-start.11 = (bf16[1,8,16,16,128]{4,3,2,1,0:T(8,128)(2,1)S(1)}, bf16[1,8,16,16,128]{4,3,2,1,0:T(8,128)(2,1)}, u32[]{:S(2)}) copy-start(bf16[1,8,16,16,128]{4,3,2,1,0:T(8,128)(2,1)} %get-tuple-element.41) | copy-start | bytes 1572868
  51.1 12.0 %copy-start = (bf16[4,8,32,16,128]{4,3,2,1,0:T(8,128)(2,1)S(1)}, bf16[4,8,32,16,128]{4,3,2,1,0:T(8,128)(2,1)}, u32[]{:S(2)}) copy-start(bf16[4,8,32,16,128]{4,3,2,1,0:T(8,128)(2,1)} %get-tuple-element.33.refs_4_) | copy-start | bytes 12582916
  51.1 12.0 %copy-start.4 = (f32[2,1,512]{2,1,0:T(1,128)S(1)}, f32[2,1,512]{2,1,0:T(1,128)}, u32[]{:S(2)}) copy-start(f32[2,1,512]{2,1,0:T(1,128)} %convert_element_type.20.mask_ref.refs_1_) | copy-start | bytes 12292
  61.6 9.6 %collective-permute-start.8 = (bf16[1,8,32,16,128]{4,3,2,1,0:T(8,128)(2,1)S(1)}, bf16[1,8,32,16,128]{4,3,2,1,0:T(8,128)(2,1)S(1)}, u32[]{:S(2)}, u32[]{:S(2)}) collective-permute-start(bf16[1,8,32,16,128]{4,3,2,1,0:T(8,128)(2,1)S(1)} %copy-done.9), channel_id=1, source_target_pairs={{4,8},{8,4},{12,16},{16,12},{20,24},{24,20},{28,32},{32,28},{36,40... | collective-permute-start | bytes 3145736 | tf_op jit(solution)/shard_map/ppermute | solution.py:419
  62.4 14.1 %collective-permute-start.9 = (bf16[1,8,16,16,128]{4,3,2,1,0:T(8,128)(2,1)S(1)}, bf16[1,8,16,16,128]{4,3,2,1,0:T(8,128)(2,1)S(1)}, u32[]{:S(2)}, u32[]{:S(2)}) collective-permute-start(bf16[1,8,16,16,128]{4,3,2,1,0:T(8,128)(2,1)S(1)} %copy-done.11), channel_id=1, source_target_pairs={{4,8},{8,4},{12,16},{16,12},{20,24},{24,20},{28,32},{32,28},{36,40... | collective-permute-start | bytes 1572872 | tf_op jit(solution)/shard_map/ppermute | solution.py:419
  63.1 7.4 %copy-start.10 = (bf16[1,8,16,16,128]{4,3,2,1,0:T(8,128)(2,1)S(1)}, bf16[1,8,16,16,128]{4,3,2,1,0:T(8,128)(2,1)}, u32[]{:S(2)}) copy-start(bf16[1,8,16,16,128]{4,3,2,1,0:T(8,128)(2,1)} %get-tuple-element.45) | copy-start | bytes 1572868
  70.5 10.6 %collective-permute-start.10 = (bf16[1,8,16,16,128]{4,3,2,1,0:T(8,128)(2,1)S(1)}, bf16[1,8,16,16,128]{4,3,2,1,0:T(8,128)(2,1)S(1)}, u32[]{:S(2)}, u32[]{:S(2)}) collective-permute-start(bf16[1,8,16,16,128]{4,3,2,1,0:T(8,128)(2,1)S(1)} %copy-done.10), channel_id=1, source_target_pairs={{4,8},{8,4},{12,16},{16,12},{20,24},{24,20},{28,32},{32,28},{36,40... | collective-permute-start | bytes 1572872 | tf_op jit(solution)/shard_map/ppermute | solution.py:419
  83.3 19.7 %collective-permute-start.11 = (f32[64,64]{1,0:T(8,128)S(1)}, f32[64,64]{1,0:T(8,128)S(1)}, u32[]{:S(2)}, u32[]{:S(2)}) collective-permute-start(f32[64,64]{1,0:T(8,128)S(1)} %get-tuple-element.51), channel_id=1, source_target_pairs={{0,4},{4,0},{8,12},{12,8},{16,20},{20,16},{24,28},{28,24},{32,36},... | collective-permute-start | bytes 49160 | tf_op jit(solution)/shard_map/ppermute | solution.py:399
  103.0 6.4 %collective-permute-start.14 = (f32[64,64]{1,0:T(8,128)S(1)}, f32[64,64]{1,0:T(8,128)S(1)}, u32[]{:S(2)}, u32[]{:S(2)}) collective-permute-start(f32[64,64]{1,0:T(8,128)S(1)} %add.26), channel_id=1, source_target_pairs={{0,24},{4,28},{8,0},{12,4},{16,8},{20,12},{24,16},{28,20},{32,56},... | collective-permute-start | bytes 49160 | tf_op jit(solution)/shard_map/ppermute | solution.py:399
  107.8 5.5 %collective-permute-start.13 = (f32[64,64]{1,0:T(8,128)S(1)}, f32[64,64]{1,0:T(8,128)S(1)}, u32[]{:S(2)}, u32[]{:S(2)}) collective-permute-start(f32[64,64]{1,0:T(8,128)S(1)} %add.26), channel_id=1, source_target_pairs={{0,8},{4,12},{8,16},{12,20},{16,24},{20,28},{24,0},{28,4},{32,40},... | collective-permute-start | bytes 49160 | tf_op jit(solution)/shard_map/ppermute | solution.py:399
  107.8 5.5 %collective-permute-start.12 = (f32[64,64]{1,0:T(8,128)S(1)}, f32[64,64]{1,0:T(8,128)S(1)}, u32[]{:S(2)}, u32[]{:S(2)}) collective-permute-start(f32[64,64]{1,0:T(8,128)S(1)} %add.26), channel_id=1, source_target_pairs={{0,16},{4,20},{8,24},{12,28},{16,0},{20,4},{24,8},{28,12},{32,48},... | collective-permute-start | bytes 49160 | tf_op jit(solution)/shard_map/ppermute | solution.py:399
  113.3 5.3 %collective-permute-start.17 = (f32[64,64]{1,0:T(8,128)S(1)}, f32[64,64]{1,0:T(8,128)S(1)}, u32[]{:S(2)}, u32[]{:S(2)}) collective-permute-start(f32[64,64]{1,0:T(8,128)S(1)} %add_add_fusion), channel_id=1, source_target_pairs={{0,96},{4,100},{8,104},{12,108},{16,112},{20,116},{24,120},{28,124... | collective-permute-start | bytes 49160 | tf_op jit(solution)/shard_map/ppermute | solution.py:399
  116.1 5.1 %collective-permute-start.16 = (f32[64,64]{1,0:T(8,128)S(1)}, f32[64,64]{1,0:T(8,128)S(1)}, u32[]{:S(2)}, u32[]{:S(2)}) collective-permute-start(f32[64,64]{1,0:T(8,128)S(1)} %add_add_fusion), channel_id=1, source_target_pairs={{0,32},{4,36},{8,40},{12,44},{16,48},{20,52},{24,56},{28,60},{32,6... | collective-permute-start | bytes 49160 | tf_op jit(solution)/shard_map/ppermute | solution.py:399
  116.1 5.5 %collective-permute-start.15 = (f32[64,64]{1,0:T(8,128)S(1)}, f32[64,64]{1,0:T(8,128)S(1)}, u32[]{:S(2)}, u32[]{:S(2)}) collective-permute-start(f32[64,64]{1,0:T(8,128)S(1)} %add_add_fusion), channel_id=1, source_target_pairs={{0,64},{4,68},{8,72},{12,76},{16,80},{20,84},{24,88},{28,92},{32,9... | collective-permute-start | bytes 49160 | tf_op jit(solution)/shard_map/ppermute | solution.py:399

commit v8 on v6

--- a/solution.py
+++ b/solution.py
@@ -390,10 +390,13 @@
 def sum_pa(value):
     size = lax.axis_size("pa")
 
-    for stride, mask in ((1, 1), (2, 1), (2, 3), (8, 1), (8, 3)):
-        pairs = [(i, i ^ (mask * stride)) for i in range(size)]
-        value = value + lax.ppermute(value, "pa", pairs)
-    return value
+    def swapped(value, mask):
+        return lax.ppermute(value, "pa", [(i, i ^ mask) for i in range(size)])
+
+    for first, second in ((1, 2), (6, 8)):
+        a, b, both = (swapped(value, mask) for mask in (first, second, first ^ second))
+        value = (value + a) + (b + both)
+    return value + swapped(value, 24)
 
 
 def after(value, *earlier):

time: 125 us -> 124 us (level)
  starting transfers between devices: 44.5 us -> 40.7 us
  waiting for transfers between devices: 25.8 us -> 28.9 us
    ppermute x5 -> x7, starting transfers between devices: 31.7 us -> 27.7 us  [swapped(): return lax.ppermute(value, 'pa', [(i, i ^ mask) for i in range(size)])]
    ppermute x5 -> x7, waiting for transfers between devices: 8.48 us -> 11.7 us  [swapped(): return lax.ppermute(value, 'pa', [(i, i ^ mask) for i in range(size)])]
  transfers between devices with their start and end apart: 16 -> 18, of which waited for: 9 -> 10; matrix products, arithmetic and copies ran while one was open for 1% -> 1% of each run, Pallas kernels for 31% -> 32%
where the time goes in v8:
time: 124 us; the launch traced here: 123 us
  Pallas kernels  45.3 us (37%)
  starting transfers between devices  40.7 us (33%)
  waiting for transfers between devices  28.9 us (23%)
  local copies, waits for them, and re-layouts  6.73 us (5%)
    ppermute x7, starting transfers between devices, swapped(): return lax.ppermute(value, 'pa', [(i, i ^ mask) for i in range(size)])  27.7 us
    pallas_call x4, Pallas kernels, fit_call(): pl.pallas_call(lambda *refs: fit_kernel(chunk, raws, role, *refs), in_spe...  19.4 us
    ppermute x3, waiting for transfers between devices, to_near(): return lax.ppermute(value, 'pa', near_pairs)  11.9 us
    ppermute x7, waiting for transfers between devices, swapped(): return lax.ppermute(value, 'pa', [(i, i ^ mask) for i in range(size)])  11.7 us
    pallas_call x1, Pallas kernels, half_call(): pl.pallas_call(half_kernel, in_specs=[WHOLE] * (1 + len(parts)) + [HBM],...  11.2 us
    pallas_call x1, Pallas kernels, raw_call(): pl.pallas_call(raw_kernel, in_specs=[WHOLE, WHOLE] + [HBM] * 5, out_specs...  10.5 us
    ppermute x3, starting transfers between devices, on_device(): lax.ppermute(local, 'mu', [((i + k) % count, i) for i in range(count)])  6.66 us
    unnamed x32, local copies, waits for them, and re-layouts  5.57 us
  transfers between devices with their start and end apart: 18, of which 10 were waited for; matrix products, arithmetic and copies ran while one was open for 1% of the time, Pallas kernels for 32%

profile of v8, /device:TPU:0, one launch (start us, length us, event | category | flops | bytes accessed | tf_op | source)
XLA Modules:
  0.0 123.3 jit_solution(15575320061163526650)
XLA Ops:
  0.7 4.2 %shard_map.68 = bf16[128,32,512]{2,1,0:T(8,128)(2,1)} custom-call(s32[2,1,8]{2,1,0:T(1,128)} %mask_ref.1, bf16[128,64,512]{2,1,0:T(8,128)(2,1)} %refs_6_.5), custom_call_target="tpu_custom_call" | custom-call | flops 1200000000 | bytes 3600000 | tf_op jit(solution)/shard_map/pallas_call | solution.py:154
  4.9 2.6 %collective-permute-start.3 = (bf16[128,32,512]{2,1,0:T(8,128)(2,1)}, bf16[128,32,512]{2,1,0:T(8,128)(2,1)}, u32[]{:S(2)}, u32[]{:S(2)}) collective-permute-start(bf16[128,32,512]{2,1,0:T(8,128)(2,1)} %shard_map.68), channel_id=1, source_target_pairs={{4,8},{8,4},{12,16},{16,12},{20,24},{24,20},{28,32},{32,28},{36,40... | collective-permute-start | bytes 12582920 | tf_op jit(solution)/shard_map/ppermute | solution.py:413
  7.5 0.1 copy.11
  7.6 0.1 broadcast_in_dim.10
  7.7 0.1 convert_element_type.22
  7.8 0.1 copy.12
  8.0 2.1 %collective-permute-start.2 = (bf16[128,512]{1,0:T(8,128)(2,1)S(1)}, bf16[128,512]{1,0:T(8,128)(2,1)S(1)}, u32[]{:S(2)}, u32[]{:S(2)}) collective-permute-start(bf16[128,512]{1,0:T(8,128)(2,1)S(1)} %mul.9.refs_0_), channel_id=1, source_target_pairs={{3,0},{0,1},{1,2},{2,3},{7,4},{4,5},{5,6},{6,7},{11,8},{8,9},{9,10... | collective-permute-start | bytes 393224 | tf_op jit(solution)/shard_map/ppermute | solution.py:422
  10.1 3.6 %collective-permute-start.1 = (bf16[128,512]{1,0:T(8,128)(2,1)S(1)}, bf16[128,512]{1,0:T(8,128)(2,1)S(1)}, u32[]{:S(2)}, u32[]{:S(2)}) collective-permute-start(bf16[128,512]{1,0:T(8,128)(2,1)S(1)} %mul.9.refs_0_), channel_id=1, source_target_pairs={{2,0},{3,1},{0,2},{1,3},{6,4},{7,5},{4,6},{5,7},{10,8},{11,9},{8,1... | collective-permute-start | bytes 393224 | tf_op jit(solution)/shard_map/ppermute | solution.py:422
  13.7 1.0 collective-permute-start
  14.7 0.1 broadcast_in_dim.9
  14.7 0.7 convert_element_type.20.mask_ref.refs_1_
  15.4 0.9 collective-permute-done.2.refs_3_
  16.3 4.4 %collective-permute-done.1.refs_2_ = bf16[128,512]{1,0:T(8,128)(2,1)S(1)} collective-permute-done((bf16[128,512]{1,0:T(8,128)(2,1)S(1)}, bf16[128,512]{1,0:T(8,128)(2,1)S(1)}, u32[]{:S(2)}, u32[]{:S(2)}) %collective-permute-start.1) | collective-permute-done | bytes 131104 | tf_op jit(solution)/shard_map/ppermute | solution.py:422
  20.7 0.6 copy-done.13
  21.4 0.7 copy-done.14
  22.1 11.2 %shard_map.69 = (bf16[512,512]{1,0:T(8,128)(2,1)}, bf16[4,8,32,16,128]{4,3,2,1,0:T(8,128)(2,1)}, bf16[2,8,32,16,128]{4,3,2,1,0:T(8,128)(2,1)}, bf16[2,8,32,16,12...) custom-call(f32[2,1,512]{2,1,0:T(1,128)} %convert_element_type.20.ma, ...), custom_call_target="tpu_custom_call" | custom-call | flops 4000000000 | bytes 12000000 | tf_op jit(solution)/shard_map/pallas_call | solution.py:96
  33.3 0.3 collective-permute-start.7
  33.6 0.3 collective-permute-start.4
  33.9 0.2 collective-permute-start.5
  34.1 0.8 collective-permute-start.6
  35.0 8.9 %collective-permute-done.4.refs_2_ = bf16[2,8,32,16,128]{4,3,2,1,0:T(8,128)(2,1)} collective-permute-done((bf16[2,8,32,16,128]{4,3,2,1,0:T(8,128)(2,1)}, bf16[2,8,32,16,128]{4,3,2,1,0:T(8,128)(2,1)}, u32[]{:S(2)}, u32[]{:S(2)}) %collective-permute-start.4) | collective-permute-done | bytes 2097184 | tf_op jit(solution)/shard_map/ppermute | solution.py:433
  43.8 3.0 %collective-permute-done.5.refs_3_ = bf16[2,8,32,16,128]{4,3,2,1,0:T(8,128)(2,1)} collective-permute-done((bf16[2,8,32,16,128]{4,3,2,1,0:T(8,128)(2,1)}, bf16[2,8,32,16,128]{4,3,2,1,0:T(8,128)(2,1)}, u32[]{:S(2)}, u32[]{:S(2)}) %collective-permute-start.5) | collective-permute-done | bytes 2097184 | tf_op jit(solution)/shard_map/ppermute | solution.py:433
  46.8 1.6 %copy-done.1 = bf16[2,8,32,16,128]{4,3,2,1,0:T(8,128)(2,1)S(1)} copy-done((bf16[2,8,32,16,128]{4,3,2,1,0:T(8,128)(2,1)S(1)}, bf16[2,8,32,16,128]{4,3,2,1,0:T(8,128)(2,1)}, u32[]{:S(2)}) %copy-start.1) | copy-done | bytes 2097176
  48.4 1.6 %copy-done.2 = bf16[2,8,32,16,128]{4,3,2,1,0:T(8,128)(2,1)S(1)} copy-done((bf16[2,8,32,16,128]{4,3,2,1,0:T(8,128)(2,1)S(1)}, bf16[2,8,32,16,128]{4,3,2,1,0:T(8,128)(2,1)}, u32[]{:S(2)}) %copy-start.2) | copy-done | bytes 2097176
  50.0 1.0 copy-done.3
  51.1 10.5 %shard_map.70 = (bf16[128,64,512]{2,1,0:T(8,128)(2,1)}, f32[64,64]{1,0:T(8,128)S(1)}) custom-call(bf16[128,384]{1,0:T(8,128)(2,1)S(1)} %maximum_select_fusion.metric_ref.refs_0_, bf16[512,512]{1,0:T(8,128)(2,1)S(1)} %copy-done.3, bf16[128,32,512]{2,1,0:T(8,128)(2,1)} %collective-permute-done.3.raw, bf16[2,8,32,16,128]{4,3,2,1,0:T(8,128)(2,1)S(1)} %copy-done.1, ...), custom_call_target="tpu_custom_call" | custom-call | flops 1200000000 | bytes 3600000 | tf_op jit(solution)/shard_map/pallas_call | solution.py:249
  61.6 0.7 collective-permute-start.8
  62.4 0.7 collective-permute-start.9
  63.1 0.0 collective-permute-done.6.refs_3_
  63.1 7.4 %shard_map.71 = (bf16[128,64,512]{2,1,0:T(8,128)(2,1)}, f32[64,64]{1,0:T(8,128)S(1)}) custom-call(bf16[128,384]{1,0:T(8,128)(2,1)S(1)} %maximum_select_fusion.metric_ref.refs_0_, f32[2,1,512]{2,1,0:T(1,128)S(1)} %copy-done.4, f32[64,64]{1,0:T(8,128)S(1)} %get-tuple-element.31.refs_2_, ...), custom_call_target="tpu_custom_call", output_to_operand_aliasing={{0}: (7, {})} | custom-call | flops 1200000000 | bytes 3600000 | tf_op jit(solution)/shard_map/pallas_call | solution.py:368
  70.5 0.7 collective-permute-start.10
  71.2 5.2 %shard_map.72 = (bf16[128,64,512]{2,1,0:T(8,128)(2,1)}, f32[64,64]{1,0:T(8,128)S(1)}) custom-call(bf16[128,384]{1,0:T(8,128)(2,1)S(1)} %maximum_select_fusion.metric_ref.refs_0_, f32[2,1,512]{2,1,0:T(1,128)S(1)} %copy-done.4, f32[64,64]{1,0:T(8,128)S(1)} %get-tuple-element.35.refs_2_, ...), custom_call_target="tpu_custom_call", output_to_operand_aliasing={{0}: (7, {})} | custom-call | flops 1200000000 | bytes 3600000 | tf_op jit(solution)/shard_map/pallas_call | solution.py:368
  76.5 4.6 %shard_map.73 = (bf16[128,64,512]{2,1,0:T(8,128)(2,1)}, f32[64,64]{1,0:T(8,128)S(1)}, bf16[1,8,32,16,128]{4,3,2,1,0:T(8,128)(2,1)S(1)}, bf16[1,8,32,16,128]{4,3,...) custom-call(bf16[128,384]{1,0:T(8,128)(2,1)S(1)} %maximum_select_fusion.metric_ref.refs_0_, ...), custom_call_target="tpu_custom_call", output_to_operand_aliasing={{0}: (7, {})} | custom-call | flops 1200000000 | bytes 3600000 | tf_op jit(solution)/shard_map/pallas_call | solution.py:368
  81.1 2.2 %shard_map.74 = (bf16[128,64,512]{2,1,0:T(8,128)(2,1)}, f32[64,64]{1,0:T(8,128)S(1)}) custom-call(bf16[128,384]{1,0:T(8,128)(2,1)S(1)} %maximum_select_fusion.metric_ref.refs_0_, f32[2,1,512]{2,1,0:T(1,128)S(1)} %copy-done.4, f32[64,64]{1,0:T(8,128)S(1)} %get-tuple-element.43.refs_2_, ...), custom_call_target="tpu_custom_call", output_to_operand_aliasing={{0}: (7, {})} | custom-call | flops 1200000000 | bytes 3600000 | tf_op jit(solution)/shard_map/pallas_call | solution.py:368
  83.3 20.1 %collective-permute-start.13 = (f32[64,64]{1,0:T(8,128)S(1)}, f32[64,64]{1,0:T(8,128)S(1)}, u32[]{:S(2)}, u32[]{:S(2)}) collective-permute-start(f32[64,64]{1,0:T(8,128)S(1)} %get-tuple-element.51), channel_id=1, source_target_pairs={{0,12},{4,8},{8,4},{12,0},{16,28},{20,24},{24,20},{28,16},{32,44},... | collective-permute-start | bytes 49160 | tf_op jit(solution)/shard_map/ppermute | solution.py:394
  103.4 0.4 collective-permute-start.12
  103.8 0.0 collective-permute-start.11
  103.8 1.4 %collective-permute-done.13 = f32[64,64]{1,0:T(8,128)S(1)} collective-permute-done((f32[64,64]{1,0:T(8,128)S(1)}, f32[64,64]{1,0:T(8,128)S(1)}, u32[]{:S(2)}, u32[]{:S(2)}) %collective-permute-start.13) | collective-permute-done | bytes 16416 | tf_op jit(solution)/shard_map/ppermute | solution.py:394
  105.2 2.2 %collective-permute-done.12 = f32[64,64]{1,0:T(8,128)S(1)} collective-permute-done((f32[64,64]{1,0:T(8,128)S(1)}, f32[64,64]{1,0:T(8,128)S(1)}, u32[]{:S(2)}, u32[]{:S(2)}) %collective-permute-start.12) | collective-permute-done | bytes 16416 | tf_op jit(solution)/shard_map/ppermute | solution.py:394
  107.4 4.5 %collective-permute-start.16 = (f32[64,64]{1,0:T(8,128)S(1)}, f32[64,64]{1,0:T(8,128)S(1)}, u32[]{:S(2)}, u32[]{:S(2)}) collective-permute-start(f32[64,64]{1,0:T(8,128)S(1)} %add_add_fusion.1), channel_id=1, source_target_pairs={{0,56},{4,60},{8,48},{12,52},{16,40},{20,44},{24,32},{28,36},{32,2... | collective-permute-start | bytes 49160 | tf_op jit(solution)/shard_map/ppermute | solution.py:394
  111.9 0.5 collective-permute-start.15
  112.3 0.4 collective-permute-start.14
  112.7 1.1 collective-permute-done.16
  113.8 2.0 %collective-permute-done.15 = f32[64,64]{1,0:T(8,128)S(1)} collective-permute-done((f32[64,64]{1,0:T(8,128)S(1)}, f32[64,64]{1,0:T(8,128)S(1)}, u32[]{:S(2)}, u32[]{:S(2)}) %collective-permute-start.15) | collective-permute-done | bytes 16416 | tf_op jit(solution)/shard_map/ppermute | solution.py:394
  115.8 1.7 %collective-permute-done.14 = f32[64,64]{1,0:T(8,128)S(1)} collective-permute-done((f32[64,64]{1,0:T(8,128)S(1)}, f32[64,64]{1,0:T(8,128)S(1)}, u32[]{:S(2)}, u32[]{:S(2)}) %collective-permute-start.14) | collective-permute-done | bytes 16416 | tf_op jit(solution)/shard_map/ppermute | solution.py:394
  117.5 1.8 %collective-permute-start.17 = (f32[64,64]{1,0:T(8,128)S(1)}, f32[64,64]{1,0:T(8,128)S(1)}, u32[]{:S(2)}, u32[]{:S(2)}) collective-permute-start(f32[64,64]{1,0:T(8,128)S(1)} %add_add_fusion), channel_id=1, source_target_pairs={{0,96},{4,100},{8,104},{12,108},{16,112},{20,116},{24,120},{28,124... | collective-permute-start | bytes 49160 | tf_op jit(solution)/shard_map/ppermute | solution.py:394
  119.3 3.4 %collective-permute-done.17 = f32[64,64]{1,0:T(8,128)S(1)} collective-permute-done((f32[64,64]{1,0:T(8,128)S(1)}, f32[64,64]{1,0:T(8,128)S(1)}, u32[]{:S(2)}, u32[]{:S(2)}) %collective-permute-start.17) | collective-permute-done | bytes 16416 | tf_op jit(solution)/shard_map/ppermute | solution.py:394
  122.7 0.6 add_multiply_fusion
  (42 shorter events, 0.2 us)
Async XLA Ops:
  0.6 14.0 %copy-start.8 = (s32[2,1,8]{2,1,0:T(1,128)S(1)}, s32[2,1,8]{2,1,0:T(1,128)}, u32[]{:S(2)}) copy-start(s32[2,1,8]{2,1,0:T(1,128)} %mask_ref.1) | copy-start | bytes 196
  0.6 6.9 %copy-start.15 = (s32[2,8]{1,0:T(2,128)S(1)}, s32[2,8]{1,0:T(2,128)}, u32[]{:S(2)}) copy-start(s32[2,8]{1,0:T(2,128)} %param.8) | copy-start | bytes 196
  0.7 7.3 %copy-start.6 = (bf16[128,512]{1,0:T(8,128)(2,1)S(1)}, bf16[128,512]{1,0:T(8,128)(2,1)}, u32[]{:S(2)}) copy-start(bf16[128,512]{1,0:T(8,128)(2,1)} %param.7) | copy-start | bytes 393220
  4.9 42.0 %collective-permute-start.3 = (bf16[128,32,512]{2,1,0:T(8,128)(2,1)}, bf16[128,32,512]{2,1,0:T(8,128)(2,1)}, u32[]{:S(2)}, u32[]{:S(2)}) collective-permute-start(bf16[128,32,512]{2,1,0:T(8,128)(2,1)} %shard_map.68), channel_id=1, source_target_pairs={{4,8},{8,4},{12,16},{16,12},{20,24},{24,20},{28,32},{32,28},{36,40... | collective-permute-start | bytes 12582920 | tf_op jit(solution)/shard_map/ppermute | solution.py:413
  8.0 12.7 %copy-start.7 = (bf16[128,512]{1,0:T(8,128)(2,1)}, bf16[128,512]{1,0:T(8,128)(2,1)S(1)}, u32[]{:S(2)}) copy-start(bf16[128,512]{1,0:T(8,128)(2,1)S(1)} %mul.9.refs_0_) | copy-start | bytes 393220
  8.0 8.3 %collective-permute-start.2 = (bf16[128,512]{1,0:T(8,128)(2,1)S(1)}, bf16[128,512]{1,0:T(8,128)(2,1)S(1)}, u32[]{:S(2)}, u32[]{:S(2)}) collective-permute-start(bf16[128,512]{1,0:T(8,128)(2,1)S(1)} %mul.9.refs_0_), channel_id=1, source_target_pairs={{3,0},{0,1},{1,2},{2,3},{7,4},{4,5},{5,6},{6,7},{11,8},{8,9},{9,10... | collective-permute-start | bytes 393224 | tf_op jit(solution)/shard_map/ppermute | solution.py:422
  10.1 10.7 %collective-permute-start.1 = (bf16[128,512]{1,0:T(8,128)(2,1)S(1)}, bf16[128,512]{1,0:T(8,128)(2,1)S(1)}, u32[]{:S(2)}, u32[]{:S(2)}) collective-permute-start(bf16[128,512]{1,0:T(8,128)(2,1)S(1)} %mul.9.refs_0_), channel_id=1, source_target_pairs={{2,0},{3,1},{0,2},{1,3},{6,4},{7,5},{4,6},{5,7},{10,8},{11,9},{8,1... | collective-permute-start | bytes 393224 | tf_op jit(solution)/shard_map/ppermute | solution.py:422
  13.7 7.1 %collective-permute-start = (bf16[128,512]{1,0:T(8,128)(2,1)S(1)}, bf16[128,512]{1,0:T(8,128)(2,1)S(1)}, u32[]{:S(2)}, u32[]{:S(2)}) collective-permute-start(bf16[128,512]{1,0:T(8,128)(2,1)S(1)} %mul.9.refs_0_), channel_id=1, source_target_pairs={{1,0},{2,1},{3,2},{0,3},{5,4},{6,5},{7,6},{4,7},{9,8},{10,9},{11,1... | collective-permute-start | bytes 393224 | tf_op jit(solution)/shard_map/ppermute | solution.py:422
  15.4 19.5 %copy-start.5 = (bf16[128,384]{1,0:T(8,128)(2,1)S(1)}, bf16[128,384]{1,0:T(8,128)(2,1)}, u32[]{:S(2)}) copy-start(bf16[128,384]{1,0:T(8,128)(2,1)} %param.9) | copy-start | bytes 294916
  16.3 4.4 %copy-start.12 = (bf16[128,512]{1,0:T(8,128)(2,1)}, bf16[128,512]{1,0:T(8,128)(2,1)S(1)}, u32[]{:S(2)}) copy-start(bf16[128,512]{1,0:T(8,128)(2,1)S(1)} %collective-permute-done.2.refs_3_) | copy-start | bytes 393220
  20.7 0.7 copy-start.13
  21.4 0.7 copy-start.14
  33.3 29.8 %collective-permute-start.7 = (bf16[4,8,32,16,128]{4,3,2,1,0:T(8,128)(2,1)}, bf16[4,8,32,16,128]{4,3,2,1,0:T(8,128)(2,1)}, u32[]{:S(2)}, u32[]{:S(2)}) collective-permute-start(bf16[4,8,32,16,128]{4,3,2,1,0:T(8,128)(2,1)} %get-tuple-element.33.refs_4_), channel_id=1, source_target_pairs={{0,4},{4,0},{8,12},{12,8},{16,20},{20,16},{24,28},{28,24},{32,36},... | collective-permute-start | bytes 12582920 | tf_op jit(solution)/shard_map/ppermute | solution.py:433
  33.6 10.3 %collective-permute-start.4 = (bf16[2,8,32,16,128]{4,3,2,1,0:T(8,128)(2,1)}, bf16[2,8,32,16,128]{4,3,2,1,0:T(8,128)(2,1)}, u32[]{:S(2)}, u32[]{:S(2)}) collective-permute-start(bf16[2,8,32,16,128]{4,3,2,1,0:T(8,128)(2,1)} %get-tuple-element.29.refs_0_), channel_id=1, source_target_pairs={{0,4},{4,0},{8,12},{12,8},{16,20},{20,16},{24,28},{28,24},{32,36},... | collective-permute-start | bytes 6291464 | tf_op jit(solution)/shard_map/ppermute | solution.py:433
  33.9 13.0 %collective-permute-start.5 = (bf16[2,8,32,16,128]{4,3,2,1,0:T(8,128)(2,1)}, bf16[2,8,32,16,128]{4,3,2,1,0:T(8,128)(2,1)}, u32[]{:S(2)}, u32[]{:S(2)}) collective-permute-start(bf16[2,8,32,16,128]{4,3,2,1,0:T(8,128)(2,1)} %get-tuple-element.30.refs_1_), channel_id=1, source_target_pairs={{0,4},{4,0},{8,12},{12,8},{16,20},{20,16},{24,28},{28,24},{32,36},... | collective-permute-start | bytes 6291464 | tf_op jit(solution)/shard_map/ppermute | solution.py:433
  34.1 29.0 %collective-permute-start.6 = (bf16[2,8,32,16,128]{4,3,2,1,0:T(8,128)(2,1)}, bf16[2,8,32,16,128]{4,3,2,1,0:T(8,128)(2,1)S(1)}, u32[]{:S(2)}, u32[]{:S(2)}) collective-permute-start(bf16[2,8,32,16,128]{4,3,2,1,0:T(8,128)(2,1)} %get-tuple-element.32), channel_id=1, source_target_pairs={{4,8},{8,4},{12,16},{16,12},{20,24},{24,20},{28,32},{32,28},{36,40... | collective-permute-start | bytes 6291464 | tf_op jit(solution)/shard_map/ppermute | solution.py:413
  46.8 1.6 %copy-start.1 = (bf16[2,8,32,16,128]{4,3,2,1,0:T(8,128)(2,1)S(1)}, bf16[2,8,32,16,128]{4,3,2,1,0:T(8,128)(2,1)}, u32[]{:S(2)}) copy-start(bf16[2,8,32,16,128]{4,3,2,1,0:T(8,128)(2,1)} %get-tuple-element.29.refs_0_) | copy-start | bytes 6291460
  48.4 1.6 %copy-start.2 = (bf16[2,8,32,16,128]{4,3,2,1,0:T(8,128)(2,1)S(1)}, bf16[2,8,32,16,128]{4,3,2,1,0:T(8,128)(2,1)}, u32[]{:S(2)}) copy-start(bf16[2,8,32,16,128]{4,3,2,1,0:T(8,128)(2,1)} %get-tuple-element.30.refs_1_) | copy-start | bytes 6291460
  50.0 1.0 copy-start.3
  51.1 10.6 %copy-start.9 = (bf16[1,8,32,16,128]{4,3,2,1,0:T(8,128)(2,1)S(1)}, bf16[1,8,32,16,128]{4,3,2,1,0:T(8,128)(2,1)}, u32[]{:S(2)}) copy-start(bf16[1,8,32,16,128]{4,3,2,1,0:T(8,128)(2,1)} %get-tuple-element.37) | copy-start | bytes 3145732
  51.1 11.3 %copy-start.11 = (bf16[1,8,16,16,128]{4,3,2,1,0:T(8,128)(2,1)S(1)}, bf16[1,8,16,16,128]{4,3,2,1,0:T(8,128)(2,1)}, u32[]{:S(2)}) copy-start(bf16[1,8,16,16,128]{4,3,2,1,0:T(8,128)(2,1)} %get-tuple-element.41) | copy-start | bytes 1572868
  51.1 12.0 %copy-start = (bf16[4,8,32,16,128]{4,3,2,1,0:T(8,128)(2,1)S(1)}, bf16[4,8,32,16,128]{4,3,2,1,0:T(8,128)(2,1)}, u32[]{:S(2)}) copy-start(bf16[4,8,32,16,128]{4,3,2,1,0:T(8,128)(2,1)} %get-tuple-element.33.refs_4_) | copy-start | bytes 12582916
  51.1 12.0 %copy-start.4 = (f32[2,1,512]{2,1,0:T(1,128)S(1)}, f32[2,1,512]{2,1,0:T(1,128)}, u32[]{:S(2)}) copy-start(f32[2,1,512]{2,1,0:T(1,128)} %convert_element_type.20.mask_ref.refs_1_) | copy-start | bytes 12292
  61.6 9.6 %collective-permute-start.8 = (bf16[1,8,32,16,128]{4,3,2,1,0:T(8,128)(2,1)S(1)}, bf16[1,8,32,16,128]{4,3,2,1,0:T(8,128)(2,1)S(1)}, u32[]{:S(2)}, u32[]{:S(2)}) collective-permute-start(bf16[1,8,32,16,128]{4,3,2,1,0:T(8,128)(2,1)S(1)} %copy-done.9), channel_id=1, source_target_pairs={{4,8},{8,4},{12,16},{16,12},{20,24},{24,20},{28,32},{32,28},{36,40... | collective-permute-start | bytes 3145736 | tf_op jit(solution)/shard_map/ppermute | solution.py:413
  62.4 14.1 %collective-permute-start.9 = (bf16[1,8,16,16,128]{4,3,2,1,0:T(8,128)(2,1)S(1)}, bf16[1,8,16,16,128]{4,3,2,1,0:T(8,128)(2,1)S(1)}, u32[]{:S(2)}, u32[]{:S(2)}) collective-permute-start(bf16[1,8,16,16,128]{4,3,2,1,0:T(8,128)(2,1)S(1)} %copy-done.11), channel_id=1, source_target_pairs={{4,8},{8,4},{12,16},{16,12},{20,24},{24,20},{28,32},{32,28},{36,40... | collective-permute-start | bytes 1572872 | tf_op jit(solution)/shard_map/ppermute | solution.py:413
  63.1 7.4 %copy-start.10 = (bf16[1,8,16,16,128]{4,3,2,1,0:T(8,128)(2,1)S(1)}, bf16[1,8,16,16,128]{4,3,2,1,0:T(8,128)(2,1)}, u32[]{:S(2)}) copy-start(bf16[1,8,16,16,128]{4,3,2,1,0:T(8,128)(2,1)} %get-tuple-element.45) | copy-start | bytes 1572868
  70.5 10.6 %collective-permute-start.10 = (bf16[1,8,16,16,128]{4,3,2,1,0:T(8,128)(2,1)S(1)}, bf16[1,8,16,16,128]{4,3,2,1,0:T(8,128)(2,1)S(1)}, u32[]{:S(2)}, u32[]{:S(2)}) collective-permute-start(bf16[1,8,16,16,128]{4,3,2,1,0:T(8,128)(2,1)S(1)} %copy-done.10), channel_id=1, source_target_pairs={{4,8},{8,4},{12,16},{16,12},{20,24},{24,20},{28,32},{32,28},{36,40... | collective-permute-start | bytes 1572872 | tf_op jit(solution)/shard_map/ppermute | solution.py:413
  83.3 21.9 %collective-permute-start.13 = (f32[64,64]{1,0:T(8,128)S(1)}, f32[64,64]{1,0:T(8,128)S(1)}, u32[]{:S(2)}, u32[]{:S(2)}) collective-permute-start(f32[64,64]{1,0:T(8,128)S(1)} %get-tuple-element.51), channel_id=1, source_target_pairs={{0,12},{4,8},{8,4},{12,0},{16,28},{20,24},{24,20},{28,16},{32,44},... | collective-permute-start | bytes 49160 | tf_op jit(solution)/shard_map/ppermute | solution.py:394
  103.4 3.9 %collective-permute-start.12 = (f32[64,64]{1,0:T(8,128)S(1)}, f32[64,64]{1,0:T(8,128)S(1)}, u32[]{:S(2)}, u32[]{:S(2)}) collective-permute-start(f32[64,64]{1,0:T(8,128)S(1)} %get-tuple-element.51), channel_id=1, source_target_pairs={{0,8},{4,12},{8,0},{12,4},{16,24},{20,28},{24,16},{28,20},{32,40},... | collective-permute-start | bytes 49160 | tf_op jit(solution)/shard_map/ppermute | solution.py:394
  103.8 3.6 %collective-permute-start.11 = (f32[64,64]{1,0:T(8,128)S(1)}, f32[64,64]{1,0:T(8,128)S(1)}, u32[]{:S(2)}, u32[]{:S(2)}) collective-permute-start(f32[64,64]{1,0:T(8,128)S(1)} %get-tuple-element.51), channel_id=1, source_target_pairs={{0,4},{4,0},{8,12},{12,8},{16,20},{20,16},{24,28},{28,24},{32,36},... | collective-permute-start | bytes 49160 | tf_op jit(solution)/shard_map/ppermute | solution.py:394
  107.4 6.4 %collective-permute-start.16 = (f32[64,64]{1,0:T(8,128)S(1)}, f32[64,64]{1,0:T(8,128)S(1)}, u32[]{:S(2)}, u32[]{:S(2)}) collective-permute-start(f32[64,64]{1,0:T(8,128)S(1)} %add_add_fusion.1), channel_id=1, source_target_pairs={{0,56},{4,60},{8,48},{12,52},{16,40},{20,44},{24,32},{28,36},{32,2... | collective-permute-start | bytes 49160 | tf_op jit(solution)/shard_map/ppermute | solution.py:394
  111.9 3.9 %collective-permute-start.15 = (f32[64,64]{1,0:T(8,128)S(1)}, f32[64,64]{1,0:T(8,128)S(1)}, u32[]{:S(2)}, u32[]{:S(2)}) collective-permute-start(f32[64,64]{1,0:T(8,128)S(1)} %add_add_fusion.1), channel_id=1, source_target_pairs={{0,32},{4,36},{8,40},{12,44},{16,48},{20,52},{24,56},{28,60},{32,0... | collective-permute-start | bytes 49160 | tf_op jit(solution)/shard_map/ppermute | solution.py:394
  112.3 5.1 %collective-permute-start.14 = (f32[64,64]{1,0:T(8,128)S(1)}, f32[64,64]{1,0:T(8,128)S(1)}, u32[]{:S(2)}, u32[]{:S(2)}) collective-permute-start(f32[64,64]{1,0:T(8,128)S(1)} %add_add_fusion.1), channel_id=1, source_target_pairs={{0,24},{4,28},{8,16},{12,20},{16,8},{20,12},{24,0},{28,4},{32,56},... | collective-permute-start | bytes 49160 | tf_op jit(solution)/shard_map/ppermute | solution.py:394
  117.5 5.2 %collective-permute-start.17 = (f32[64,64]{1,0:T(8,128)S(1)}, f32[64,64]{1,0:T(8,128)S(1)}, u32[]{:S(2)}, u32[]{:S(2)}) collective-permute-start(f32[64,64]{1,0:T(8,128)S(1)} %add_add_fusion), channel_id=1, source_target_pairs={{0,96},{4,100},{8,104},{12,108},{16,112},{20,116},{24,120},{28,124... | collective-permute-start | bytes 49160 | tf_op jit(solution)/shard_map/ppermute | solution.py:394
